TPU v7x, 32 devices: a whole 2x2x4 slice. The times are simulated.
32 devices in a mesh: sect: 2 (over core), exp: 8 (over z, x), tp: 2 (over y).
Axes of the slice: x: 2, y: 2, z: 4, core: 2. Of those that a mesh axis runs over, the one named last changes fastest.
Arguments:
- tokens: bfloat16 [256, 6144], P(('sect', 'exp', 'tp')), may hold values from -6 to 6
- router_logits: float32 [256, 2], P(('sect', 'exp', 'tp')), may hold values from -6 to 6
- expert_ids: int32 [256, 2], P(('sect', 'exp', 'tp')), may hold values from 0 to 3, all different within a row; in each aligned block of 8 rows (0 to 7, 8 to 15, ...) at most 8 rows name the same one
- w_gate: bfloat16 [16, 6144, 2048], P(('sect', 'exp'), None, 'tp'), may hold values from -0.078125 to 0.078125
- w_up: bfloat16 [16, 6144, 2048], P(('sect', 'exp'), None, 'tp'), may hold values from -0.078125 to 0.078125
- w_down: bfloat16 [16, 2048, 6144], P(('sect', 'exp'), 'tp'), may hold values from -0.0625 to 0.0625
Outputs:
- mixture: bfloat16 [256, 6144], P(('sect', 'exp', 'tp'))
Inputs may be any that keep to these rules, and one draw needn't show every extreme that they name: `expert_ids`: each token names two different experts. Among the 8 tokens of one device no expert is named more than 8 times, and in every draw some expert is named exactly 8 times by the tokens of some device.
All inputs are finite; a program needn't handle non-finite values.
Results may differ from a plain program's by a relative error of at most 0.0049.
Values may be sent and summed in bfloat16 or wider, within the bound.
No kernel may reach another device: no remote copies, remote signals or barrier semaphores. Data moves between devices by JAX's collectives and lax.ppermute only.
A program may use at most 128 MiB of HBM per device.

v0:
```python
import jax
import jax.numpy as jnp
from jax import lax
from jax.sharding import PartitionSpec as P


def place_slots(ids_block, experts):
    flat_ids = ids_block.reshape(-1)
    hits_mask = (flat_ids[:, None] == jnp.arange(experts, dtype=jnp.int32)[None, :]).astype(
        jnp.int32
    )
    earlier = jnp.cumsum(hits_mask, axis=0) - hits_mask
    slot_rank = jnp.sum(earlier * hits_mask, axis=1)
    return (flat_ids, slot_rank)


def per_device(tokens, router_logits, expert_ids, w_gate, w_up, w_down):
    device_count = lax.axis_size(("sect", "exp", "tp"))
    tp_count = lax.axis_size("tp")
    experts_all = device_count // tp_count // 4
    token_count = tokens.shape[0]
    capacity = min(token_count, 4 * token_count // experts_all)
    model_width = tokens.shape[1]
    quarter_width = model_width // tp_count
    flat_ids, slot_rank = place_slots(expert_ids, experts_all)
    columns = flat_ids * capacity + slot_rank
    positions = jnp.arange(experts_all * capacity, dtype=jnp.int32)
    picker = (positions[:, None] == columns[None, :]).astype(jnp.bfloat16)
    repeated = jnp.repeat(tokens, 2, axis=0)
    slab_rows = jnp.dot(picker, repeated, preferred_element_type=jnp.float32).astype(jnp.bfloat16)
    slab_rows = slab_rows.reshape(experts_all, capacity, model_width)
    fanout = device_count // experts_all
    outbound = jnp.repeat(slab_rows, fanout, axis=0)
    received = lax.all_to_all(
        outbound, ("sect", "exp", "tp"), split_axis=0, concat_axis=0, tiled=True
    )
    row_count = device_count * capacity
    expert_rows = received.reshape(row_count, model_width)
    gate_proj = jnp.dot(expert_rows, w_gate[0], preferred_element_type=jnp.float32)
    up_proj = jnp.dot(expert_rows, w_up[0], preferred_element_type=jnp.float32)
    hidden = (jax.nn.silu(gate_proj) * up_proj).astype(jnp.bfloat16)
    partial_value = jnp.dot(hidden, w_down[0], preferred_element_type=jnp.float32)
    owned_part = lax.psum_scatter(partial_value, "tp", scatter_dimension=1, tiled=True)
    returned = lax.all_to_all(
        owned_part.reshape(device_count, capacity, quarter_width),
        ("sect", "exp", "tp"),
        split_axis=0,
        concat_axis=0,
        tiled=True,
    )
    piece_sums = jnp.sum(
        returned.reshape(experts_all, 4, tp_count, capacity, quarter_width), axis=1
    )
    expert_out = piece_sums.transpose(0, 2, 1, 3).reshape(experts_all * capacity, model_width)
    weights = jax.nn.sigmoid(router_logits - router_logits[:, ::-1]).reshape(-1)
    combine_w = jnp.where(positions[None, :] == columns[:, None], weights[:, None], 0.0)
    combine_w = jnp.sum(combine_w.reshape(token_count, 2, experts_all * capacity), axis=1)
    mixture = jnp.dot(
        combine_w, expert_out, precision=lax.Precision.HIGHEST, preferred_element_type=jnp.float32
    )
    return mixture.astype(jnp.bfloat16)


def solution(mesh):
    in_specs = (
        P(("sect", "exp", "tp"), None),
        P(("sect", "exp", "tp"), None),
        P(("sect", "exp", "tp"), None),
        P(("sect", "exp"), None, "tp"),
        P(("sect", "exp"), None, "tp"),
        P(("sect", "exp"), "tp", None),
    )
    out_specs = P(("sect", "exp", "tp"), None)
    return jax.shard_map(
        per_device, mesh=mesh, in_specs=in_specs, out_specs=out_specs, check_vma=False
    )
```

profile of v0, /device:TPU:0, one launch (start us, length us, event | category | flops | bytes accessed | tf_op | source)
XLA Modules:
  0.0 278.0 jit_solution(2524805688427105803)
XLA Ops:
  6.5 0.0 reduce-scatter.2.cloned.1.call-start
  6.5 0.8 copy.13
  7.3 0.1 eq.43
  7.4 0.1 fusion.30
  7.5 0.2 select_reduce_fusion.1
  7.7 1.0 broadcast_in_dim.25
  8.7 0.1 reshape.54
  8.8 0.2 fusion.6
  9.0 0.4 broadcast_in_dim.26
  9.4 80.1 %all_to_all.10 = bf16[32,8,6144]{2,1,0:T(8,128)(2,1)S(1)} all-to-all(bf16[32,8,6144]{2,1,0:T(8,128)(2,1)S(1)} %bitcast.38), channel_id=1, replica_groups=mesh['sect'=2,'exp'=8,'tp'=2] {'sect','exp','tp'}, dimensions={0} | all-to-all | bytes 6291456 | tf_op jit(solution)/shard_map/all_to_all | solution.py:34
  89.5 7.5 %fusion.4 = f32[256,1024]{1,0:T(8,128)} fusion(bf16[1,6144,1024]{2,1,0:T(8,128)(2,1)} %param.9, bf16[32,8,6144]{2,1,0:T(8,128)(2,1)S(1)} %all_to_all.10), kind=kOutput, calls=%fused_computation.4 | convolution fusion | flops 3221225472 | bytes 16777216 | tf_op jit(solution)/shard_map/dot_general | solution.py:39
  97.0 18.0 %fusion = f32[256,6144]{1,0:T(8,128)} fusion(bf16[1,1024,6144]{2,1,0:T(8,128)(2,1)} %param.11, bf16[1,6144,1024]{2,1,0:T(8,128)(2,1)} %param.10, bf16[32,8,6144]{2,1,0:T(8,128)(2,1)S(1)} %all_to_all.10, f32[256,1024]{1,0:T(8,128)} %fusion.4), kind=kOutput, calls=%fused_computation | convolution fusion | flops 6444023808 | bytes 35651584 | tf_op jit(solution)/shard_map/dot_general | solution.py:42
  115.0 0.0 copy-start
  115.0 0.0 reduce-scatter.2.cloned.1.call-update
  115.0 73.7 %reduce-scatter.2.cloned.1.call-done = f32[256,3072]{1,0:T(8,128)} async-done(((f32[256,6144]{1,0:T(8,128)}), f32[256,3072]{1,0:T(8,128)}) %reduce-scatter.2.cloned.1.call-update) | async-done | bytes 3145744 | tf_op jit(solution)/shard_map/reduce_scatter | solution.py:43
  188.8 4.6 %all-to-all-start.1 = ((f32[32,8,3072]{2,1,0:T(8,128)}), f32[32,8,3072]{2,1,0:T(8,128)S(1)}, u32[]{:S(2)}, u32[]{:S(2)}) async-start(f32[32,8,3072]{2,1,0:T(8,128)} %bitcast.39), calls=%async_computation.2 | async-start | bytes 6291456 | tf_op jit(solution)/shard_map/all_to_all | solution.py:44
  193.4 0.1 reduce_sum.30
  193.5 0.0 copy-done
  193.5 0.1 copy.15
  193.6 0.1 select_reduce_fusion
  193.7 74.1 %all-to-all-done.1 = f32[32,8,3072]{2,1,0:T(8,128)S(1)} async-done(((f32[32,8,3072]{2,1,0:T(8,128)}), f32[32,8,3072]{2,1,0:T(8,128)S(1)}, u32[]{:S(2)}, u32[]{:S(2)}) %all-to-all-start.1) | async-done | bytes 3145760 | tf_op jit(solution)/shard_map/all_to_all | solution.py:44
  267.8 1.1 reduce_sum.32
  268.9 2.3 convolution_convert_fusion.1
  (5 shorter events, 0.1 us)
Async XLA Ops:
  6.5 182.2 %reduce-scatter.2.cloned.1.call-start = ((), (), s32[]{:S(2)}) async-start(), calls=%async_computation.3 | async-start | bytes 9437184 | tf_op jit(solution)/shard_map/reduce_scatter | solution.py:43
  115.0 78.5 %copy-start = (f32[8,2]{0,1:T(2,128)S(1)}, f32[8,2]{0,1:T(2,128)}, u32[]{:S(2)}) copy-start(f32[8,2]{0,1:T(2,128)} %param.7) | copy-start | bytes 196
  188.8 79.0 %all-to-all-start.1 = ((f32[32,8,3072]{2,1,0:T(8,128)}), f32[32,8,3072]{2,1,0:T(8,128)S(1)}, u32[]{:S(2)}, u32[]{:S(2)}) async-start(f32[32,8,3072]{2,1,0:T(8,128)} %bitcast.39), calls=%async_computation.2 | async-start | bytes 6291456 | tf_op jit(solution)/shard_map/all_to_all | solution.py:44
Sparse Core Ops, SparseCore 0:
  115.1 73.5 reduce-scatter.1
where the time goes:
time: 278 us
  waiting for transfers between devices  148 us (53%)
  blocking collectives  80.1 us (29%)
  matrix products  28 us (10%)
  between operations  13.4 us (5%)
  starting transfers between devices  4.61 us (2%)
    all_to_all x1, blocking collectives, per_device(): lax.all_to_all(outbound, ('sect', 'exp', 'tp'), split_axis=0, concat_axis...  80.1 us
    all_to_all x1, waiting for transfers between devices, per_device(): lax.all_to_all(owned_part.reshape(device_count, capacity, quarter_width),...  74.1 us
    reduce_scatter x1, waiting for transfers between devices, per_device(): lax.psum_scatter(partial_value, 'tp', scatter_dimension=1, tiled=True)  73.7 us
    dot_general x1, matrix products, per_device(): jnp.dot(hidden, w_down[0], preferred_element_type=jnp.float32)  18 us
    dot_general x1, matrix products, per_device(): jnp.dot(expert_rows, w_gate[0], preferred_element_type=jnp.float32)  7.48 us
  transfers between devices with their start and end apart: 2, of which 2 were waited for; matrix products, arithmetic and copies ran while one was open for 0% of the time, Pallas kernels for 0%

commit v1 on v0

v1 whole, which is shorter than its diff:
```python
import jax
import jax.numpy as jnp
from jax import lax
from jax.experimental import pallas as pl
from jax.experimental.pallas import tpu as pltpu
from jax.sharding import PartitionSpec as P

AXES = ("sect", "exp", "tp")
CHUNKS = 2
LANES = 128
VMEM = pl.BlockSpec(memory_space=pltpu.VMEM)


def gate_up_kernel(depth, part_count, has_prev, *refs):
    parts = refs[:part_count]
    wg_ref, wu_ref = refs[part_count : part_count + 2]
    rest = refs[part_count + 2 :]
    rows = jnp.concatenate([p[:, :depth] for p in parts], axis=0)
    gate = jnp.dot(rows, wg_ref[0], preferred_element_type=jnp.float32)
    up = jnp.dot(rows, wu_ref[0], preferred_element_type=jnp.float32)
    if has_prev:
        gate = gate + rest[0][...]
        up = up + rest[1][...]
        rest = rest[2:]
    if len(rest) == 1:
        rest[0][...] = (gate / (1.0 + jnp.exp(-gate)) * up).astype(jnp.bfloat16)
    else:
        rest[0][...] = gate
        rest[1][...] = up


def gate_up(parts, w_gate, w_up, chunk, depth, prev, last):
    row_count = sum(p.shape[0] for p in parts)
    width = w_gate.shape[2]
    tile = 256
    weight_spec = pl.BlockSpec((1, depth, tile), lambda i: (0, chunk, i))
    tile_spec = pl.BlockSpec((row_count, tile), lambda i: (0, i))
    out_types = [jnp.bfloat16] if last else [jnp.float32, jnp.float32]
    return pl.pallas_call(
        lambda *refs: gate_up_kernel(depth, len(parts), bool(prev), *refs),
        grid=(width // tile,),
        in_specs=[VMEM] * len(parts) + [weight_spec] * 2 + [tile_spec] * len(prev),
        out_specs=[tile_spec] * len(out_types),
        out_shape=[jax.ShapeDtypeStruct((row_count, width), t) for t in out_types],
        cost_estimate=pl.CostEstimate(
            flops=4 * row_count * depth * width,
            bytes_accessed=4 * depth * width,
            transcendentals=row_count * width if last else 0,
        ),
        compiler_params=pltpu.CompilerParams(vmem_limit_bytes=40 << 20),
        name="gate_up",
    )(*parts, w_gate, w_up, *prev)


def down_kernel(pick_ref, hidden_ref, wd_ref, mine_ref, other_ref, keep_ref, send_ref):
    out = jnp.dot(hidden_ref[...], wd_ref[0], preferred_element_type=jnp.float32)
    half = keep_ref.shape[0]
    columns = mine_ref.shape[1] - LANES

    def share(ref):
        shares = ref[:, columns:].astype(jnp.float32)
        return jnp.sum(shares * pick_ref[...], axis=1, keepdims=True)

    keep_ref[...] = out[:half] * share(mine_ref)
    send_ref[...] = (out[half:] * share(other_ref)).astype(jnp.bfloat16)


def down(pick, hidden, w_down, mine, other, chunk, chunk_width):
    row_count, depth = hidden.shape
    half = row_count // 2
    tile = 512
    first = chunk * (chunk_width // tile)
    return pl.pallas_call(
        down_kernel,
        grid=(chunk_width // tile,),
        in_specs=[
            VMEM,
            VMEM,
            pl.BlockSpec((1, depth, tile), lambda i: (0, 0, first + i)),
            VMEM,
            VMEM,
        ],
        out_specs=[pl.BlockSpec((half, tile), lambda i: (0, i))] * 2,
        out_shape=[
            jax.ShapeDtypeStruct((half, chunk_width), jnp.float32),
            jax.ShapeDtypeStruct((half, chunk_width), jnp.bfloat16),
        ],
        cost_estimate=pl.CostEstimate(
            flops=2 * row_count * depth * chunk_width,
            bytes_accessed=2 * depth * chunk_width,
            transcendentals=0,
        ),
        compiler_params=pltpu.CompilerParams(vmem_limit_bytes=40 << 20),
        name="down",
    )(pick, hidden, w_down, mine, other)


def share_columns(router_logits, expert_ids, experts):
    weights = jax.nn.sigmoid(router_logits - router_logits[:, ::-1])
    named = expert_ids[:, :, None] == jnp.arange(experts, dtype=jnp.int32)[None, None, :]
    share = jnp.sum(jnp.where(named, weights[:, :, None], 0.0), axis=1)
    high = lax.reduce_precision(share, 8, 7)
    middle = lax.reduce_precision(share - high, 8, 7)
    low = share - high - middle
    pieces = jnp.concatenate([high, middle, low], axis=1)
    pieces = jnp.pad(pieces, ((0, 0), (0, LANES - 3 * experts)))
    return pieces.astype(jnp.bfloat16)


def per_device(tokens, router_logits, expert_ids, w_gate, w_up, w_down):
    chips = lax.axis_size(("exp", "tp"))
    experts = lax.axis_size(("sect", "exp")) // 4
    bits = chips.bit_length() - 1
    model_width = tokens.shape[1]
    chunk_width = model_width // CHUNKS

    def swap_with(flips):
        return [
            (core * chips + chip, (core ^ flips[2]) * chips + (chip ^ flips[core]))
            for core in range(2)
            for chip in range(chips)
        ]

    high_bits = list(range(bits - 1, 1, -1))
    orders = (high_bits + [1, 0], high_bits + [0, 1])
    chip_swaps = [swap_with((1 << a, 1 << b, 0)) for a, b in zip(*orders)]
    core_swap = swap_with((0, 0, 1))

    my_expert = lax.axis_index(("sect", "exp")) // 4
    lane = jnp.arange(LANES, dtype=jnp.int32)[None, :]
    pick = jnp.where((lane % experts == my_expert) & (lane < 3 * experts), 1.0, 0.0)

    prev = ()
    for chunk in range(CHUNKS):
        rows = tokens[:, chunk * chunk_width : (chunk + 1) * chunk_width]
        last = chunk == CHUNKS - 1
        if last:
            shares = share_columns(router_logits, expert_ids, experts)
            rows = jnp.concatenate([rows, shares], axis=1)
        for pairs in chip_swaps:
            rows = jnp.concatenate([rows, lax.ppermute(rows, AXES, pairs)], axis=0)
        other = lax.ppermute(rows, AXES, core_swap)
        prev = gate_up((rows, other), w_gate, w_up, chunk, chunk_width, prev, last)
    hidden = prev[0]

    results = []
    for chunk in range(CHUNKS):
        keep, send = down(pick, hidden, w_down, rows, other, chunk, chunk_width)
        total = keep + lax.ppermute(send, AXES, core_swap).astype(jnp.float32)
        for pairs in chip_swaps[::-1]:
            half = total.shape[0] // 2
            send = total[half:].astype(jnp.bfloat16)
            received = lax.ppermute(send, AXES, pairs)
            total = total[:half] + received.astype(jnp.float32)
        results.append(total.astype(jnp.bfloat16))
    return jnp.concatenate(results, axis=1)


def solution(mesh):
    in_specs = (
        P(AXES, None),
        P(AXES, None),
        P(AXES, None),
        P(("sect", "exp"), None, "tp"),
        P(("sect", "exp"), None, "tp"),
        P(("sect", "exp"), "tp", None),
    )
    return jax.shard_map(
        per_device, mesh=mesh, in_specs=in_specs, out_specs=P(AXES, None), check_vma=False
    )
```

time: 278 us -> 90.8 us (0.33)
  waiting for transfers between devices: 148 us -> 30.8 us
  blocking collectives: 80.1 us -> 0 us
  matrix products: 28 us -> 0 us
  Pallas kernels: 0 us -> 25.7 us
  starting transfers between devices: 4.61 us -> 28.8 us
  between operations: 13.4 us -> 0.25 us
    all_to_all x1 -> x0, blocking collectives: 80.1 us -> none  [per_device(): lax.all_to_all(outbound, ('sect', 'exp', 'tp'), split_axis=0, concat_axis...]
    all_to_all x1 -> x0, waiting for transfers between devices: 74.1 us -> none  [per_device(): lax.all_to_all(owned_part.reshape(device_count, capacity, quarter_width),...]
    reduce_scatter x1 -> x0, waiting for transfers between devices: 73.7 us -> none  [per_device(): lax.psum_scatter(partial_value, 'tp', scatter_dimension=1, tiled=True)]
    ppermute x0 -> x20, waiting for transfers between devices: none -> 30.8 us  [the longest x8 16.2 us: per_device(): rows = jnp.concatenate([rows, lax.ppermute(rows, AXES, pairs)], axis=0)]
    ppermute x0 -> x20, starting transfers between devices: none -> 28.8 us  [the longest x8 14.2 us: per_device(): received = lax.ppermute(send, AXES, pairs)]
    dot_general x4 -> x0, matrix products: 28 us -> none  [the longest x1 18 us: per_device(): jnp.dot(hidden, w_down[0], preferred_element_type=jnp.float32)]
    pallas_call x0 -> x4, Pallas kernels: none -> 25.7 us  [the longest x2 14.2 us: gate_up(): pl.pallas_call(lambda *refs: gate_up_kernel(depth, len(parts), bool(prev)...]
    all_to_all x1 -> x0, starting transfers between devices: 4.61 us -> none  [per_device(): lax.all_to_all(owned_part.reshape(device_count, capacity, quarter_width),...]
  transfers between devices with their start and end apart: 2 -> 20, of which waited for: 2 -> 14; matrix products, arithmetic and copies ran while one was open for 0% -> 4% of each run, Pallas kernels for 0% -> 14%
where the time goes in v1:
time: 90.8 us; the launch traced here: 90.4 us
  waiting for transfers between devices  30.8 us (34%)
  starting transfers between devices  28.8 us (32%)
  Pallas kernels  25.7 us (28%)
  other arithmetic  2.91 us (3%)
  local copies, waits for them, and re-layouts  1.92 us (2%)
    ppermute x8, waiting for transfers between devices, per_device(): rows = jnp.concatenate([rows, lax.ppermute(rows, AXES, pairs)], axis=0)  16.2 us
    ppermute x8, waiting for transfers between devices, per_device(): received = lax.ppermute(send, AXES, pairs)  14.3 us
    pallas_call x2, Pallas kernels, gate_up(): pl.pallas_call(lambda *refs: gate_up_kernel(depth, len(parts), bool(prev)...  14.2 us
    ppermute x8, starting transfers between devices, per_device(): received = lax.ppermute(send, AXES, pairs)  14.2 us
    ppermute x8, starting transfers between devices, per_device(): rows = jnp.concatenate([rows, lax.ppermute(rows, AXES, pairs)], axis=0)  13.8 us
    pallas_call x2, Pallas kernels, down(): pl.pallas_call(down_kernel, grid=(chunk_width // tile,), in_specs=[VMEM,...  11.4 us
  transfers between devices with their start and end apart: 20, of which 14 were waited for; matrix products, arithmetic and copies ran while one was open for 4% of the time, Pallas kernels for 14%

profile of v1, /device:TPU:0, one launch (start us, length us, event | category | flops | bytes accessed | tf_op | source)
XLA Modules:
  0.0 90.4 jit_solution(8079627034063919216)
XLA Ops:
  0.0 0.8 fusion.8
  0.8 4.1 %collective-permute-start.5 = (bf16[8,3072]{1,0:T(8,128)(2,1)S(1)}, bf16[8,3072]{1,0:T(8,128)(2,1)S(1)}, u32[]{:S(2)}, u32[]{:S(2)}) collective-permute-start(bf16[8,3072]{1,0:T(8,128)(2,1)S(1)} %get-tuple-element.17), channel_id=1, source_target_pairs={{0,8},{1,9},{2,10},{3,11},{4,12},{5,13},{6,14},{7,15},{8,0},{9,1},... | collective-permute-start | bytes 147464 | tf_op jit(solution)/shard_map/ppermute | solution.py:141
  4.9 0.7 rev.3
  5.6 0.7 add_divide_fusion
  6.3 0.7 select_reduce_fusion
  7.0 0.1 copy.9
  7.1 0.1 fusion.7
  7.2 0.1 collective-permute-start
  7.3 0.2 collective-permute-done.5
  7.5 1.7 %collective-permute-start.6 = (bf16[16,3072]{1,0:T(8,128)(2,1)S(1)}, bf16[16,3072]{1,0:T(8,128)(2,1)S(1)}, u32[]{:S(2)}, u32[]{:S(2)}) collective-permute-start(bf16[16,3072]{1,0:T(8,128)(2,1)S(1)} %pad_maximum_fusion.5), channel_id=1, source_target_pairs={{0,4},{1,5},{2,6},{3,7},{4,0},{5,1},{6,2},{7,3},{8,12},{9,13},{10,... | collective-permute-start | bytes 294920 | tf_op jit(solution)/shard_map/ppermute | solution.py:141
  9.3 3.3 %collective-permute-done = bf16[8,3200]{1,0:T(8,128)(2,1)S(1)} collective-permute-done((bf16[8,3200]{1,0:T(8,128)(2,1)S(1)}, bf16[8,3200]{1,0:T(8,128)(2,1)S(1)}, u32[]{:S(2)}, u32[]{:S(2)}) %collective-permute-start) | collective-permute-done | bytes 51232 | tf_op jit(solution)/shard_map/ppermute | solution.py:141
  12.6 1.7 %collective-permute-start.1 = (bf16[16,3200]{1,0:T(8,128)(2,1)S(1)}, bf16[16,3200]{1,0:T(8,128)(2,1)S(1)}, u32[]{:S(2)}, u32[]{:S(2)}) collective-permute-start(bf16[16,3200]{1,0:T(8,128)(2,1)S(1)} %pad_maximum_fusion.4), channel_id=1, source_target_pairs={{0,4},{1,5},{2,6},{3,7},{4,0},{5,1},{6,2},{7,3},{8,12},{9,13},{10,... | collective-permute-start | bytes 307208 | tf_op jit(solution)/shard_map/ppermute | solution.py:141
  14.3 1.5 %collective-permute-start.7 = (bf16[32,3072]{1,0:T(8,128)(2,1)S(1)}, bf16[32,3072]{1,0:T(8,128)(2,1)S(1)}, u32[]{:S(2)}, u32[]{:S(2)}) collective-permute-start(bf16[32,3072]{1,0:T(8,128)(2,1)S(1)} %pad_maximum_fusion.3), channel_id=1, source_target_pairs={{0,2},{1,3},{2,0},{3,1},{4,6},{5,7},{6,4},{7,5},{8,10},{9,11},{10,... | collective-permute-start | bytes 589832 | tf_op jit(solution)/shard_map/ppermute | solution.py:141
  15.9 1.4 %collective-permute-done.1 = bf16[16,3200]{1,0:T(8,128)(2,1)S(1)} collective-permute-done((bf16[16,3200]{1,0:T(8,128)(2,1)S(1)}, bf16[16,3200]{1,0:T(8,128)(2,1)S(1)}, u32[]{:S(2)}, u32[]{:S(2)}) %collective-permute-start.1) | collective-permute-done | bytes 102432 | tf_op jit(solution)/shard_map/ppermute | solution.py:141
  17.3 1.6 %collective-permute-start.2 = (bf16[32,3200]{1,0:T(8,128)(2,1)S(1)}, bf16[32,3200]{1,0:T(8,128)(2,1)S(1)}, u32[]{:S(2)}, u32[]{:S(2)}) collective-permute-start(bf16[32,3200]{1,0:T(8,128)(2,1)S(1)} %pad_maximum_fusion.2), channel_id=1, source_target_pairs={{0,2},{1,3},{2,0},{3,1},{4,6},{5,7},{6,4},{7,5},{8,10},{9,11},{10,... | collective-permute-start | bytes 614408 | tf_op jit(solution)/shard_map/ppermute | solution.py:141
  18.9 1.5 %collective-permute-done.7 = bf16[32,3072]{1,0:T(8,128)(2,1)S(1)} collective-permute-done((bf16[32,3072]{1,0:T(8,128)(2,1)S(1)}, bf16[32,3072]{1,0:T(8,128)(2,1)S(1)}, u32[]{:S(2)}, u32[]{:S(2)}) %collective-permute-start.7) | collective-permute-done | bytes 196640 | tf_op jit(solution)/shard_map/ppermute | solution.py:141
  20.4 1.5 %collective-permute-start.8 = (bf16[64,3072]{1,0:T(8,128)(2,1)S(1)}, bf16[64,3072]{1,0:T(8,128)(2,1)S(1)}, u32[]{:S(2)}, u32[]{:S(2)}) collective-permute-start(bf16[64,3072]{1,0:T(8,128)(2,1)S(1)} %pad_maximum_fusion.1), channel_id=1, source_target_pairs={{0,1},{1,0},{2,3},{3,2},{4,5},{5,4},{6,7},{7,6},{8,9},{9,8},{10,11... | collective-permute-start | bytes 1179656 | tf_op jit(solution)/shard_map/ppermute | solution.py:141
  21.9 3.4 %collective-permute-done.2 = bf16[32,3200]{1,0:T(8,128)(2,1)S(1)} collective-permute-done((bf16[32,3200]{1,0:T(8,128)(2,1)S(1)}, bf16[32,3200]{1,0:T(8,128)(2,1)S(1)}, u32[]{:S(2)}, u32[]{:S(2)}) %collective-permute-start.2) | collective-permute-done | bytes 204832 | tf_op jit(solution)/shard_map/ppermute | solution.py:141
  25.4 1.6 %collective-permute-start.3 = (bf16[64,3200]{1,0:T(8,128)(2,1)S(1)}, bf16[64,3200]{1,0:T(8,128)(2,1)S(1)}, u32[]{:S(2)}, u32[]{:S(2)}) collective-permute-start(bf16[64,3200]{1,0:T(8,128)(2,1)S(1)} %pad_maximum_fusion), channel_id=1, source_target_pairs={{0,1},{1,0},{2,3},{3,2},{4,5},{5,4},{6,7},{7,6},{8,9},{9,8},{10,11... | collective-permute-start | bytes 1228808 | tf_op jit(solution)/shard_map/ppermute | solution.py:141
  27.0 1.3 %collective-permute-done.8 = bf16[64,3072]{1,0:T(8,128)(2,1)S(1)} collective-permute-done((bf16[64,3072]{1,0:T(8,128)(2,1)S(1)}, bf16[64,3072]{1,0:T(8,128)(2,1)S(1)}, u32[]{:S(2)}, u32[]{:S(2)}) %collective-permute-start.8) | collective-permute-done | bytes 393248 | tf_op jit(solution)/shard_map/ppermute | solution.py:141
  28.3 0.1 collective-permute-start.9
  28.4 5.0 %collective-permute-done.3 = bf16[64,3200]{1,0:T(8,128)(2,1)S(1)} collective-permute-done((bf16[64,3200]{1,0:T(8,128)(2,1)S(1)}, bf16[64,3200]{1,0:T(8,128)(2,1)S(1)}, u32[]{:S(2)}, u32[]{:S(2)}) %collective-permute-start.3) | collective-permute-done | bytes 409632 | tf_op jit(solution)/shard_map/ppermute | solution.py:141
  33.4 0.1 collective-permute-start.4
  33.6 7.1 %gate_up.2 = (f32[256,1024]{1,0:T(8,128)S(1)}, f32[256,1024]{1,0:T(8,128)S(1)}) custom-call(bf16[128,3072]{1,0:T(8,128)(2,1)S(1)} %constant_dynamic-update-slice_fusion.5.refs_0_, bf16[128,3072]{1,0:T(8,128)(2,1)S(1)} %collective-permute-done.9.refs_1_, bf16[1,6144,1024]{2,1,0:T(8,128)(2,1)} %refs_2_.3, bf16[1,6144,1024]{2,1,0:T(8,128)(2,1)} %refs_3_.3), custom_call_target="tpu_custom_call" | custom-call | flops 3221225472 | bytes 12582912 | tf_op jit(solution)/shard_map/gate_up/pallas_call | solution.py:39
  40.6 7.1 %gate_up.3.hidden_ref = bf16[256,1024]{1,0:T(8,128)(2,1)S(1)} custom-call(bf16[128,3200]{1,0:T(8,128)(2,1)S(1)} %constant_dynamic-update-slice_fusion.refs_0_.mine_ref, bf16[128,3200]{1,0:T(8,128)(2,1)S(1)} %collective-permute-done.4.refs_1_.other_ref, bf16[1,6144,1024]{2,1,0:T(8,128)(2,1)} %refs_2_.3, bf16[1,6144,1024]{2,1,0:T(8,128)(2,1)} %refs_3_.3, ...), custom_call_target="tpu_custom_call" | custom-call | flops 3221225472 | bytes 12582912 | tf_op jit(solution)/shard_map/gate_up/pallas_call | solution.py:39
  47.8 5.7 %down.2 = (f32[128,3072]{1,0:T(8,128)S(1)}, bf16[128,3072]{1,0:T(8,128)(2,1)S(1)}) custom-call(f32[1,128]{1,0:T(1,128)S(1)} %and_select_fusion.pick_ref, bf16[256,1024]{1,0:T(8,128)(2,1)S(1)} %gate_up.3.hidden_ref, bf16[1,1024,6144]{2,1,0:T(8,128)(2,1)} %wd_ref.3, bf16[128,3200]{1,0:T(8,128)(2,1)S(1)} %constant_dynamic-update-slice_fusion.refs_0_.mine_ref, ...), custom_call_target="tpu_custom_call" | custom-call | flops 1610612736 | bytes 6291456 | tf_op jit(solution)/shard_map/down/pallas_call | solution.py:73
  53.5 0.5 collective-permute-start.10
  54.1 5.7 %down.3 = (f32[128,3072]{1,0:T(8,128)S(1)}, bf16[128,3072]{1,0:T(8,128)(2,1)S(1)}) custom-call(f32[1,128]{1,0:T(1,128)S(1)} %and_select_fusion.pick_ref, bf16[256,1024]{1,0:T(8,128)(2,1)S(1)} %gate_up.3.hidden_ref, bf16[1,1024,6144]{2,1,0:T(8,128)(2,1)} %wd_ref.3, bf16[128,3200]{1,0:T(8,128)(2,1)S(1)} %constant_dynamic-update-slice_fusion.refs_0_.mine_ref, ...), custom_call_target="tpu_custom_call" | custom-call | flops 1610612736 | bytes 6291456 | tf_op jit(solution)/shard_map/down/pallas_call | solution.py:73
  59.8 0.1 collective-permute-start.15
  59.9 0.2 convert_add_fusion.1
  60.2 1.6 %collective-permute-start.11 = (bf16[64,3072]{1,0:T(8,128)(2,1)S(1)}, bf16[64,3072]{1,0:T(8,128)(2,1)S(1)}, u32[]{:S(2)}, u32[]{:S(2)}) collective-permute-start(bf16[64,3072]{1,0:T(8,128)(2,1)S(1)} %slice.118), channel_id=1, source_target_pairs={{0,1},{1,0},{2,3},{3,2},{4,5},{5,4},{6,7},{7,6},{8,9},{9,8},{10,11... | collective-permute-start | bytes 1179656 | tf_op jit(solution)/shard_map/ppermute | solution.py:153
  61.8 0.4 collective-permute-done.15
  62.2 0.2 convert_add_fusion
  62.4 1.6 %collective-permute-start.16 = (bf16[64,3072]{1,0:T(8,128)(2,1)S(1)}, bf16[64,3072]{1,0:T(8,128)(2,1)S(1)}, u32[]{:S(2)}, u32[]{:S(2)}) collective-permute-start(bf16[64,3072]{1,0:T(8,128)(2,1)S(1)} %slice.117), channel_id=1, source_target_pairs={{0,1},{1,0},{2,3},{3,2},{4,5},{5,4},{6,7},{7,6},{8,9},{9,8},{10,11... | collective-permute-start | bytes 1179656 | tf_op jit(solution)/shard_map/ppermute | solution.py:153
  64.0 4.0 %collective-permute-done.11 = bf16[64,3072]{1,0:T(8,128)(2,1)S(1)} collective-permute-done((bf16[64,3072]{1,0:T(8,128)(2,1)S(1)}, bf16[64,3072]{1,0:T(8,128)(2,1)S(1)}, u32[]{:S(2)}, u32[]{:S(2)}) %collective-permute-start.11) | collective-permute-done | bytes 393248 | tf_op jit(solution)/shard_map/ppermute | solution.py:153
  68.0 0.1 slice_add_fusion.1
  68.1 1.5 %collective-permute-start.12 = (bf16[32,3072]{1,0:T(8,128)(2,1)S(1)}, bf16[32,3072]{1,0:T(8,128)(2,1)S(1)}, u32[]{:S(2)}, u32[]{:S(2)}) collective-permute-start(bf16[32,3072]{1,0:T(8,128)(2,1)S(1)} %slice.120), channel_id=1, source_target_pairs={{0,2},{1,3},{2,0},{3,1},{4,6},{5,7},{6,4},{7,5},{8,10},{9,11},{10,... | collective-permute-start | bytes 589832 | tf_op jit(solution)/shard_map/ppermute | solution.py:153
  69.7 4.3 %collective-permute-done.16 = bf16[64,3072]{1,0:T(8,128)(2,1)S(1)} collective-permute-done((bf16[64,3072]{1,0:T(8,128)(2,1)S(1)}, bf16[64,3072]{1,0:T(8,128)(2,1)S(1)}, u32[]{:S(2)}, u32[]{:S(2)}) %collective-permute-start.16) | collective-permute-done | bytes 393248 | tf_op jit(solution)/shard_map/ppermute | solution.py:153
  74.1 1.5 %collective-permute-start.17 = (bf16[32,3072]{1,0:T(8,128)(2,1)S(1)}, bf16[32,3072]{1,0:T(8,128)(2,1)S(1)}, u32[]{:S(2)}, u32[]{:S(2)}) collective-permute-start(bf16[32,3072]{1,0:T(8,128)(2,1)S(1)} %slice.119), channel_id=1, source_target_pairs={{0,2},{1,3},{2,0},{3,1},{4,6},{5,7},{6,4},{7,5},{8,10},{9,11},{10,... | collective-permute-start | bytes 589832 | tf_op jit(solution)/shard_map/ppermute | solution.py:153
  75.7 1.7 %collective-permute-start.13 = (bf16[16,3072]{1,0:T(8,128)(2,1)S(1)}, bf16[16,3072]{1,0:T(8,128)(2,1)S(1)}, u32[]{:S(2)}, u32[]{:S(2)}) collective-permute-start(bf16[16,3072]{1,0:T(8,128)(2,1)S(1)} %slice.122), channel_id=1, source_target_pairs={{0,4},{1,5},{2,6},{3,7},{4,0},{5,1},{6,2},{7,3},{8,12},{9,13},{10,... | collective-permute-start | bytes 294920 | tf_op jit(solution)/shard_map/ppermute | solution.py:153
  77.4 2.4 %collective-permute-done.17 = bf16[32,3072]{1,0:T(8,128)(2,1)S(1)} collective-permute-done((bf16[32,3072]{1,0:T(8,128)(2,1)S(1)}, bf16[32,3072]{1,0:T(8,128)(2,1)S(1)}, u32[]{:S(2)}, u32[]{:S(2)}) %collective-permute-start.17) | collective-permute-done | bytes 196640 | tf_op jit(solution)/shard_map/ppermute | solution.py:153
  79.9 1.8 %collective-permute-start.18 = (bf16[16,3072]{1,0:T(8,128)(2,1)S(1)}, bf16[16,3072]{1,0:T(8,128)(2,1)S(1)}, u32[]{:S(2)}, u32[]{:S(2)}) collective-permute-start(bf16[16,3072]{1,0:T(8,128)(2,1)S(1)} %slice.121), channel_id=1, source_target_pairs={{0,4},{1,5},{2,6},{3,7},{4,0},{5,1},{6,2},{7,3},{8,12},{9,13},{10,... | collective-permute-start | bytes 294920 | tf_op jit(solution)/shard_map/ppermute | solution.py:153
  81.7 2.1 %collective-permute-start.14 = (bf16[8,3072]{1,0:T(8,128)(2,1)S(1)}, bf16[8,3072]{1,0:T(8,128)(2,1)S(1)}, u32[]{:S(2)}, u32[]{:S(2)}) collective-permute-start(bf16[8,3072]{1,0:T(8,128)(2,1)S(1)} %slice.124), channel_id=1, source_target_pairs={{0,8},{1,9},{2,10},{3,11},{4,12},{5,13},{6,14},{7,15},{8,0},{9,1},... | collective-permute-start | bytes 147464 | tf_op jit(solution)/shard_map/ppermute | solution.py:153
  83.8 0.8 collective-permute-done.18
  84.6 2.4 %collective-permute-start.19 = (bf16[8,3072]{1,0:T(8,128)(2,1)S(1)}, bf16[8,3072]{1,0:T(8,128)(2,1)S(1)}, u32[]{:S(2)}, u32[]{:S(2)}) collective-permute-start(bf16[8,3072]{1,0:T(8,128)(2,1)S(1)} %slice.123), channel_id=1, source_target_pairs={{0,8},{1,9},{2,10},{3,11},{4,12},{5,13},{6,14},{7,15},{8,0},{9,1},... | collective-permute-start | bytes 147464 | tf_op jit(solution)/shard_map/ppermute | solution.py:153
  87.0 0.8 collective-permute-done.14
  87.8 1.9 %collective-permute-done.19 = bf16[8,3072]{1,0:T(8,128)(2,1)S(1)} collective-permute-done((bf16[8,3072]{1,0:T(8,128)(2,1)S(1)}, bf16[8,3072]{1,0:T(8,128)(2,1)S(1)}, u32[]{:S(2)}, u32[]{:S(2)}) %collective-permute-start.19) | collective-permute-done | bytes 49184 | tf_op jit(solution)/shard_map/ppermute | solution.py:153
  89.7 0.6 pad_maximum_fusion.6
  (38 shorter events, 0.7 us)
Async XLA Ops:
  0.8 6.7 %collective-permute-start.5 = (bf16[8,3072]{1,0:T(8,128)(2,1)S(1)}, bf16[8,3072]{1,0:T(8,128)(2,1)S(1)}, u32[]{:S(2)}, u32[]{:S(2)}) collective-permute-start(bf16[8,3072]{1,0:T(8,128)(2,1)S(1)} %get-tuple-element.17), channel_id=1, source_target_pairs={{0,8},{1,9},{2,10},{3,11},{4,12},{5,13},{6,14},{7,15},{8,0},{9,1},... | collective-permute-start | bytes 147464 | tf_op jit(solution)/shard_map/ppermute | solution.py:141
  7.2 5.3 %collective-permute-start = (bf16[8,3200]{1,0:T(8,128)(2,1)S(1)}, bf16[8,3200]{1,0:T(8,128)(2,1)S(1)}, u32[]{:S(2)}, u32[]{:S(2)}) collective-permute-start(bf16[8,3200]{1,0:T(8,128)(2,1)S(1)} %get-tuple-element.20), channel_id=1, source_target_pairs={{0,8},{1,9},{2,10},{3,11},{4,12},{5,13},{6,14},{7,15},{8,0},{9,1},... | collective-permute-start | bytes 153608 | tf_op jit(solution)/shard_map/ppermute | solution.py:141
  7.5 6.8 %collective-permute-start.6 = (bf16[16,3072]{1,0:T(8,128)(2,1)S(1)}, bf16[16,3072]{1,0:T(8,128)(2,1)S(1)}, u32[]{:S(2)}, u32[]{:S(2)}) collective-permute-start(bf16[16,3072]{1,0:T(8,128)(2,1)S(1)} %pad_maximum_fusion.5), channel_id=1, source_target_pairs={{0,4},{1,5},{2,6},{3,7},{4,0},{5,1},{6,2},{7,3},{8,12},{9,13},{10,... | collective-permute-start | bytes 294920 | tf_op jit(solution)/shard_map/ppermute | solution.py:141
  12.6 4.7 %collective-permute-start.1 = (bf16[16,3200]{1,0:T(8,128)(2,1)S(1)}, bf16[16,3200]{1,0:T(8,128)(2,1)S(1)}, u32[]{:S(2)}, u32[]{:S(2)}) collective-permute-start(bf16[16,3200]{1,0:T(8,128)(2,1)S(1)} %pad_maximum_fusion.4), channel_id=1, source_target_pairs={{0,4},{1,5},{2,6},{3,7},{4,0},{5,1},{6,2},{7,3},{8,12},{9,13},{10,... | collective-permute-start | bytes 307208 | tf_op jit(solution)/shard_map/ppermute | solution.py:141
  14.3 6.1 %collective-permute-start.7 = (bf16[32,3072]{1,0:T(8,128)(2,1)S(1)}, bf16[32,3072]{1,0:T(8,128)(2,1)S(1)}, u32[]{:S(2)}, u32[]{:S(2)}) collective-permute-start(bf16[32,3072]{1,0:T(8,128)(2,1)S(1)} %pad_maximum_fusion.3), channel_id=1, source_target_pairs={{0,2},{1,3},{2,0},{3,1},{4,6},{5,7},{6,4},{7,5},{8,10},{9,11},{10,... | collective-permute-start | bytes 589832 | tf_op jit(solution)/shard_map/ppermute | solution.py:141
  17.3 8.1 %collective-permute-start.2 = (bf16[32,3200]{1,0:T(8,128)(2,1)S(1)}, bf16[32,3200]{1,0:T(8,128)(2,1)S(1)}, u32[]{:S(2)}, u32[]{:S(2)}) collective-permute-start(bf16[32,3200]{1,0:T(8,128)(2,1)S(1)} %pad_maximum_fusion.2), channel_id=1, source_target_pairs={{0,2},{1,3},{2,0},{3,1},{4,6},{5,7},{6,4},{7,5},{8,10},{9,11},{10,... | collective-permute-start | bytes 614408 | tf_op jit(solution)/shard_map/ppermute | solution.py:141
  20.4 7.8 %collective-permute-start.8 = (bf16[64,3072]{1,0:T(8,128)(2,1)S(1)}, bf16[64,3072]{1,0:T(8,128)(2,1)S(1)}, u32[]{:S(2)}, u32[]{:S(2)}) collective-permute-start(bf16[64,3072]{1,0:T(8,128)(2,1)S(1)} %pad_maximum_fusion.1), channel_id=1, source_target_pairs={{0,1},{1,0},{2,3},{3,2},{4,5},{5,4},{6,7},{7,6},{8,9},{9,8},{10,11... | collective-permute-start | bytes 1179656 | tf_op jit(solution)/shard_map/ppermute | solution.py:141
  25.4 8.0 %collective-permute-start.3 = (bf16[64,3200]{1,0:T(8,128)(2,1)S(1)}, bf16[64,3200]{1,0:T(8,128)(2,1)S(1)}, u32[]{:S(2)}, u32[]{:S(2)}) collective-permute-start(bf16[64,3200]{1,0:T(8,128)(2,1)S(1)} %pad_maximum_fusion), channel_id=1, source_target_pairs={{0,1},{1,0},{2,3},{3,2},{4,5},{5,4},{6,7},{7,6},{8,9},{9,8},{10,11... | collective-permute-start | bytes 1228808 | tf_op jit(solution)/shard_map/ppermute | solution.py:141
  28.3 5.3 %collective-permute-start.9 = (bf16[128,3072]{1,0:T(8,128)(2,1)S(1)}, bf16[128,3072]{1,0:T(8,128)(2,1)S(1)}, u32[]{:S(2)}, u32[]{:S(2)}) collective-permute-start(bf16[128,3072]{1,0:T(8,128)(2,1)S(1)} %constant_dynamic-update-slice_fusion.5.refs_0_), channel_id=1, source_target_pairs={{0,16},{1,17},{2,18},{3,19},{4,20},{5,21},{6,22},{7,23},{8,24},{9,... | collective-permute-start | bytes 2359304 | tf_op jit(solution)/shard_map/ppermute | solution.py:142
  33.4 7.2 %collective-permute-start.4 = (bf16[128,3200]{1,0:T(8,128)(2,1)S(1)}, bf16[128,3200]{1,0:T(8,128)(2,1)S(1)}, u32[]{:S(2)}, u32[]{:S(2)}) collective-permute-start(bf16[128,3200]{1,0:T(8,128)(2,1)S(1)} %constant_dynamic-update-slice_fusion.refs_0_.mine_ref), channel_id=1, source_target_pairs={{0,16},{1,17},{2,18},{3,19},{4,20},{5,21},{6,22},{7,23},{8,24},{9,... | collective-permute-start | bytes 2457608 | tf_op jit(solution)/shard_map/ppermute | solution.py:142
  53.5 6.4 %collective-permute-start.10 = (bf16[128,3072]{1,0:T(8,128)(2,1)S(1)}, bf16[128,3072]{1,0:T(8,128)(2,1)S(1)}, u32[]{:S(2)}, u32[]{:S(2)}) collective-permute-start(bf16[128,3072]{1,0:T(8,128)(2,1)S(1)} %get-tuple-element.14), channel_id=1, source_target_pairs={{0,16},{1,17},{2,18},{3,19},{4,20},{5,21},{6,22},{7,23},{8,24},{9,... | collective-permute-start | bytes 2359304 | tf_op jit(solution)/shard_map/ppermute | solution.py:149
  59.8 2.4 %collective-permute-start.15 = (bf16[128,3072]{1,0:T(8,128)(2,1)S(1)}, bf16[128,3072]{1,0:T(8,128)(2,1)S(1)}, u32[]{:S(2)}, u32[]{:S(2)}) collective-permute-start(bf16[128,3072]{1,0:T(8,128)(2,1)S(1)} %get-tuple-element.16), channel_id=1, source_target_pairs={{0,16},{1,17},{2,18},{3,19},{4,20},{5,21},{6,22},{7,23},{8,24},{9,... | collective-permute-start | bytes 2359304 | tf_op jit(solution)/shard_map/ppermute | solution.py:149
  60.2 7.8 %collective-permute-start.11 = (bf16[64,3072]{1,0:T(8,128)(2,1)S(1)}, bf16[64,3072]{1,0:T(8,128)(2,1)S(1)}, u32[]{:S(2)}, u32[]{:S(2)}) collective-permute-start(bf16[64,3072]{1,0:T(8,128)(2,1)S(1)} %slice.118), channel_id=1, source_target_pairs={{0,1},{1,0},{2,3},{3,2},{4,5},{5,4},{6,7},{7,6},{8,9},{9,8},{10,11... | collective-permute-start | bytes 1179656 | tf_op jit(solution)/shard_map/ppermute | solution.py:153
  62.4 11.6 %collective-permute-start.16 = (bf16[64,3072]{1,0:T(8,128)(2,1)S(1)}, bf16[64,3072]{1,0:T(8,128)(2,1)S(1)}, u32[]{:S(2)}, u32[]{:S(2)}) collective-permute-start(bf16[64,3072]{1,0:T(8,128)(2,1)S(1)} %slice.117), channel_id=1, source_target_pairs={{0,1},{1,0},{2,3},{3,2},{4,5},{5,4},{6,7},{7,6},{8,9},{9,8},{10,11... | collective-permute-start | bytes 1179656 | tf_op jit(solution)/shard_map/ppermute | solution.py:153
  68.1 7.5 %collective-permute-start.12 = (bf16[32,3072]{1,0:T(8,128)(2,1)S(1)}, bf16[32,3072]{1,0:T(8,128)(2,1)S(1)}, u32[]{:S(2)}, u32[]{:S(2)}) collective-permute-start(bf16[32,3072]{1,0:T(8,128)(2,1)S(1)} %slice.120), channel_id=1, source_target_pairs={{0,2},{1,3},{2,0},{3,1},{4,6},{5,7},{6,4},{7,5},{8,10},{9,11},{10,... | collective-permute-start | bytes 589832 | tf_op jit(solution)/shard_map/ppermute | solution.py:153
  74.1 5.7 %collective-permute-start.17 = (bf16[32,3072]{1,0:T(8,128)(2,1)S(1)}, bf16[32,3072]{1,0:T(8,128)(2,1)S(1)}, u32[]{:S(2)}, u32[]{:S(2)}) collective-permute-start(bf16[32,3072]{1,0:T(8,128)(2,1)S(1)} %slice.119), channel_id=1, source_target_pairs={{0,2},{1,3},{2,0},{3,1},{4,6},{5,7},{6,4},{7,5},{8,10},{9,11},{10,... | collective-permute-start | bytes 589832 | tf_op jit(solution)/shard_map/ppermute | solution.py:153
  75.7 6.0 %collective-permute-start.13 = (bf16[16,3072]{1,0:T(8,128)(2,1)S(1)}, bf16[16,3072]{1,0:T(8,128)(2,1)S(1)}, u32[]{:S(2)}, u32[]{:S(2)}) collective-permute-start(bf16[16,3072]{1,0:T(8,128)(2,1)S(1)} %slice.122), channel_id=1, source_target_pairs={{0,4},{1,5},{2,6},{3,7},{4,0},{5,1},{6,2},{7,3},{8,12},{9,13},{10,... | collective-permute-start | bytes 294920 | tf_op jit(solution)/shard_map/ppermute | solution.py:153
  79.9 4.7 %collective-permute-start.18 = (bf16[16,3072]{1,0:T(8,128)(2,1)S(1)}, bf16[16,3072]{1,0:T(8,128)(2,1)S(1)}, u32[]{:S(2)}, u32[]{:S(2)}) collective-permute-start(bf16[16,3072]{1,0:T(8,128)(2,1)S(1)} %slice.121), channel_id=1, source_target_pairs={{0,4},{1,5},{2,6},{3,7},{4,0},{5,1},{6,2},{7,3},{8,12},{9,13},{10,... | collective-permute-start | bytes 294920 | tf_op jit(solution)/shard_map/ppermute | solution.py:153
  81.7 6.1 %collective-permute-start.14 = (bf16[8,3072]{1,0:T(8,128)(2,1)S(1)}, bf16[8,3072]{1,0:T(8,128)(2,1)S(1)}, u32[]{:S(2)}, u32[]{:S(2)}) collective-permute-start(bf16[8,3072]{1,0:T(8,128)(2,1)S(1)} %slice.124), channel_id=1, source_target_pairs={{0,8},{1,9},{2,10},{3,11},{4,12},{5,13},{6,14},{7,15},{8,0},{9,1},... | collective-permute-start | bytes 147464 | tf_op jit(solution)/shard_map/ppermute | solution.py:153
  84.6 5.1 %collective-permute-start.19 = (bf16[8,3072]{1,0:T(8,128)(2,1)S(1)}, bf16[8,3072]{1,0:T(8,128)(2,1)S(1)}, u32[]{:S(2)}, u32[]{:S(2)}) collective-permute-start(bf16[8,3072]{1,0:T(8,128)(2,1)S(1)} %slice.123), channel_id=1, source_target_pairs={{0,8},{1,9},{2,10},{3,11},{4,12},{5,13},{6,14},{7,15},{8,0},{9,1},... | collective-permute-start | bytes 147464 | tf_op jit(solution)/shard_map/ppermute | solution.py:153

commit v2 on v0

v2 whole, which is shorter than its diff:
```python
import jax
import jax.numpy as jnp
from jax import lax
from jax.experimental import pallas as pl
from jax.experimental.pallas import tpu as pltpu
from jax.sharding import PartitionSpec as P

AXES = ("sect", "exp", "tp")
LANES = 128
TILE = 256
SCOPED = 1 << 20
SMALL = 2 << 20
GIGA = 10**9
STACK_COST = ((1, 1), (4, 4))
FFN_COST = (0.1, 0.1, 0.1, 0.1, 0.1)
STRIP = 512
VMEM = pl.BlockSpec(memory_space=pltpu.VMEM)
ANY = pl.BlockSpec(memory_space=pl.ANY)
HBM = pl.BlockSpec(memory_space=pltpu.HBM)


def side_by_side(parts, depth):
    return jnp.concatenate([p[:, :depth] for p in parts], axis=0)


def pair_kernel(depth, part_count, *refs):
    parts, (wg_ref, wu_ref) = refs[:part_count], refs[part_count : part_count + 2]
    gate_ref, up_ref = refs[-2:]
    for at in range(0, gate_ref.shape[1], TILE):
        columns = pl.ds(at, TILE)
        rows = side_by_side(parts, depth)
        for w_ref, out_ref in ((wg_ref, gate_ref), (wu_ref, up_ref)):
            out_ref[:, columns] = jnp.dot(
                rows, w_ref[0, :depth, columns], preferred_element_type=jnp.float32
            )


def pair(parts, w_gate, w_up, depth, cost, after=()):
    row_count = sum(p.shape[0] for p in parts)
    width = w_gate.shape[2]
    return pl.pallas_call(
        lambda *refs: pair_kernel(depth, len(parts), *refs),
        in_specs=[VMEM] * (len(parts) + 2) + [ANY] * len(after),
        out_specs=[VMEM] * 2,
        out_shape=[jax.ShapeDtypeStruct((row_count, width), jnp.float32)] * 2,
        cost_estimate=pl.CostEstimate(flops=int(cost * GIGA), bytes_accessed=0, transcendentals=0),
        compiler_params=pltpu.CompilerParams(vmem_limit_bytes=SCOPED),
        name="pair",
    )(*parts, w_gate, w_up, *after)


def hidden_kernel(depth, part_count, *refs):
    parts, refs = refs[:part_count], refs[part_count:]
    weights, sums, hidden_ref = refs[:2], refs[2:4], refs[-1]
    for at in range(0, hidden_ref.shape[1], TILE):
        columns = pl.ds(at, TILE)
        rows = side_by_side(parts, depth)
        gate, up = [
            total[:, columns]
            + jnp.dot(
                rows, weight[0, pl.ds(depth, depth), columns], preferred_element_type=jnp.float32
            )
            for weight, total in zip(weights, sums)
        ]
        hidden_ref[:, columns] = (gate / (1.0 + jnp.exp(-gate)) * up).astype(jnp.bfloat16)


def hidden_rows(parts, w_gate, w_up, sums, depth, cost, after=()):
    row_count = sum(p.shape[0] for p in parts)
    width = w_gate.shape[2]
    return pl.pallas_call(
        lambda *refs: hidden_kernel(depth, len(parts), *refs),
        in_specs=[VMEM] * (len(parts) + 2 + len(sums)) + [ANY] * len(after),
        out_specs=VMEM,
        out_shape=jax.ShapeDtypeStruct((row_count, width), jnp.bfloat16),
        cost_estimate=pl.CostEstimate(
            flops=int(cost * GIGA), bytes_accessed=0, transcendentals=row_count * width
        ),
        compiler_params=pltpu.CompilerParams(vmem_limit_bytes=SCOPED),
        name="hidden_rows",
    )(*parts, w_gate, w_up, *sums, *after)


def down_kernel(first, experts, group_count, *refs):
    hidden, wd_ref, parts = refs[:group_count], refs[group_count], refs[group_count + 1 : -2]
    keep_ref, send_ref = refs[-2:]
    quarter = parts[0].shape[0]
    entry = lax.axis_index("sect") * lax.axis_size("exp") + lax.axis_index("exp")

    def share(part):
        lanes = part.shape[1] - LANES
        lane = lax.broadcasted_iota(jnp.int32, (quarter, LANES), 1)
        chosen = (lane % experts == entry // 4) & (lane < 3 * experts)
        shares = jnp.where(chosen, part[:, lanes:].astype(jnp.float32), 0.0)
        return jnp.sum(shares, axis=1, keepdims=True)

    shares = [share(p) for p in parts]
    for at in range(0, keep_ref.shape[1], TILE):
        columns = pl.ds(at, TILE)
        rows = jnp.concatenate([h[...] for h in hidden], axis=0)
        out = jnp.dot(
            rows, wd_ref[0, :, pl.ds(first + at, TILE)], preferred_element_type=jnp.float32
        )
        for k, part_share in enumerate(shares):
            piece = part_share * out[k * quarter : (k + 1) * quarter]
            place = pl.ds(k // 2 * quarter, quarter)
            if k % 2 == 0:
                keep_ref[place, columns] = piece
            else:
                send_ref[place, columns] = piece.astype(jnp.bfloat16)


def down(experts, hidden, w_down, parts, chunk, chunk_width, cost):
    half = sum(h.shape[0] for h in hidden) // 2
    first = chunk * chunk_width
    return pl.pallas_call(
        lambda *refs: down_kernel(first, experts, len(hidden), *refs),
        in_specs=[VMEM] * (len(hidden) + 1 + len(parts)),
        out_specs=[VMEM] * 2,
        out_shape=[
            jax.ShapeDtypeStruct((half, chunk_width), jnp.float32),
            jax.ShapeDtypeStruct((half, chunk_width), jnp.bfloat16),
        ],
        cost_estimate=pl.CostEstimate(
            flops=int(cost * GIGA), bytes_accessed=0, transcendentals=0
        ),
        compiler_params=pltpu.CompilerParams(vmem_limit_bytes=SCOPED),
        name="down",
    )(*hidden, w_down, *parts)


def small_call(kernel, name, out_shape, *operands, after=(), flops=10**6):
    return pl.pallas_call(
        kernel,
        in_specs=[VMEM] * len(operands) + [ANY] * len(after),
        out_specs=jax.tree.map(lambda _: VMEM, out_shape),
        out_shape=out_shape,
        cost_estimate=pl.CostEstimate(flops=flops, bytes_accessed=0, transcendentals=0),
        compiler_params=pltpu.CompilerParams(vmem_limit_bytes=SMALL),
        name=name,
    )(*operands, *after)


def cut_kernel(experts, tokens_hbm, logits_hbm, ids_hbm, plain_ref, shared_ref, *scratch):
    tokens_ref, logits_ref, ids_ref, sems = scratch
    sources = (tokens_hbm, logits_hbm, ids_hbm)
    copies = [
        pltpu.make_async_copy(src, dst, sems.at[k])
        for k, (src, dst) in enumerate(zip(sources, scratch))
    ]
    for copy in copies:
        copy.start()
    for copy in copies:
        copy.wait()
    row_count, width = plain_ref.shape
    plain_ref[...] = tokens_ref[:, :width]
    shared_ref[:, :width] = tokens_ref[:, width:]
    square = (row_count, row_count)
    diagonal = lax.broadcasted_iota(jnp.int32, square, 0) == lax.broadcasted_iota(
        jnp.int32, square, 1
    )

    def column(row):
        spread = jnp.broadcast_to(row, square)
        return jnp.sum(jnp.where(diagonal, spread, 0.0), axis=1, keepdims=True)

    logits = [column(logits_ref[k : k + 1, :]) for k in range(2)]
    ids = [column(ids_ref[k : k + 1, :].astype(jnp.float32)) for k in range(2)]
    lane = lax.broadcasted_iota(jnp.int32, (row_count, LANES), 1)
    expert = (lane % experts).astype(jnp.float32)
    share = jnp.zeros((row_count, LANES), jnp.float32)
    for k in range(2):
        prob = 1.0 / (1.0 + jnp.exp(logits[1 - k] - logits[k]))
        share = share + jnp.where(ids[k] == expert, prob, 0.0)
    high = share.astype(jnp.bfloat16).astype(jnp.float32)
    middle = (share - high).astype(jnp.bfloat16).astype(jnp.float32)
    low = share - high - middle
    piece = lane // experts
    pieces = jnp.where(piece == 0, high, jnp.where(piece == 1, middle, low))
    shared_ref[:, width:] = jnp.where(piece < 3, pieces, 0.0).astype(jnp.bfloat16)


def stack_kernel(fan, *refs):
    out_ref = refs[-1]
    count = refs[0].shape[0]
    if count % 16:
        blocks = [r[...].astype(jnp.float32) for r in refs[:fan]]
        out_ref[...] = jnp.concatenate(blocks, axis=0).astype(out_ref.dtype)
    else:
        for k in range(fan):
            out_ref[k * count : (k + 1) * count] = refs[k][...]


def stack(mine, received, after, flops):
    fan = 1 + len(received)
    return small_call(
        lambda *refs: stack_kernel(fan, *refs),
        "stack",
        jax.ShapeDtypeStruct((fan * mine.shape[0], mine.shape[1]), mine.dtype),
        mine,
        *received,
        after=after,
        flops=flops,
    )


def merge_kernel(taken, fan, total_ref, *refs):
    received, (keep_ref, *sent) = refs[:taken], refs[len(refs) - fan :]
    count = keep_ref.shape[0]
    for at in range(0, total_ref.shape[1], STRIP):
        columns = pl.ds(at, STRIP)
        total = total_ref[:, columns]
        for r in received:
            total = total + r[:, columns].astype(jnp.float32)
        keep_ref[:, columns] = total[:count]
        for k in range(1, fan):
            piece = total[k * count : (k + 1) * count]
            sent[k - 1][:, columns] = piece.astype(jnp.bfloat16)


def merge(total, received, fan, after):
    shape = (total.shape[0] // fan, total.shape[1])
    keep, *sent = small_call(
        lambda *refs: merge_kernel(len(received), fan, *refs),
        "merge",
        [jax.ShapeDtypeStruct(shape, jnp.float32 if k == 0 else jnp.bfloat16) for k in range(fan)],
        total,
        *received,
        after=after,
    )
    return keep, sent


def finish_kernel(taken, *refs):
    out_ref = refs[-1]
    at = 0
    for k in range(2):
        total_ref, *received = refs[k * (taken + 1) : (k + 1) * (taken + 1)]
        columns = pl.ds(at, total_ref.shape[1])
        total = total_ref[...]
        for r in received:
            total = total + r[...].astype(jnp.float32)
        out_ref[:, columns] = total.astype(jnp.bfloat16)
        at += total_ref.shape[1]


def per_device(tokens, router_logits, expert_ids, w_gate, w_up, w_down):
    chips = lax.axis_size(("exp", "tp"))
    experts = lax.axis_size(("sect", "exp")) // 4
    bits = chips.bit_length() - 1
    own, model_width = tokens.shape
    width = model_width // 2

    def swap_with(flips):
        return [
            (core * chips + chip, (core ^ flips[2]) * chips + (chip ^ flips[core]))
            for core in range(2)
            for chip in range(chips)
        ]

    def permute(rows, step):
        rows = rows if isinstance(rows, list) else [rows] * len(step)
        return [lax.ppermute(r, AXES, swap_with(flips)) for r, flips in zip(rows, step)]

    core_swap = [(0, 0, 1)]
    steps = [[(1 << k, 1 << k, 0)] for k in range(bits - 1, 3, -1)]
    steps.append([(m, m, 0) for m in (4, 8, 12)])
    steps.append([(2, 1, 0)])
    steps.append([(1, 2, 0)])

    sources = [
        pltpu.with_memory_space_constraint(x, pltpu.HBM)
        for x in (tokens, router_logits.T, expert_ids.T)
    ]
    rows = pl.pallas_call(
        lambda *refs: cut_kernel(experts, *refs),
        in_specs=[HBM] * 3,
        out_specs=[VMEM] * 2,
        out_shape=[
            jax.ShapeDtypeStruct((own, width), tokens.dtype),
            jax.ShapeDtypeStruct((own, width + LANES), tokens.dtype),
        ],
        scratch_shapes=[pltpu.VMEM(x.shape, x.dtype) for x in sources]
        + [pltpu.SemaphoreType.DMA((3,))],
        cost_estimate=pl.CostEstimate(flops=10**6, bytes_accessed=0, transcendentals=0),
        compiler_params=pltpu.CompilerParams(vmem_limit_bytes=2 << 20),
        name="cut",
    )(*sources)
    rows = list(rows)
    flying = [permute(r, steps[0]) for r in rows]
    for k in range(len(steps) - 1):
        for c in range(2):
            rows[c] = stack(rows[c], flying[c], (rows[1 - c],), int(STACK_COST[c][min(k, 1)] * GIGA))
            flying[c] = permute(rows[c], steps[k + 1])
    early = [permute(r, core_swap)[0] for r in rows]
    arrived = [f[0] for f in flying]
    weights, cost = (w_gate, w_up), FFN_COST

    sums = list(pair((rows[0], early[0]), *weights, width, cost[0], (rows[1],)))
    arrived[0], sums[0] = lax.optimization_barrier((arrived[0], sums[0]))
    late = permute(arrived[0], core_swap)[0]
    hidden = [hidden_rows((rows[1], early[1]), *weights, sums, width, cost[1], (arrived[0],))]
    sums = list(pair((arrived[0], late), *weights, width, cost[2], (hidden[0],)))
    arrived[1], sums[0] = lax.optimization_barrier((arrived[1], sums[0]))
    late = permute(arrived[1], core_swap)[0]
    hidden.append(hidden_rows((arrived[1], late), *weights, sums, width, cost[3]))
    parts = (rows[1], early[1], arrived[1], late)

    totals, flying = [], []
    for c in range(2):
        kept, sent = down(experts, hidden, w_down, parts, c, width, cost[4])
        totals.append(kept)
        flying.append(permute([sent], core_swap))
    for step in steps[::-1]:
        for c in range(2):
            totals[c], sent = merge(totals[c], flying[c], 1 + len(step), (totals[1 - c],))
            flying[c] = permute(sent, step)
    return small_call(
        lambda *refs: finish_kernel(len(flying[0]), *refs),
        "finish",
        jax.ShapeDtypeStruct(tokens.shape, tokens.dtype),
        totals[0],
        *flying[0],
        totals[1],
        *flying[1],
    )


def solution(mesh):
    in_specs = (
        P(AXES, None),
        P(AXES, None),
        P(AXES, None),
        P(("sect", "exp"), None, "tp"),
        P(("sect", "exp"), None, "tp"),
        P(("sect", "exp"), "tp", None),
    )
    return jax.shard_map(
        per_device, mesh=mesh, in_specs=in_specs, out_specs=P(AXES, None), check_vma=False
    )
```

time: 278 us -> 69.1 us (0.25)
  waiting for transfers between devices: 148 us -> 22.1 us
  blocking collectives: 80.1 us -> 0 us
  matrix products: 28 us -> 0 us
  starting transfers between devices: 4.61 us -> 32.6 us
  Pallas kernels: 0 us -> 13.8 us
  between operations: 13.4 us -> 0.26 us
    all_to_all x1 -> x0, blocking collectives: 80.1 us -> none  [per_device(): lax.all_to_all(outbound, ('sect', 'exp', 'tp'), split_axis=0, concat_axis...]
    all_to_all x1 -> x0, waiting for transfers between devices: 74.1 us -> none  [per_device(): lax.all_to_all(owned_part.reshape(device_count, capacity, quarter_width),...]
    reduce_scatter x1 -> x0, waiting for transfers between devices: 73.7 us -> none  [per_device(): lax.psum_scatter(partial_value, 'tp', scatter_dimension=1, tiled=True)]
    ppermute x0 -> x26, starting transfers between devices: none -> 32.6 us  [permute(): lax.ppermute(r, AXES, swap_with(flips))]
    dot_general x4 -> x0, matrix products: 28 us -> none  [the longest x1 18 us: per_device(): jnp.dot(hidden, w_down[0], preferred_element_type=jnp.float32)]
    ppermute x0 -> x26, waiting for transfers between devices: none -> 22.1 us  [permute(): lax.ppermute(r, AXES, swap_with(flips))]
    pallas_call x0 -> x18, Pallas kernels: none -> 13.8 us  [the longest x2 4.1 us: hidden_rows(): pl.pallas_call(lambda *refs: hidden_kernel(depth, len(parts), *refs), in_...]
    all_to_all x1 -> x0, starting transfers between devices: 4.61 us -> none  [per_device(): lax.all_to_all(owned_part.reshape(device_count, capacity, quarter_width),...]
  transfers between devices with their start and end apart: 2 -> 26, of which waited for: 2 -> 13; matrix products, arithmetic and copies ran while one was open for 0% -> 0% of each run, Pallas kernels for 0% -> 12%
where the time goes in v2:
time: 69.1 us; the launch traced here: 68.9 us
  starting transfers between devices  32.6 us (47%)
  waiting for transfers between devices  22.1 us (32%)
  Pallas kernels  13.8 us (20%)
    ppermute x26, starting transfers between devices, permute(): lax.ppermute(r, AXES, swap_with(flips))  32.6 us
    ppermute x26, waiting for transfers between devices, permute(): lax.ppermute(r, AXES, swap_with(flips))  22.1 us
    pallas_call x2, Pallas kernels, hidden_rows(): pl.pallas_call(lambda *refs: hidden_kernel(depth, len(parts), *refs), in_...  4.1 us
    pallas_call x2, Pallas kernels, pair(): pl.pallas_call(lambda *refs: pair_kernel(depth, len(parts), *refs), in_sp...  3.83 us
    pallas_call x2, Pallas kernels, down(): pl.pallas_call(lambda *refs: down_kernel(first, experts, len(hidden), *re...  3.58 us
  transfers between devices with their start and end apart: 26, of which 13 were waited for; matrix products, arithmetic and copies ran while one was open for 0% of the time, Pallas kernels for 12%

profile of v2, /device:TPU:0, one launch (start us, length us, event | category | flops | bytes accessed | tf_op | source)
XLA Modules:
  0.0 68.9 jit_solution(3659857365978216554)
XLA Ops:
  0.0 1.0 %cut.1 = (bf16[8,3072]{1,0:T(8,128)(2,1)S(1)}, bf16[8,3200]{1,0:T(8,128)(2,1)S(1)}) custom-call(bf16[8,6144]{1,0:T(8,128)(2,1)} %refs_0_.1, f32[2,8]{1,0:T(2,128)} %bitcast.8, s32[2,8]{1,0:T(2,128)} %bitcast.9), custom_call_target="tpu_custom_call" | custom-call | flops 1000000 | tf_op jit(solution)/shard_map/cut/pallas_call | solution.py:275
  1.0 5.1 %collective-permute-start.5 = (bf16[8,3072]{1,0:T(8,128)(2,1)S(1)}, bf16[8,3072]{1,0:T(8,128)(2,1)S(1)}, u32[]{:S(2)}, u32[]{:S(2)}) collective-permute-start(bf16[8,3072]{1,0:T(8,128)(2,1)S(1)} %get-tuple-element.36.refs_0_), channel_id=1, source_target_pairs={{0,12},{1,13},{2,14},{3,15},{4,8},{5,9},{6,10},{7,11},{8,4},{9,5},... | collective-permute-start | bytes 147464 | tf_op jit(solution)/shard_map/ppermute | solution.py:263
  6.2 0.6 collective-permute-start.3
  6.8 3.7 %collective-permute-start.2 = (bf16[8,3200]{1,0:T(8,128)(2,1)S(1)}, bf16[8,3200]{1,0:T(8,128)(2,1)S(1)}, u32[]{:S(2)}, u32[]{:S(2)}) collective-permute-start(bf16[8,3200]{1,0:T(8,128)(2,1)S(1)} %get-tuple-element.35.refs_4_.refs_0_), channel_id=1, source_target_pairs={{0,12},{1,13},{2,14},{3,15},{4,8},{5,9},{6,10},{7,11},{8,4},{9,5},... | collective-permute-start | bytes 153608 | tf_op jit(solution)/shard_map/ppermute | solution.py:263
  10.5 0.6 collective-permute-start
  11.2 1.3 %collective-permute-done.4.refs_2_ = bf16[8,3072]{1,0:T(8,128)(2,1)S(1)} collective-permute-done((bf16[8,3072]{1,0:T(8,128)(2,1)S(1)}, bf16[8,3072]{1,0:T(8,128)(2,1)S(1)}, u32[]{:S(2)}, u32[]{:S(2)}) %collective-permute-start.4) | collective-permute-done | bytes 49184 | tf_op jit(solution)/shard_map/ppermute | solution.py:263
  12.5 1.6 %collective-permute-start.7 = (bf16[32,3072]{1,0:T(8,128)(2,1)S(1)}, bf16[32,3072]{1,0:T(8,128)(2,1)S(1)}, u32[]{:S(2)}, u32[]{:S(2)}) collective-permute-start(bf16[32,3072]{1,0:T(8,128)(2,1)S(1)} %stack.4.refs_4_.refs_0_), channel_id=1, source_target_pairs={{0,2},{1,3},{2,0},{3,1},{4,6},{5,7},{6,4},{7,5},{8,10},{9,11},{10,... | collective-permute-start | bytes 589832 | tf_op jit(solution)/shard_map/ppermute | solution.py:263
  14.1 1.5 %collective-permute-done.1.refs_2_ = bf16[8,3200]{1,0:T(8,128)(2,1)S(1)} collective-permute-done((bf16[8,3200]{1,0:T(8,128)(2,1)S(1)}, bf16[8,3200]{1,0:T(8,128)(2,1)S(1)}, u32[]{:S(2)}, u32[]{:S(2)}) %collective-permute-start.1) | collective-permute-done | bytes 51232 | tf_op jit(solution)/shard_map/ppermute | solution.py:263
  15.6 1.6 %collective-permute-start.6 = (bf16[32,3200]{1,0:T(8,128)(2,1)S(1)}, bf16[32,3200]{1,0:T(8,128)(2,1)S(1)}, u32[]{:S(2)}, u32[]{:S(2)}) collective-permute-start(bf16[32,3200]{1,0:T(8,128)(2,1)S(1)} %stack.5.refs_2_.refs_0_), channel_id=1, source_target_pairs={{0,2},{1,3},{2,0},{3,1},{4,6},{5,7},{6,4},{7,5},{8,10},{9,11},{10,... | collective-permute-start | bytes 614408 | tf_op jit(solution)/shard_map/ppermute | solution.py:263
  17.1 1.1 %collective-permute-done.7.refs_1_ = bf16[32,3072]{1,0:T(8,128)(2,1)S(1)} collective-permute-done((bf16[32,3072]{1,0:T(8,128)(2,1)S(1)}, bf16[32,3072]{1,0:T(8,128)(2,1)S(1)}, u32[]{:S(2)}, u32[]{:S(2)}) %collective-permute-start.7) | collective-permute-done | bytes 196640 | tf_op jit(solution)/shard_map/ppermute | solution.py:263
  18.3 0.1 collective-permute-start.10
  18.4 1.6 %collective-permute-start.9 = (bf16[64,3072]{1,0:T(8,128)(2,1)S(1)}, bf16[64,3072]{1,0:T(8,128)(2,1)S(1)}, u32[]{:S(2)}, u32[]{:S(2)}) collective-permute-start(bf16[64,3072]{1,0:T(8,128)(2,1)S(1)} %stack.6.refs_2_.refs_0_), channel_id=1, source_target_pairs={{0,1},{1,0},{2,3},{3,2},{4,5},{5,4},{6,7},{7,6},{8,9},{9,8},{10,11... | collective-permute-start | bytes 1179656 | tf_op jit(solution)/shard_map/ppermute | solution.py:263
  20.0 1.4 %collective-permute-done.6.refs_1_ = bf16[32,3200]{1,0:T(8,128)(2,1)S(1)} collective-permute-done((bf16[32,3200]{1,0:T(8,128)(2,1)S(1)}, bf16[32,3200]{1,0:T(8,128)(2,1)S(1)}, u32[]{:S(2)}, u32[]{:S(2)}) %collective-permute-start.6) | collective-permute-done | bytes 204832 | tf_op jit(solution)/shard_map/ppermute | solution.py:263
  21.4 0.1 collective-permute-start.8
  21.5 1.6 %collective-permute-start.11 = (bf16[64,3200]{1,0:T(8,128)(2,1)S(1)}, bf16[64,3200]{1,0:T(8,128)(2,1)S(1)}, u32[]{:S(2)}, u32[]{:S(2)}) collective-permute-start(bf16[64,3200]{1,0:T(8,128)(2,1)S(1)} %stack.7.refs_4_.refs_0_.refs_3_), channel_id=1, source_target_pairs={{0,1},{1,0},{2,3},{3,2},{4,5},{5,4},{6,7},{7,6},{8,9},{9,8},{10,11... | collective-permute-start | bytes 1228808 | tf_op jit(solution)/shard_map/ppermute | solution.py:263
  23.2 1.9 %pair.2 = (f32[128,1024]{1,0:T(8,128)S(1)}, f32[128,1024]{1,0:T(8,128)S(1)}) custom-call(bf16[64,3072]{1,0:T(8,128)(2,1)S(1)} %stack.6.refs_2_.refs_0_, bf16[64,3072]{1,0:T(8,128)(2,1)S(1)} %collective-permute-done.10.refs_1_, bf16[1,6144,1024]{2,1,0:T(8,128)(2,1)S(1)} %bitcast.3, bf16[1,6144,1024]{2,1,0:T(8,128)(2,1)S(1)} %bitcast.5, ...), custom_call_target="tpu_custom_call" | custom-call | flops 100000000 | tf_op jit(solution)/shard_map/pair/pallas_call | solution.py:41
  25.1 1.2 %collective-permute-done.9.refs_6_.refs_0_ = bf16[64,3072]{1,0:T(8,128)(2,1)S(1)} collective-permute-done((bf16[64,3072]{1,0:T(8,128)(2,1)S(1)}, bf16[64,3072]{1,0:T(8,128)(2,1)S(1)}, u32[]{:S(2)}, u32[]{:S(2)}) %collective-permute-start.9) | collective-permute-done | bytes 393248 | tf_op jit(solution)/shard_map/ppermute | solution.py:263
  26.3 2.0 %hidden_rows.2.refs_4_.refs_0_ = bf16[128,1024]{1,0:T(8,128)(2,1)S(1)} custom-call(bf16[64,3200]{1,0:T(8,128)(2,1)S(1)} %stack.7.refs_4_.refs_0_.refs_3_, bf16[64,3200]{1,0:T(8,128)(2,1)S(1)} %collective-permute-done.8.refs_1_.refs_4_, bf16[1,6144,1024]{2,1,0:T(8,128)(2,1)S(1)} %bitcast.3, bf16[1,6144,1024]{2,1,0:T(8,128)(2,1)S(1)} %bitcast.5, ...), custom_call_target="tpu_custom_call" | custom-call | flops 100000000 | tf_op jit(solution)/shard_map/hidden_rows/pallas_call | solution.py:71
  28.3 1.9 %pair.3 = (f32[128,1024]{1,0:T(8,128)S(1)}, f32[128,1024]{1,0:T(8,128)S(1)}) custom-call(bf16[64,3072]{1,0:T(8,128)(2,1)S(1)} %collective-permute-done.9.refs_6_.refs_0_, bf16[64,3072]{1,0:T(8,128)(2,1)S(1)} %collective-permute-done.12.refs_1_, bf16[1,6144,1024]{2,1,0:T(8,128)(2,1)S(1)} %bitcast.3, bf16[1,6144,1024]{2,1,0:T(8,128)(2,1)S(1)} %bitcast.5, ...), custom_call_target="tpu_custom_call" | custom-call | flops 100000000 | tf_op jit(solution)/shard_map/pair/pallas_call | solution.py:41
  30.3 0.4 collective-permute-done.11.refs_0_.refs_5_
  30.6 0.2 collective-permute-start.13
  30.9 1.5 %collective-permute-done.13.refs_1_.refs_6_ = bf16[64,3200]{1,0:T(8,128)(2,1)S(1)} collective-permute-done((bf16[64,3200]{1,0:T(8,128)(2,1)S(1)}, bf16[64,3200]{1,0:T(8,128)(2,1)S(1)}, u32[]{:S(2)}, u32[]{:S(2)}) %collective-permute-start.13) | collective-permute-done | bytes 409632 | tf_op jit(solution)/shard_map/ppermute | solution.py:263
  32.4 2.1 %hidden_rows.3.refs_1_ = bf16[128,1024]{1,0:T(8,128)(2,1)S(1)} custom-call(bf16[64,3200]{1,0:T(8,128)(2,1)S(1)} %collective-permute-done.11.refs_0_.refs_5_, bf16[64,3200]{1,0:T(8,128)(2,1)S(1)} %collective-permute-done.13.refs_1_.refs_6_, bf16[1,6144,1024]{2,1,0:T(8,128)(2,1)S(1)} %bitcast.3, bf16[1,6144,1024]{2,1,0:T(8,128)(2,1)S(1)} %bitcast.5, ...), custom_call_target="tpu_custom_call" | custom-call | flops 100000000 | tf_op jit(solution)/shard_map/hidden_rows/pallas_call | solution.py:71
  34.5 0.1 slice-done.8
  34.6 1.8 %down.2 = (f32[128,3072]{1,0:T(8,128)S(1)}, bf16[128,3072]{1,0:T(8,128)(2,1)S(1)}) custom-call(bf16[128,1024]{1,0:T(8,128)(2,1)S(1)} %hidden_rows.2.refs_4_.refs_0_, bf16[128,1024]{1,0:T(8,128)(2,1)S(1)} %hidden_rows.3.refs_1_, bf16[1,1024,6144]{2,1,0:T(8,128)(2,1)S(1)} %bitcast.7, bf16[64,3200]{1,0:T(8,128)(2,1)S(1)} %stack.7.refs_4_.refs_0_.refs_3_, ...), custom_call_target="tpu_custom_call" | custom-call | flops 100000000 | tf_op jit(solution)/shard_map/down/pallas_call | solution.py:116
  36.4 0.3 collective-permute-start.14
  36.7 1.8 %down.3 = (f32[128,3072]{1,0:T(8,128)S(1)}, bf16[128,3072]{1,0:T(8,128)(2,1)S(1)}) custom-call(bf16[128,1024]{1,0:T(8,128)(2,1)S(1)} %hidden_rows.2.refs_4_.refs_0_, bf16[128,1024]{1,0:T(8,128)(2,1)S(1)} %hidden_rows.3.refs_1_, bf16[1,1024,6144]{2,1,0:T(8,128)(2,1)S(1)} %bitcast.7, bf16[64,3200]{1,0:T(8,128)(2,1)S(1)} %stack.7.refs_4_.refs_0_.refs_3_, ...), custom_call_target="tpu_custom_call" | custom-call | flops 100000000 | tf_op jit(solution)/shard_map/down/pallas_call | solution.py:116
  38.5 0.4 collective-permute-start.16
  38.8 0.1 merge.6
  38.9 1.6 %collective-permute-start.15 = (bf16[64,3072]{1,0:T(8,128)(2,1)S(1)}, bf16[64,3072]{1,0:T(8,128)(2,1)S(1)}, u32[]{:S(2)}, u32[]{:S(2)}) collective-permute-start(bf16[64,3072]{1,0:T(8,128)(2,1)S(1)} %get-tuple-element.49), channel_id=1, source_target_pairs={{0,1},{1,0},{2,3},{3,2},{4,5},{5,4},{6,7},{7,6},{8,9},{9,8},{10,11... | collective-permute-start | bytes 1179656 | tf_op jit(solution)/shard_map/ppermute | solution.py:263
  40.5 0.3 collective-permute-done.16.refs_1_
  40.8 0.1 merge.7
  40.9 1.6 %collective-permute-start.18 = (bf16[64,3072]{1,0:T(8,128)(2,1)S(1)}, bf16[64,3072]{1,0:T(8,128)(2,1)S(1)}, u32[]{:S(2)}, u32[]{:S(2)}) collective-permute-start(bf16[64,3072]{1,0:T(8,128)(2,1)S(1)} %get-tuple-element.54), channel_id=1, source_target_pairs={{0,1},{1,0},{2,3},{3,2},{4,5},{5,4},{6,7},{7,6},{8,9},{9,8},{10,11... | collective-permute-start | bytes 1179656 | tf_op jit(solution)/shard_map/ppermute | solution.py:263
  42.5 4.3 %collective-permute-done.15.refs_1_ = bf16[64,3072]{1,0:T(8,128)(2,1)S(1)} collective-permute-done((bf16[64,3072]{1,0:T(8,128)(2,1)S(1)}, bf16[64,3072]{1,0:T(8,128)(2,1)S(1)}, u32[]{:S(2)}, u32[]{:S(2)}) %collective-permute-start.15) | collective-permute-done | bytes 393248 | tf_op jit(solution)/shard_map/ppermute | solution.py:263
  46.9 1.6 %collective-permute-start.17 = (bf16[32,3072]{1,0:T(8,128)(2,1)S(1)}, bf16[32,3072]{1,0:T(8,128)(2,1)S(1)}, u32[]{:S(2)}, u32[]{:S(2)}) collective-permute-start(bf16[32,3072]{1,0:T(8,128)(2,1)S(1)} %get-tuple-element.53), channel_id=1, source_target_pairs={{0,2},{1,3},{2,0},{3,1},{4,6},{5,7},{6,4},{7,5},{8,10},{9,11},{10,... | collective-permute-start | bytes 589832 | tf_op jit(solution)/shard_map/ppermute | solution.py:263
  48.4 4.6 %collective-permute-done.18.refs_1_ = bf16[64,3072]{1,0:T(8,128)(2,1)S(1)} collective-permute-done((bf16[64,3072]{1,0:T(8,128)(2,1)S(1)}, bf16[64,3072]{1,0:T(8,128)(2,1)S(1)}, u32[]{:S(2)}, u32[]{:S(2)}) %collective-permute-start.18) | collective-permute-done | bytes 393248 | tf_op jit(solution)/shard_map/ppermute | solution.py:263
  53.1 0.1 merge.9
  53.1 1.6 %collective-permute-start.22 = (bf16[32,3072]{1,0:T(8,128)(2,1)S(1)}, bf16[32,3072]{1,0:T(8,128)(2,1)S(1)}, u32[]{:S(2)}, u32[]{:S(2)}) collective-permute-start(bf16[32,3072]{1,0:T(8,128)(2,1)S(1)} %get-tuple-element.60), channel_id=1, source_target_pairs={{0,2},{1,3},{2,0},{3,1},{4,6},{5,7},{6,4},{7,5},{8,10},{9,11},{10,... | collective-permute-start | bytes 589832 | tf_op jit(solution)/shard_map/ppermute | solution.py:263
  54.7 0.2 collective-permute-start.19
  54.9 2.9 %collective-permute-start.20 = (bf16[8,3072]{1,0:T(8,128)(2,1)S(1)}, bf16[8,3072]{1,0:T(8,128)(2,1)S(1)}, u32[]{:S(2)}, u32[]{:S(2)}) collective-permute-start(bf16[8,3072]{1,0:T(8,128)(2,1)S(1)} %get-tuple-element.58), channel_id=1, source_target_pairs={{0,8},{1,9},{2,10},{3,11},{4,12},{5,13},{6,14},{7,15},{8,0},{9,1},... | collective-permute-start | bytes 147464 | tf_op jit(solution)/shard_map/ppermute | solution.py:263
  57.8 1.4 %collective-permute-start.21 = (bf16[8,3072]{1,0:T(8,128)(2,1)S(1)}, bf16[8,3072]{1,0:T(8,128)(2,1)S(1)}, u32[]{:S(2)}, u32[]{:S(2)}) collective-permute-start(bf16[8,3072]{1,0:T(8,128)(2,1)S(1)} %get-tuple-element.59), channel_id=1, source_target_pairs={{0,12},{1,13},{2,14},{3,15},{4,8},{5,9},{6,10},{7,11},{8,4},{9,5},... | collective-permute-start | bytes 147464 | tf_op jit(solution)/shard_map/ppermute | solution.py:263
  59.2 0.1 collective-permute-start.23
  59.3 3.0 %collective-permute-start.24 = (bf16[8,3072]{1,0:T(8,128)(2,1)S(1)}, bf16[8,3072]{1,0:T(8,128)(2,1)S(1)}, u32[]{:S(2)}, u32[]{:S(2)}) collective-permute-start(bf16[8,3072]{1,0:T(8,128)(2,1)S(1)} %get-tuple-element.63), channel_id=1, source_target_pairs={{0,8},{1,9},{2,10},{3,11},{4,12},{5,13},{6,14},{7,15},{8,0},{9,1},... | collective-permute-start | bytes 147464 | tf_op jit(solution)/shard_map/ppermute | solution.py:263
  62.3 1.4 %collective-permute-start.25 = (bf16[8,3072]{1,0:T(8,128)(2,1)S(1)}, bf16[8,3072]{1,0:T(8,128)(2,1)S(1)}, u32[]{:S(2)}, u32[]{:S(2)}) collective-permute-start(bf16[8,3072]{1,0:T(8,128)(2,1)S(1)} %get-tuple-element.64), channel_id=1, source_target_pairs={{0,12},{1,13},{2,14},{3,15},{4,8},{5,9},{6,10},{7,11},{8,4},{9,5},... | collective-permute-start | bytes 147464 | tf_op jit(solution)/shard_map/ppermute | solution.py:263
  63.7 0.2 collective-permute-done.21.refs_3_
  63.9 1.1 %collective-permute-done.23.refs_5_ = bf16[8,3072]{1,0:T(8,128)(2,1)S(1)} collective-permute-done((bf16[8,3072]{1,0:T(8,128)(2,1)S(1)}, bf16[8,3072]{1,0:T(8,128)(2,1)S(1)}, u32[]{:S(2)}, u32[]{:S(2)}) %collective-permute-start.23) | collective-permute-done | bytes 49184 | tf_op jit(solution)/shard_map/ppermute | solution.py:263
  65.0 3.2 %collective-permute-done.25.refs_7_ = bf16[8,3072]{1,0:T(8,128)(2,1)S(1)} collective-permute-done((bf16[8,3072]{1,0:T(8,128)(2,1)S(1)}, bf16[8,3072]{1,0:T(8,128)(2,1)S(1)}, u32[]{:S(2)}, u32[]{:S(2)}) %collective-permute-start.25) | collective-permute-done | bytes 49184 | tf_op jit(solution)/shard_map/ppermute | solution.py:263
  68.2 0.7 finish.1
  (43 shorter events, 0.3 us)
Async XLA Ops:
  1.0 9.5 %collective-permute-start.5 = (bf16[8,3072]{1,0:T(8,128)(2,1)S(1)}, bf16[8,3072]{1,0:T(8,128)(2,1)S(1)}, u32[]{:S(2)}, u32[]{:S(2)}) collective-permute-start(bf16[8,3072]{1,0:T(8,128)(2,1)S(1)} %get-tuple-element.36.refs_0_), channel_id=1, source_target_pairs={{0,12},{1,13},{2,14},{3,15},{4,8},{5,9},{6,10},{7,11},{8,4},{9,5},... | collective-permute-start | bytes 147464 | tf_op jit(solution)/shard_map/ppermute | solution.py:263
  6.2 6.3 %collective-permute-start.4 = (bf16[8,3072]{1,0:T(8,128)(2,1)S(1)}, bf16[8,3072]{1,0:T(8,128)(2,1)S(1)}, u32[]{:S(2)}, u32[]{:S(2)}) collective-permute-start(bf16[8,3072]{1,0:T(8,128)(2,1)S(1)} %get-tuple-element.36.refs_0_), channel_id=1, source_target_pairs={{0,8},{1,9},{2,10},{3,11},{4,12},{5,13},{6,14},{7,15},{8,0},{9,1},... | collective-permute-start | bytes 147464 | tf_op jit(solution)/shard_map/ppermute | solution.py:263
  6.2 6.3 %collective-permute-start.3 = (bf16[8,3072]{1,0:T(8,128)(2,1)S(1)}, bf16[8,3072]{1,0:T(8,128)(2,1)S(1)}, u32[]{:S(2)}, u32[]{:S(2)}) collective-permute-start(bf16[8,3072]{1,0:T(8,128)(2,1)S(1)} %get-tuple-element.36.refs_0_), channel_id=1, source_target_pairs={{0,4},{1,5},{2,6},{3,7},{4,0},{5,1},{6,2},{7,3},{8,12},{9,13},{10,... | collective-permute-start | bytes 147464 | tf_op jit(solution)/shard_map/ppermute | solution.py:263
  6.8 7.3 %collective-permute-start.2 = (bf16[8,3200]{1,0:T(8,128)(2,1)S(1)}, bf16[8,3200]{1,0:T(8,128)(2,1)S(1)}, u32[]{:S(2)}, u32[]{:S(2)}) collective-permute-start(bf16[8,3200]{1,0:T(8,128)(2,1)S(1)} %get-tuple-element.35.refs_4_.refs_0_), channel_id=1, source_target_pairs={{0,12},{1,13},{2,14},{3,15},{4,8},{5,9},{6,10},{7,11},{8,4},{9,5},... | collective-permute-start | bytes 153608 | tf_op jit(solution)/shard_map/ppermute | solution.py:263
  10.5 5.0 %collective-permute-start.1 = (bf16[8,3200]{1,0:T(8,128)(2,1)S(1)}, bf16[8,3200]{1,0:T(8,128)(2,1)S(1)}, u32[]{:S(2)}, u32[]{:S(2)}) collective-permute-start(bf16[8,3200]{1,0:T(8,128)(2,1)S(1)} %get-tuple-element.35.refs_4_.refs_0_), channel_id=1, source_target_pairs={{0,8},{1,9},{2,10},{3,11},{4,12},{5,13},{6,14},{7,15},{8,0},{9,1},... | collective-permute-start | bytes 153608 | tf_op jit(solution)/shard_map/ppermute | solution.py:263
  10.5 5.0 %collective-permute-start = (bf16[8,3200]{1,0:T(8,128)(2,1)S(1)}, bf16[8,3200]{1,0:T(8,128)(2,1)S(1)}, u32[]{:S(2)}, u32[]{:S(2)}) collective-permute-start(bf16[8,3200]{1,0:T(8,128)(2,1)S(1)} %get-tuple-element.35.refs_4_.refs_0_), channel_id=1, source_target_pairs={{0,4},{1,5},{2,6},{3,7},{4,0},{5,1},{6,2},{7,3},{8,12},{9,13},{10,... | collective-permute-start | bytes 153608 | tf_op jit(solution)/shard_map/ppermute | solution.py:263
  12.5 10.6 %slice-start.3 = ((s8[12582912]{0:T(1024)(128)(4,1)}), s8[4194304]{0:T(1024)(128)(4,1)S(1)}, s32[]{:S(2)}) async-start(s8[12582912]{0:T(1024)(128)(4,1)} %bitcast.4), calls=%async_computation.3 | async-start | bytes 8388608
  12.5 10.6 %slice-start.4 = ((s8[12582912]{0:T(1024)(128)(4,1)}), s8[4194304]{0:T(1024)(128)(4,1)S(1)}, s32[]{:S(2)}) async-start(s8[12582912]{0:T(1024)(128)(4,1)} %bitcast.4), calls=%async_computation.4 | async-start | bytes 8388608
  12.5 5.7 %collective-permute-start.7 = (bf16[32,3072]{1,0:T(8,128)(2,1)S(1)}, bf16[32,3072]{1,0:T(8,128)(2,1)S(1)}, u32[]{:S(2)}, u32[]{:S(2)}) collective-permute-start(bf16[32,3072]{1,0:T(8,128)(2,1)S(1)} %stack.4.refs_4_.refs_0_), channel_id=1, source_target_pairs={{0,2},{1,3},{2,0},{3,1},{4,6},{5,7},{6,4},{7,5},{8,10},{9,11},{10,... | collective-permute-start | bytes 589832 | tf_op jit(solution)/shard_map/ppermute | solution.py:263
  15.6 7.6 %slice-start = ((s8[12582912]{0:T(1024)(128)(4,1)}), s8[4194304]{0:T(1024)(128)(4,1)S(1)}, s32[]{:S(2)}) async-start(s8[12582912]{0:T(1024)(128)(4,1)} %bitcast.2), calls=%async_computation | async-start | bytes 8388608
  15.6 7.6 %slice-start.1 = ((s8[12582912]{0:T(1024)(128)(4,1)}), s8[4194304]{0:T(1024)(128)(4,1)S(1)}, s32[]{:S(2)}) async-start(s8[12582912]{0:T(1024)(128)(4,1)} %bitcast.2), calls=%async_computation.1 | async-start | bytes 8388608
  15.6 5.8 %collective-permute-start.6 = (bf16[32,3200]{1,0:T(8,128)(2,1)S(1)}, bf16[32,3200]{1,0:T(8,128)(2,1)S(1)}, u32[]{:S(2)}, u32[]{:S(2)}) collective-permute-start(bf16[32,3200]{1,0:T(8,128)(2,1)S(1)} %stack.5.refs_2_.refs_0_), channel_id=1, source_target_pairs={{0,2},{1,3},{2,0},{3,1},{4,6},{5,7},{6,4},{7,5},{8,10},{9,11},{10,... | collective-permute-start | bytes 614408 | tf_op jit(solution)/shard_map/ppermute | solution.py:263
  18.3 4.8 %slice-start.2 = ((s8[12582912]{0:T(1024)(128)(4,1)}), s8[4194304]{0:T(1024)(128)(4,1)S(1)}, s32[]{:S(2)}) async-start(s8[12582912]{0:T(1024)(128)(4,1)} %bitcast.2), calls=%async_computation.2 | async-start | bytes 8388608
  18.3 4.8 %slice-start.5 = ((s8[12582912]{0:T(1024)(128)(4,1)}), s8[4194304]{0:T(1024)(128)(4,1)S(1)}, s32[]{:S(2)}) async-start(s8[12582912]{0:T(1024)(128)(4,1)} %bitcast.4), calls=%async_computation.5 | async-start | bytes 8388608
  18.3 4.8 %collective-permute-start.10 = (bf16[64,3072]{1,0:T(8,128)(2,1)S(1)}, bf16[64,3072]{1,0:T(8,128)(2,1)S(1)}, u32[]{:S(2)}, u32[]{:S(2)}) collective-permute-start(bf16[64,3072]{1,0:T(8,128)(2,1)S(1)} %stack.6.refs_2_.refs_0_), channel_id=1, source_target_pairs={{0,16},{1,17},{2,18},{3,19},{4,20},{5,21},{6,22},{7,23},{8,24},{9,... | collective-permute-start | bytes 1179656 | tf_op jit(solution)/shard_map/ppermute | solution.py:263
  18.4 7.8 %collective-permute-start.9 = (bf16[64,3072]{1,0:T(8,128)(2,1)S(1)}, bf16[64,3072]{1,0:T(8,128)(2,1)S(1)}, u32[]{:S(2)}, u32[]{:S(2)}) collective-permute-start(bf16[64,3072]{1,0:T(8,128)(2,1)S(1)} %stack.6.refs_2_.refs_0_), channel_id=1, source_target_pairs={{0,1},{1,0},{2,3},{3,2},{4,5},{5,4},{6,7},{7,6},{8,9},{9,8},{10,11... | collective-permute-start | bytes 1179656 | tf_op jit(solution)/shard_map/ppermute | solution.py:263
  21.4 4.8 %collective-permute-start.8 = (bf16[64,3200]{1,0:T(8,128)(2,1)S(1)}, bf16[64,3200]{1,0:T(8,128)(2,1)S(1)}, u32[]{:S(2)}, u32[]{:S(2)}) collective-permute-start(bf16[64,3200]{1,0:T(8,128)(2,1)S(1)} %stack.7.refs_4_.refs_0_.refs_3_), channel_id=1, source_target_pairs={{0,16},{1,17},{2,18},{3,19},{4,20},{5,21},{6,22},{7,23},{8,24},{9,... | collective-permute-start | bytes 1228808 | tf_op jit(solution)/shard_map/ppermute | solution.py:263
  21.5 9.1 %collective-permute-start.11 = (bf16[64,3200]{1,0:T(8,128)(2,1)S(1)}, bf16[64,3200]{1,0:T(8,128)(2,1)S(1)}, u32[]{:S(2)}, u32[]{:S(2)}) collective-permute-start(bf16[64,3200]{1,0:T(8,128)(2,1)S(1)} %stack.7.refs_4_.refs_0_.refs_3_), channel_id=1, source_target_pairs={{0,1},{1,0},{2,3},{3,2},{4,5},{5,4},{6,7},{7,6},{8,9},{9,8},{10,11... | collective-permute-start | bytes 1228808 | tf_op jit(solution)/shard_map/ppermute | solution.py:263
  26.2 2.1 %collective-permute-start.12 = (bf16[64,3072]{1,0:T(8,128)(2,1)S(1)}, bf16[64,3072]{1,0:T(8,128)(2,1)S(1)}, u32[]{:S(2)}, u32[]{:S(2)}) collective-permute-start(bf16[64,3072]{1,0:T(8,128)(2,1)S(1)} %collective-permute-done.9.refs_6_.refs_0_), channel_id=1, source_target_pairs={{0,16},{1,17},{2,18},{3,19},{4,20},{5,21},{6,22},{7,23},{8,24},{9,... | collective-permute-start | bytes 1179656 | tf_op jit(solution)/shard_map/ppermute | solution.py:263
  28.3 6.1 %slice-start.6 = ((s8[12582912]{0:T(1024)(128)(4,1)}), s8[4194304]{0:T(1024)(128)(4,1)S(1)}, s32[]{:S(2)}) async-start(s8[12582912]{0:T(1024)(128)(4,1)} %bitcast.6), calls=%async_computation.6 | async-start | bytes 8388608
  28.3 6.1 %slice-start.7 = ((s8[12582912]{0:T(1024)(128)(4,1)}), s8[4194304]{0:T(1024)(128)(4,1)S(1)}, s32[]{:S(2)}) async-start(s8[12582912]{0:T(1024)(128)(4,1)} %bitcast.6), calls=%async_computation.7 | async-start | bytes 8388608
  30.6 1.7 %collective-permute-start.13 = (bf16[64,3200]{1,0:T(8,128)(2,1)S(1)}, bf16[64,3200]{1,0:T(8,128)(2,1)S(1)}, u32[]{:S(2)}, u32[]{:S(2)}) collective-permute-start(bf16[64,3200]{1,0:T(8,128)(2,1)S(1)} %collective-permute-done.11.refs_0_.refs_5_), channel_id=1, source_target_pairs={{0,16},{1,17},{2,18},{3,19},{4,20},{5,21},{6,22},{7,23},{8,24},{9,... | collective-permute-start | bytes 1228808 | tf_op jit(solution)/shard_map/ppermute | solution.py:263
  32.4 2.2 %slice-start.8 = ((s8[12582912]{0:T(1024)(128)(4,1)}), s8[4194304]{0:T(1024)(128)(4,1)S(1)}, s32[]{:S(2)}) async-start(s8[12582912]{0:T(1024)(128)(4,1)} %bitcast.6), calls=%async_computation.8 | async-start | bytes 8388608
  36.4 2.4 %collective-permute-start.14 = (bf16[128,3072]{1,0:T(8,128)(2,1)S(1)}, bf16[128,3072]{1,0:T(8,128)(2,1)S(1)}, u32[]{:S(2)}, u32[]{:S(2)}) collective-permute-start(bf16[128,3072]{1,0:T(8,128)(2,1)S(1)} %get-tuple-element.46), channel_id=1, source_target_pairs={{0,16},{1,17},{2,18},{3,19},{4,20},{5,21},{6,22},{7,23},{8,24},{9,... | collective-permute-start | bytes 2359304 | tf_op jit(solution)/shard_map/ppermute | solution.py:263
  38.5 2.4 %collective-permute-start.16 = (bf16[128,3072]{1,0:T(8,128)(2,1)S(1)}, bf16[128,3072]{1,0:T(8,128)(2,1)S(1)}, u32[]{:S(2)}, u32[]{:S(2)}) collective-permute-start(bf16[128,3072]{1,0:T(8,128)(2,1)S(1)} %get-tuple-element.50), channel_id=1, source_target_pairs={{0,16},{1,17},{2,18},{3,19},{4,20},{5,21},{6,22},{7,23},{8,24},{9,... | collective-permute-start | bytes 2359304 | tf_op jit(solution)/shard_map/ppermute | solution.py:263
  38.9 7.8 %collective-permute-start.15 = (bf16[64,3072]{1,0:T(8,128)(2,1)S(1)}, bf16[64,3072]{1,0:T(8,128)(2,1)S(1)}, u32[]{:S(2)}, u32[]{:S(2)}) collective-permute-start(bf16[64,3072]{1,0:T(8,128)(2,1)S(1)} %get-tuple-element.49), channel_id=1, source_target_pairs={{0,1},{1,0},{2,3},{3,2},{4,5},{5,4},{6,7},{7,6},{8,9},{9,8},{10,11... | collective-permute-start | bytes 1179656 | tf_op jit(solution)/shard_map/ppermute | solution.py:263
  40.9 12.1 %collective-permute-start.18 = (bf16[64,3072]{1,0:T(8,128)(2,1)S(1)}, bf16[64,3072]{1,0:T(8,128)(2,1)S(1)}, u32[]{:S(2)}, u32[]{:S(2)}) collective-permute-start(bf16[64,3072]{1,0:T(8,128)(2,1)S(1)} %get-tuple-element.54), channel_id=1, source_target_pairs={{0,1},{1,0},{2,3},{3,2},{4,5},{5,4},{6,7},{7,6},{8,9},{9,8},{10,11... | collective-permute-start | bytes 1179656 | tf_op jit(solution)/shard_map/ppermute | solution.py:263
  46.9 7.8 %collective-permute-start.17 = (bf16[32,3072]{1,0:T(8,128)(2,1)S(1)}, bf16[32,3072]{1,0:T(8,128)(2,1)S(1)}, u32[]{:S(2)}, u32[]{:S(2)}) collective-permute-start(bf16[32,3072]{1,0:T(8,128)(2,1)S(1)} %get-tuple-element.53), channel_id=1, source_target_pairs={{0,2},{1,3},{2,0},{3,1},{4,6},{5,7},{6,4},{7,5},{8,10},{9,11},{10,... | collective-permute-start | bytes 589832 | tf_op jit(solution)/shard_map/ppermute | solution.py:263
  53.1 6.0 %collective-permute-start.22 = (bf16[32,3072]{1,0:T(8,128)(2,1)S(1)}, bf16[32,3072]{1,0:T(8,128)(2,1)S(1)}, u32[]{:S(2)}, u32[]{:S(2)}) collective-permute-start(bf16[32,3072]{1,0:T(8,128)(2,1)S(1)} %get-tuple-element.60), channel_id=1, source_target_pairs={{0,2},{1,3},{2,0},{3,1},{4,6},{5,7},{6,4},{7,5},{8,10},{9,11},{10,... | collective-permute-start | bytes 589832 | tf_op jit(solution)/shard_map/ppermute | solution.py:263
  54.7 7.6 %collective-permute-start.19 = (bf16[8,3072]{1,0:T(8,128)(2,1)S(1)}, bf16[8,3072]{1,0:T(8,128)(2,1)S(1)}, u32[]{:S(2)}, u32[]{:S(2)}) collective-permute-start(bf16[8,3072]{1,0:T(8,128)(2,1)S(1)} %get-tuple-element.57), channel_id=1, source_target_pairs={{0,4},{1,5},{2,6},{3,7},{4,0},{5,1},{6,2},{7,3},{8,12},{9,13},{10,... | collective-permute-start | bytes 147464 | tf_op jit(solution)/shard_map/ppermute | solution.py:263
  54.9 8.8 %collective-permute-start.20 = (bf16[8,3072]{1,0:T(8,128)(2,1)S(1)}, bf16[8,3072]{1,0:T(8,128)(2,1)S(1)}, u32[]{:S(2)}, u32[]{:S(2)}) collective-permute-start(bf16[8,3072]{1,0:T(8,128)(2,1)S(1)} %get-tuple-element.58), channel_id=1, source_target_pairs={{0,8},{1,9},{2,10},{3,11},{4,12},{5,13},{6,14},{7,15},{8,0},{9,1},... | collective-permute-start | bytes 147464 | tf_op jit(solution)/shard_map/ppermute | solution.py:263
  57.8 6.0 %collective-permute-start.21 = (bf16[8,3072]{1,0:T(8,128)(2,1)S(1)}, bf16[8,3072]{1,0:T(8,128)(2,1)S(1)}, u32[]{:S(2)}, u32[]{:S(2)}) collective-permute-start(bf16[8,3072]{1,0:T(8,128)(2,1)S(1)} %get-tuple-element.59), channel_id=1, source_target_pairs={{0,12},{1,13},{2,14},{3,15},{4,8},{5,9},{6,10},{7,11},{8,4},{9,5},... | collective-permute-start | bytes 147464 | tf_op jit(solution)/shard_map/ppermute | solution.py:263
  59.2 5.7 %collective-permute-start.23 = (bf16[8,3072]{1,0:T(8,128)(2,1)S(1)}, bf16[8,3072]{1,0:T(8,128)(2,1)S(1)}, u32[]{:S(2)}, u32[]{:S(2)}) collective-permute-start(bf16[8,3072]{1,0:T(8,128)(2,1)S(1)} %get-tuple-element.62), channel_id=1, source_target_pairs={{0,4},{1,5},{2,6},{3,7},{4,0},{5,1},{6,2},{7,3},{8,12},{9,13},{10,... | collective-permute-start | bytes 147464 | tf_op jit(solution)/shard_map/ppermute | solution.py:263
  59.3 5.7 %collective-permute-start.24 = (bf16[8,3072]{1,0:T(8,128)(2,1)S(1)}, bf16[8,3072]{1,0:T(8,128)(2,1)S(1)}, u32[]{:S(2)}, u32[]{:S(2)}) collective-permute-start(bf16[8,3072]{1,0:T(8,128)(2,1)S(1)} %get-tuple-element.63), channel_id=1, source_target_pairs={{0,8},{1,9},{2,10},{3,11},{4,12},{5,13},{6,14},{7,15},{8,0},{9,1},... | collective-permute-start | bytes 147464 | tf_op jit(solution)/shard_map/ppermute | solution.py:263
  62.3 5.9 %collective-permute-start.25 = (bf16[8,3072]{1,0:T(8,128)(2,1)S(1)}, bf16[8,3072]{1,0:T(8,128)(2,1)S(1)}, u32[]{:S(2)}, u32[]{:S(2)}) collective-permute-start(bf16[8,3072]{1,0:T(8,128)(2,1)S(1)} %get-tuple-element.64), channel_id=1, source_target_pairs={{0,12},{1,13},{2,14},{3,15},{4,8},{5,9},{6,10},{7,11},{8,4},{9,5},... | collective-permute-start | bytes 147464 | tf_op jit(solution)/shard_map/ppermute | solution.py:263

commit v3 on v2

--- a/solution.py
+++ b/solution.py
@@ -320,9 +320,9 @@
         "finish",
         jax.ShapeDtypeStruct(tokens.shape, tokens.dtype),
         totals[0],
-        *flying[0],
+        *flying[0][::-1],
         totals[1],
-        *flying[1],
+        *flying[1][::-1],
     )
 
 

time: 69.1 us -> 67.6 us (0.978)
  waiting for transfers between devices: 22.1 us -> 20.7 us
    ppermute x26, waiting for transfers between devices: 22.1 us -> 20.7 us  [permute(): lax.ppermute(r, AXES, swap_with(flips))]
  transfers between devices with their start and end apart: 26 -> 26, of which waited for: 13 -> 12; matrix products, arithmetic and copies ran while one was open for 0% -> 0% of each run, Pallas kernels for 12% -> 12%
where the time goes in v3:
time: 67.6 us; the launch traced here: 67.4 us
  starting transfers between devices  32.6 us (48%)
  waiting for transfers between devices  20.7 us (31%)
  Pallas kernels  13.8 us (20%)
    ppermute x26, starting transfers between devices, permute(): lax.ppermute(r, AXES, swap_with(flips))  32.6 us
    ppermute x26, waiting for transfers between devices, permute(): lax.ppermute(r, AXES, swap_with(flips))  20.7 us
    pallas_call x2, Pallas kernels, hidden_rows(): pl.pallas_call(lambda *refs: hidden_kernel(depth, len(parts), *refs), in_...  4.1 us
    pallas_call x2, Pallas kernels, pair(): pl.pallas_call(lambda *refs: pair_kernel(depth, len(parts), *refs), in_sp...  3.83 us
    pallas_call x2, Pallas kernels, down(): pl.pallas_call(lambda *refs: down_kernel(first, experts, len(hidden), *re...  3.58 us
  transfers between devices with their start and end apart: 26, of which 12 were waited for; matrix products, arithmetic and copies ran while one was open for 0% of the time, Pallas kernels for 12%

profile of v3, /device:TPU:0, one launch (start us, length us, event | category | flops | bytes accessed | tf_op | source)
XLA Modules:
  0.0 67.4 jit_solution(15508491392044035324)
XLA Ops:
  0.0 1.0 %cut.1 = (bf16[8,3072]{1,0:T(8,128)(2,1)S(1)}, bf16[8,3200]{1,0:T(8,128)(2,1)S(1)}) custom-call(bf16[8,6144]{1,0:T(8,128)(2,1)} %refs_0_.1, f32[2,8]{1,0:T(2,128)} %bitcast.8, s32[2,8]{1,0:T(2,128)} %bitcast.9), custom_call_target="tpu_custom_call" | custom-call | flops 1000000 | tf_op jit(solution)/shard_map/cut/pallas_call | solution.py:275
  1.0 5.1 %collective-permute-start.5 = (bf16[8,3072]{1,0:T(8,128)(2,1)S(1)}, bf16[8,3072]{1,0:T(8,128)(2,1)S(1)}, u32[]{:S(2)}, u32[]{:S(2)}) collective-permute-start(bf16[8,3072]{1,0:T(8,128)(2,1)S(1)} %get-tuple-element.36.refs_0_), channel_id=1, source_target_pairs={{0,12},{1,13},{2,14},{3,15},{4,8},{5,9},{6,10},{7,11},{8,4},{9,5},... | collective-permute-start | bytes 147464 | tf_op jit(solution)/shard_map/ppermute | solution.py:263
  6.2 0.6 collective-permute-start.3
  6.8 3.7 %collective-permute-start.2 = (bf16[8,3200]{1,0:T(8,128)(2,1)S(1)}, bf16[8,3200]{1,0:T(8,128)(2,1)S(1)}, u32[]{:S(2)}, u32[]{:S(2)}) collective-permute-start(bf16[8,3200]{1,0:T(8,128)(2,1)S(1)} %get-tuple-element.35.refs_4_.refs_0_), channel_id=1, source_target_pairs={{0,12},{1,13},{2,14},{3,15},{4,8},{5,9},{6,10},{7,11},{8,4},{9,5},... | collective-permute-start | bytes 153608 | tf_op jit(solution)/shard_map/ppermute | solution.py:263
  10.5 0.6 collective-permute-start
  11.2 1.3 %collective-permute-done.4.refs_2_ = bf16[8,3072]{1,0:T(8,128)(2,1)S(1)} collective-permute-done((bf16[8,3072]{1,0:T(8,128)(2,1)S(1)}, bf16[8,3072]{1,0:T(8,128)(2,1)S(1)}, u32[]{:S(2)}, u32[]{:S(2)}) %collective-permute-start.4) | collective-permute-done | bytes 49184 | tf_op jit(solution)/shard_map/ppermute | solution.py:263
  12.5 0.0 slice-start.4
  12.5 1.6 %collective-permute-start.7 = (bf16[32,3072]{1,0:T(8,128)(2,1)S(1)}, bf16[32,3072]{1,0:T(8,128)(2,1)S(1)}, u32[]{:S(2)}, u32[]{:S(2)}) collective-permute-start(bf16[32,3072]{1,0:T(8,128)(2,1)S(1)} %stack.4.refs_4_.refs_0_), channel_id=1, source_target_pairs={{0,2},{1,3},{2,0},{3,1},{4,6},{5,7},{6,4},{7,5},{8,10},{9,11},{10,... | collective-permute-start | bytes 589832 | tf_op jit(solution)/shard_map/ppermute | solution.py:263
  14.1 1.5 %collective-permute-done.1.refs_2_ = bf16[8,3200]{1,0:T(8,128)(2,1)S(1)} collective-permute-done((bf16[8,3200]{1,0:T(8,128)(2,1)S(1)}, bf16[8,3200]{1,0:T(8,128)(2,1)S(1)}, u32[]{:S(2)}, u32[]{:S(2)}) %collective-permute-start.1) | collective-permute-done | bytes 51232 | tf_op jit(solution)/shard_map/ppermute | solution.py:263
  15.6 1.6 %collective-permute-start.6 = (bf16[32,3200]{1,0:T(8,128)(2,1)S(1)}, bf16[32,3200]{1,0:T(8,128)(2,1)S(1)}, u32[]{:S(2)}, u32[]{:S(2)}) collective-permute-start(bf16[32,3200]{1,0:T(8,128)(2,1)S(1)} %stack.5.refs_2_.refs_0_), channel_id=1, source_target_pairs={{0,2},{1,3},{2,0},{3,1},{4,6},{5,7},{6,4},{7,5},{8,10},{9,11},{10,... | collective-permute-start | bytes 614408 | tf_op jit(solution)/shard_map/ppermute | solution.py:263
  17.1 1.1 %collective-permute-done.7.refs_1_ = bf16[32,3072]{1,0:T(8,128)(2,1)S(1)} collective-permute-done((bf16[32,3072]{1,0:T(8,128)(2,1)S(1)}, bf16[32,3072]{1,0:T(8,128)(2,1)S(1)}, u32[]{:S(2)}, u32[]{:S(2)}) %collective-permute-start.7) | collective-permute-done | bytes 196640 | tf_op jit(solution)/shard_map/ppermute | solution.py:263
  18.3 0.1 collective-permute-start.10
  18.4 1.6 %collective-permute-start.9 = (bf16[64,3072]{1,0:T(8,128)(2,1)S(1)}, bf16[64,3072]{1,0:T(8,128)(2,1)S(1)}, u32[]{:S(2)}, u32[]{:S(2)}) collective-permute-start(bf16[64,3072]{1,0:T(8,128)(2,1)S(1)} %stack.6.refs_2_.refs_0_), channel_id=1, source_target_pairs={{0,1},{1,0},{2,3},{3,2},{4,5},{5,4},{6,7},{7,6},{8,9},{9,8},{10,11... | collective-permute-start | bytes 1179656 | tf_op jit(solution)/shard_map/ppermute | solution.py:263
  20.0 1.4 %collective-permute-done.6.refs_1_ = bf16[32,3200]{1,0:T(8,128)(2,1)S(1)} collective-permute-done((bf16[32,3200]{1,0:T(8,128)(2,1)S(1)}, bf16[32,3200]{1,0:T(8,128)(2,1)S(1)}, u32[]{:S(2)}, u32[]{:S(2)}) %collective-permute-start.6) | collective-permute-done | bytes 204832 | tf_op jit(solution)/shard_map/ppermute | solution.py:263
  21.4 0.1 collective-permute-start.8
  21.5 1.6 %collective-permute-start.11 = (bf16[64,3200]{1,0:T(8,128)(2,1)S(1)}, bf16[64,3200]{1,0:T(8,128)(2,1)S(1)}, u32[]{:S(2)}, u32[]{:S(2)}) collective-permute-start(bf16[64,3200]{1,0:T(8,128)(2,1)S(1)} %stack.7.refs_4_.refs_0_.refs_3_), channel_id=1, source_target_pairs={{0,1},{1,0},{2,3},{3,2},{4,5},{5,4},{6,7},{7,6},{8,9},{9,8},{10,11... | collective-permute-start | bytes 1228808 | tf_op jit(solution)/shard_map/ppermute | solution.py:263
  23.2 1.9 %pair.2 = (f32[128,1024]{1,0:T(8,128)S(1)}, f32[128,1024]{1,0:T(8,128)S(1)}) custom-call(bf16[64,3072]{1,0:T(8,128)(2,1)S(1)} %stack.6.refs_2_.refs_0_, bf16[64,3072]{1,0:T(8,128)(2,1)S(1)} %collective-permute-done.10.refs_1_, bf16[1,6144,1024]{2,1,0:T(8,128)(2,1)S(1)} %bitcast.3, bf16[1,6144,1024]{2,1,0:T(8,128)(2,1)S(1)} %bitcast.5, ...), custom_call_target="tpu_custom_call" | custom-call | flops 100000000 | tf_op jit(solution)/shard_map/pair/pallas_call | solution.py:41
  25.1 1.2 %collective-permute-done.9.refs_6_.refs_0_ = bf16[64,3072]{1,0:T(8,128)(2,1)S(1)} collective-permute-done((bf16[64,3072]{1,0:T(8,128)(2,1)S(1)}, bf16[64,3072]{1,0:T(8,128)(2,1)S(1)}, u32[]{:S(2)}, u32[]{:S(2)}) %collective-permute-start.9) | collective-permute-done | bytes 393248 | tf_op jit(solution)/shard_map/ppermute | solution.py:263
  26.3 2.0 %hidden_rows.2.refs_4_.refs_0_ = bf16[128,1024]{1,0:T(8,128)(2,1)S(1)} custom-call(bf16[64,3200]{1,0:T(8,128)(2,1)S(1)} %stack.7.refs_4_.refs_0_.refs_3_, bf16[64,3200]{1,0:T(8,128)(2,1)S(1)} %collective-permute-done.8.refs_1_.refs_4_, bf16[1,6144,1024]{2,1,0:T(8,128)(2,1)S(1)} %bitcast.3, bf16[1,6144,1024]{2,1,0:T(8,128)(2,1)S(1)} %bitcast.5, ...), custom_call_target="tpu_custom_call" | custom-call | flops 100000000 | tf_op jit(solution)/shard_map/hidden_rows/pallas_call | solution.py:71
  28.3 1.9 %pair.3 = (f32[128,1024]{1,0:T(8,128)S(1)}, f32[128,1024]{1,0:T(8,128)S(1)}) custom-call(bf16[64,3072]{1,0:T(8,128)(2,1)S(1)} %collective-permute-done.9.refs_6_.refs_0_, bf16[64,3072]{1,0:T(8,128)(2,1)S(1)} %collective-permute-done.12.refs_1_, bf16[1,6144,1024]{2,1,0:T(8,128)(2,1)S(1)} %bitcast.3, bf16[1,6144,1024]{2,1,0:T(8,128)(2,1)S(1)} %bitcast.5, ...), custom_call_target="tpu_custom_call" | custom-call | flops 100000000 | tf_op jit(solution)/shard_map/pair/pallas_call | solution.py:41
  30.3 0.4 collective-permute-done.11.refs_0_.refs_5_
  30.6 0.2 collective-permute-start.13
  30.9 1.5 %collective-permute-done.13.refs_1_.refs_6_ = bf16[64,3200]{1,0:T(8,128)(2,1)S(1)} collective-permute-done((bf16[64,3200]{1,0:T(8,128)(2,1)S(1)}, bf16[64,3200]{1,0:T(8,128)(2,1)S(1)}, u32[]{:S(2)}, u32[]{:S(2)}) %collective-permute-start.13) | collective-permute-done | bytes 409632 | tf_op jit(solution)/shard_map/ppermute | solution.py:263
  32.4 2.1 %hidden_rows.3.refs_1_ = bf16[128,1024]{1,0:T(8,128)(2,1)S(1)} custom-call(bf16[64,3200]{1,0:T(8,128)(2,1)S(1)} %collective-permute-done.11.refs_0_.refs_5_, bf16[64,3200]{1,0:T(8,128)(2,1)S(1)} %collective-permute-done.13.refs_1_.refs_6_, bf16[1,6144,1024]{2,1,0:T(8,128)(2,1)S(1)} %bitcast.3, bf16[1,6144,1024]{2,1,0:T(8,128)(2,1)S(1)} %bitcast.5, ...), custom_call_target="tpu_custom_call" | custom-call | flops 100000000 | tf_op jit(solution)/shard_map/hidden_rows/pallas_call | solution.py:71
  34.5 0.1 slice-done.8
  34.6 1.8 %down.2 = (f32[128,3072]{1,0:T(8,128)S(1)}, bf16[128,3072]{1,0:T(8,128)(2,1)S(1)}) custom-call(bf16[128,1024]{1,0:T(8,128)(2,1)S(1)} %hidden_rows.2.refs_4_.refs_0_, bf16[128,1024]{1,0:T(8,128)(2,1)S(1)} %hidden_rows.3.refs_1_, bf16[1,1024,6144]{2,1,0:T(8,128)(2,1)S(1)} %bitcast.7, bf16[64,3200]{1,0:T(8,128)(2,1)S(1)} %stack.7.refs_4_.refs_0_.refs_3_, ...), custom_call_target="tpu_custom_call" | custom-call | flops 100000000 | tf_op jit(solution)/shard_map/down/pallas_call | solution.py:116
  36.4 0.3 collective-permute-start.14
  36.7 1.8 %down.3 = (f32[128,3072]{1,0:T(8,128)S(1)}, bf16[128,3072]{1,0:T(8,128)(2,1)S(1)}) custom-call(bf16[128,1024]{1,0:T(8,128)(2,1)S(1)} %hidden_rows.2.refs_4_.refs_0_, bf16[128,1024]{1,0:T(8,128)(2,1)S(1)} %hidden_rows.3.refs_1_, bf16[1,1024,6144]{2,1,0:T(8,128)(2,1)S(1)} %bitcast.7, bf16[64,3200]{1,0:T(8,128)(2,1)S(1)} %stack.7.refs_4_.refs_0_.refs_3_, ...), custom_call_target="tpu_custom_call" | custom-call | flops 100000000 | tf_op jit(solution)/shard_map/down/pallas_call | solution.py:116
  38.5 0.4 collective-permute-start.16
  38.8 0.1 merge.6
  38.9 1.6 %collective-permute-start.15 = (bf16[64,3072]{1,0:T(8,128)(2,1)S(1)}, bf16[64,3072]{1,0:T(8,128)(2,1)S(1)}, u32[]{:S(2)}, u32[]{:S(2)}) collective-permute-start(bf16[64,3072]{1,0:T(8,128)(2,1)S(1)} %get-tuple-element.49), channel_id=1, source_target_pairs={{0,1},{1,0},{2,3},{3,2},{4,5},{5,4},{6,7},{7,6},{8,9},{9,8},{10,11... | collective-permute-start | bytes 1179656 | tf_op jit(solution)/shard_map/ppermute | solution.py:263
  40.5 0.3 collective-permute-done.16.refs_1_
  40.8 0.1 merge.7
  40.9 1.6 %collective-permute-start.18 = (bf16[64,3072]{1,0:T(8,128)(2,1)S(1)}, bf16[64,3072]{1,0:T(8,128)(2,1)S(1)}, u32[]{:S(2)}, u32[]{:S(2)}) collective-permute-start(bf16[64,3072]{1,0:T(8,128)(2,1)S(1)} %get-tuple-element.54), channel_id=1, source_target_pairs={{0,1},{1,0},{2,3},{3,2},{4,5},{5,4},{6,7},{7,6},{8,9},{9,8},{10,11... | collective-permute-start | bytes 1179656 | tf_op jit(solution)/shard_map/ppermute | solution.py:263
  42.5 4.3 %collective-permute-done.15.refs_1_ = bf16[64,3072]{1,0:T(8,128)(2,1)S(1)} collective-permute-done((bf16[64,3072]{1,0:T(8,128)(2,1)S(1)}, bf16[64,3072]{1,0:T(8,128)(2,1)S(1)}, u32[]{:S(2)}, u32[]{:S(2)}) %collective-permute-start.15) | collective-permute-done | bytes 393248 | tf_op jit(solution)/shard_map/ppermute | solution.py:263
  46.8 0.1 merge.8
  46.9 1.6 %collective-permute-start.17 = (bf16[32,3072]{1,0:T(8,128)(2,1)S(1)}, bf16[32,3072]{1,0:T(8,128)(2,1)S(1)}, u32[]{:S(2)}, u32[]{:S(2)}) collective-permute-start(bf16[32,3072]{1,0:T(8,128)(2,1)S(1)} %get-tuple-element.53), channel_id=1, source_target_pairs={{0,2},{1,3},{2,0},{3,1},{4,6},{5,7},{6,4},{7,5},{8,10},{9,11},{10,... | collective-permute-start | bytes 589832 | tf_op jit(solution)/shard_map/ppermute | solution.py:263
  48.4 4.6 %collective-permute-done.18.refs_1_ = bf16[64,3072]{1,0:T(8,128)(2,1)S(1)} collective-permute-done((bf16[64,3072]{1,0:T(8,128)(2,1)S(1)}, bf16[64,3072]{1,0:T(8,128)(2,1)S(1)}, u32[]{:S(2)}, u32[]{:S(2)}) %collective-permute-start.18) | collective-permute-done | bytes 393248 | tf_op jit(solution)/shard_map/ppermute | solution.py:263
  53.1 0.1 merge.9
  53.1 1.6 %collective-permute-start.22 = (bf16[32,3072]{1,0:T(8,128)(2,1)S(1)}, bf16[32,3072]{1,0:T(8,128)(2,1)S(1)}, u32[]{:S(2)}, u32[]{:S(2)}) collective-permute-start(bf16[32,3072]{1,0:T(8,128)(2,1)S(1)} %get-tuple-element.60), channel_id=1, source_target_pairs={{0,2},{1,3},{2,0},{3,1},{4,6},{5,7},{6,4},{7,5},{8,10},{9,11},{10,... | collective-permute-start | bytes 589832 | tf_op jit(solution)/shard_map/ppermute | solution.py:263
  54.7 2.5 %collective-permute-start.19 = (bf16[8,3072]{1,0:T(8,128)(2,1)S(1)}, bf16[8,3072]{1,0:T(8,128)(2,1)S(1)}, u32[]{:S(2)}, u32[]{:S(2)}) collective-permute-start(bf16[8,3072]{1,0:T(8,128)(2,1)S(1)} %get-tuple-element.57), channel_id=1, source_target_pairs={{0,12},{1,13},{2,14},{3,15},{4,8},{5,9},{6,10},{7,11},{8,4},{9,5},... | collective-permute-start | bytes 147464 | tf_op jit(solution)/shard_map/ppermute | solution.py:263
  57.2 1.9 %collective-permute-start.21 = (bf16[8,3072]{1,0:T(8,128)(2,1)S(1)}, bf16[8,3072]{1,0:T(8,128)(2,1)S(1)}, u32[]{:S(2)}, u32[]{:S(2)}) collective-permute-start(bf16[8,3072]{1,0:T(8,128)(2,1)S(1)} %get-tuple-element.59), channel_id=1, source_target_pairs={{0,4},{1,5},{2,6},{3,7},{4,0},{5,1},{6,2},{7,3},{8,12},{9,13},{10,... | collective-permute-start | bytes 147464 | tf_op jit(solution)/shard_map/ppermute | solution.py:263
  59.2 2.5 %collective-permute-start.23 = (bf16[8,3072]{1,0:T(8,128)(2,1)S(1)}, bf16[8,3072]{1,0:T(8,128)(2,1)S(1)}, u32[]{:S(2)}, u32[]{:S(2)}) collective-permute-start(bf16[8,3072]{1,0:T(8,128)(2,1)S(1)} %get-tuple-element.62), channel_id=1, source_target_pairs={{0,12},{1,13},{2,14},{3,15},{4,8},{5,9},{6,10},{7,11},{8,4},{9,5},... | collective-permute-start | bytes 147464 | tf_op jit(solution)/shard_map/ppermute | solution.py:263
  61.7 1.9 %collective-permute-start.25 = (bf16[8,3072]{1,0:T(8,128)(2,1)S(1)}, bf16[8,3072]{1,0:T(8,128)(2,1)S(1)}, u32[]{:S(2)}, u32[]{:S(2)}) collective-permute-start(bf16[8,3072]{1,0:T(8,128)(2,1)S(1)} %get-tuple-element.64), channel_id=1, source_target_pairs={{0,4},{1,5},{2,6},{3,7},{4,0},{5,1},{6,2},{7,3},{8,12},{9,13},{10,... | collective-permute-start | bytes 147464 | tf_op jit(solution)/shard_map/ppermute | solution.py:263
  63.7 0.0 collective-permute-done.20.refs_2_
  63.7 1.4 %collective-permute-done.23.refs_5_ = bf16[8,3072]{1,0:T(8,128)(2,1)S(1)} collective-permute-done((bf16[8,3072]{1,0:T(8,128)(2,1)S(1)}, bf16[8,3072]{1,0:T(8,128)(2,1)S(1)}, u32[]{:S(2)}, u32[]{:S(2)}) %collective-permute-start.23) | collective-permute-done | bytes 49184 | tf_op jit(solution)/shard_map/ppermute | solution.py:263
  65.2 1.6 %collective-permute-done.24.refs_6_ = bf16[8,3072]{1,0:T(8,128)(2,1)S(1)} collective-permute-done((bf16[8,3072]{1,0:T(8,128)(2,1)S(1)}, bf16[8,3072]{1,0:T(8,128)(2,1)S(1)}, u32[]{:S(2)}, u32[]{:S(2)}) %collective-permute-start.24) | collective-permute-done | bytes 49184 | tf_op jit(solution)/shard_map/ppermute | solution.py:263
  66.7 0.7 %finish.1 = bf16[8,6144]{1,0:T(8,128)(2,1)} custom-call(f32[8,3072]{1,0:T(8,128)S(1)} %get-tuple-element.56.refs_2_.refs_0_, bf16[8,3072]{1,0:T(8,128)(2,1)S(1)} %collective-permute-done.19.refs_1_, bf16[8,3072]{1,0:T(8,128)(2,1)S(1)} %collective-permute-done.20.refs_2_, bf16[8,3072]{1,0:T(8,128)(2,1)S(1)} %collective-permute-done.21.refs_3_, ...), custom_call_target="tpu_custom_call" | custom-call | flops 1000000 | tf_op jit(solution)/shard_map/finish/pallas_call | solution.py:133
  (43 shorter events, 0.2 us)
Async XLA Ops:
  1.0 9.5 %collective-permute-start.5 = (bf16[8,3072]{1,0:T(8,128)(2,1)S(1)}, bf16[8,3072]{1,0:T(8,128)(2,1)S(1)}, u32[]{:S(2)}, u32[]{:S(2)}) collective-permute-start(bf16[8,3072]{1,0:T(8,128)(2,1)S(1)} %get-tuple-element.36.refs_0_), channel_id=1, source_target_pairs={{0,12},{1,13},{2,14},{3,15},{4,8},{5,9},{6,10},{7,11},{8,4},{9,5},... | collective-permute-start | bytes 147464 | tf_op jit(solution)/shard_map/ppermute | solution.py:263
  6.2 6.3 %collective-permute-start.4 = (bf16[8,3072]{1,0:T(8,128)(2,1)S(1)}, bf16[8,3072]{1,0:T(8,128)(2,1)S(1)}, u32[]{:S(2)}, u32[]{:S(2)}) collective-permute-start(bf16[8,3072]{1,0:T(8,128)(2,1)S(1)} %get-tuple-element.36.refs_0_), channel_id=1, source_target_pairs={{0,8},{1,9},{2,10},{3,11},{4,12},{5,13},{6,14},{7,15},{8,0},{9,1},... | collective-permute-start | bytes 147464 | tf_op jit(solution)/shard_map/ppermute | solution.py:263
  6.2 6.3 %collective-permute-start.3 = (bf16[8,3072]{1,0:T(8,128)(2,1)S(1)}, bf16[8,3072]{1,0:T(8,128)(2,1)S(1)}, u32[]{:S(2)}, u32[]{:S(2)}) collective-permute-start(bf16[8,3072]{1,0:T(8,128)(2,1)S(1)} %get-tuple-element.36.refs_0_), channel_id=1, source_target_pairs={{0,4},{1,5},{2,6},{3,7},{4,0},{5,1},{6,2},{7,3},{8,12},{9,13},{10,... | collective-permute-start | bytes 147464 | tf_op jit(solution)/shard_map/ppermute | solution.py:263
  6.8 7.3 %collective-permute-start.2 = (bf16[8,3200]{1,0:T(8,128)(2,1)S(1)}, bf16[8,3200]{1,0:T(8,128)(2,1)S(1)}, u32[]{:S(2)}, u32[]{:S(2)}) collective-permute-start(bf16[8,3200]{1,0:T(8,128)(2,1)S(1)} %get-tuple-element.35.refs_4_.refs_0_), channel_id=1, source_target_pairs={{0,12},{1,13},{2,14},{3,15},{4,8},{5,9},{6,10},{7,11},{8,4},{9,5},... | collective-permute-start | bytes 153608 | tf_op jit(solution)/shard_map/ppermute | solution.py:263
  10.5 5.0 %collective-permute-start.1 = (bf16[8,3200]{1,0:T(8,128)(2,1)S(1)}, bf16[8,3200]{1,0:T(8,128)(2,1)S(1)}, u32[]{:S(2)}, u32[]{:S(2)}) collective-permute-start(bf16[8,3200]{1,0:T(8,128)(2,1)S(1)} %get-tuple-element.35.refs_4_.refs_0_), channel_id=1, source_target_pairs={{0,8},{1,9},{2,10},{3,11},{4,12},{5,13},{6,14},{7,15},{8,0},{9,1},... | collective-permute-start | bytes 153608 | tf_op jit(solution)/shard_map/ppermute | solution.py:263
  10.5 5.0 %collective-permute-start = (bf16[8,3200]{1,0:T(8,128)(2,1)S(1)}, bf16[8,3200]{1,0:T(8,128)(2,1)S(1)}, u32[]{:S(2)}, u32[]{:S(2)}) collective-permute-start(bf16[8,3200]{1,0:T(8,128)(2,1)S(1)} %get-tuple-element.35.refs_4_.refs_0_), channel_id=1, source_target_pairs={{0,4},{1,5},{2,6},{3,7},{4,0},{5,1},{6,2},{7,3},{8,12},{9,13},{10,... | collective-permute-start | bytes 153608 | tf_op jit(solution)/shard_map/ppermute | solution.py:263
  12.5 10.6 %slice-start.3 = ((s8[12582912]{0:T(1024)(128)(4,1)}), s8[4194304]{0:T(1024)(128)(4,1)S(1)}, s32[]{:S(2)}) async-start(s8[12582912]{0:T(1024)(128)(4,1)} %bitcast.4), calls=%async_computation.3 | async-start | bytes 8388608
  12.5 10.6 %slice-start.4 = ((s8[12582912]{0:T(1024)(128)(4,1)}), s8[4194304]{0:T(1024)(128)(4,1)S(1)}, s32[]{:S(2)}) async-start(s8[12582912]{0:T(1024)(128)(4,1)} %bitcast.4), calls=%async_computation.4 | async-start | bytes 8388608
  12.5 5.7 %collective-permute-start.7 = (bf16[32,3072]{1,0:T(8,128)(2,1)S(1)}, bf16[32,3072]{1,0:T(8,128)(2,1)S(1)}, u32[]{:S(2)}, u32[]{:S(2)}) collective-permute-start(bf16[32,3072]{1,0:T(8,128)(2,1)S(1)} %stack.4.refs_4_.refs_0_), channel_id=1, source_target_pairs={{0,2},{1,3},{2,0},{3,1},{4,6},{5,7},{6,4},{7,5},{8,10},{9,11},{10,... | collective-permute-start | bytes 589832 | tf_op jit(solution)/shard_map/ppermute | solution.py:263
  15.6 7.6 %slice-start = ((s8[12582912]{0:T(1024)(128)(4,1)}), s8[4194304]{0:T(1024)(128)(4,1)S(1)}, s32[]{:S(2)}) async-start(s8[12582912]{0:T(1024)(128)(4,1)} %bitcast.2), calls=%async_computation | async-start | bytes 8388608
  15.6 7.6 %slice-start.1 = ((s8[12582912]{0:T(1024)(128)(4,1)}), s8[4194304]{0:T(1024)(128)(4,1)S(1)}, s32[]{:S(2)}) async-start(s8[12582912]{0:T(1024)(128)(4,1)} %bitcast.2), calls=%async_computation.1 | async-start | bytes 8388608
  15.6 5.8 %collective-permute-start.6 = (bf16[32,3200]{1,0:T(8,128)(2,1)S(1)}, bf16[32,3200]{1,0:T(8,128)(2,1)S(1)}, u32[]{:S(2)}, u32[]{:S(2)}) collective-permute-start(bf16[32,3200]{1,0:T(8,128)(2,1)S(1)} %stack.5.refs_2_.refs_0_), channel_id=1, source_target_pairs={{0,2},{1,3},{2,0},{3,1},{4,6},{5,7},{6,4},{7,5},{8,10},{9,11},{10,... | collective-permute-start | bytes 614408 | tf_op jit(solution)/shard_map/ppermute | solution.py:263
  18.3 4.8 %slice-start.2 = ((s8[12582912]{0:T(1024)(128)(4,1)}), s8[4194304]{0:T(1024)(128)(4,1)S(1)}, s32[]{:S(2)}) async-start(s8[12582912]{0:T(1024)(128)(4,1)} %bitcast.2), calls=%async_computation.2 | async-start | bytes 8388608
  18.3 4.8 %slice-start.5 = ((s8[12582912]{0:T(1024)(128)(4,1)}), s8[4194304]{0:T(1024)(128)(4,1)S(1)}, s32[]{:S(2)}) async-start(s8[12582912]{0:T(1024)(128)(4,1)} %bitcast.4), calls=%async_computation.5 | async-start | bytes 8388608
  18.3 4.8 %collective-permute-start.10 = (bf16[64,3072]{1,0:T(8,128)(2,1)S(1)}, bf16[64,3072]{1,0:T(8,128)(2,1)S(1)}, u32[]{:S(2)}, u32[]{:S(2)}) collective-permute-start(bf16[64,3072]{1,0:T(8,128)(2,1)S(1)} %stack.6.refs_2_.refs_0_), channel_id=1, source_target_pairs={{0,16},{1,17},{2,18},{3,19},{4,20},{5,21},{6,22},{7,23},{8,24},{9,... | collective-permute-start | bytes 1179656 | tf_op jit(solution)/shard_map/ppermute | solution.py:263
  18.4 7.8 %collective-permute-start.9 = (bf16[64,3072]{1,0:T(8,128)(2,1)S(1)}, bf16[64,3072]{1,0:T(8,128)(2,1)S(1)}, u32[]{:S(2)}, u32[]{:S(2)}) collective-permute-start(bf16[64,3072]{1,0:T(8,128)(2,1)S(1)} %stack.6.refs_2_.refs_0_), channel_id=1, source_target_pairs={{0,1},{1,0},{2,3},{3,2},{4,5},{5,4},{6,7},{7,6},{8,9},{9,8},{10,11... | collective-permute-start | bytes 1179656 | tf_op jit(solution)/shard_map/ppermute | solution.py:263
  21.4 4.8 %collective-permute-start.8 = (bf16[64,3200]{1,0:T(8,128)(2,1)S(1)}, bf16[64,3200]{1,0:T(8,128)(2,1)S(1)}, u32[]{:S(2)}, u32[]{:S(2)}) collective-permute-start(bf16[64,3200]{1,0:T(8,128)(2,1)S(1)} %stack.7.refs_4_.refs_0_.refs_3_), channel_id=1, source_target_pairs={{0,16},{1,17},{2,18},{3,19},{4,20},{5,21},{6,22},{7,23},{8,24},{9,... | collective-permute-start | bytes 1228808 | tf_op jit(solution)/shard_map/ppermute | solution.py:263
  21.5 9.1 %collective-permute-start.11 = (bf16[64,3200]{1,0:T(8,128)(2,1)S(1)}, bf16[64,3200]{1,0:T(8,128)(2,1)S(1)}, u32[]{:S(2)}, u32[]{:S(2)}) collective-permute-start(bf16[64,3200]{1,0:T(8,128)(2,1)S(1)} %stack.7.refs_4_.refs_0_.refs_3_), channel_id=1, source_target_pairs={{0,1},{1,0},{2,3},{3,2},{4,5},{5,4},{6,7},{7,6},{8,9},{9,8},{10,11... | collective-permute-start | bytes 1228808 | tf_op jit(solution)/shard_map/ppermute | solution.py:263
  26.2 2.1 %collective-permute-start.12 = (bf16[64,3072]{1,0:T(8,128)(2,1)S(1)}, bf16[64,3072]{1,0:T(8,128)(2,1)S(1)}, u32[]{:S(2)}, u32[]{:S(2)}) collective-permute-start(bf16[64,3072]{1,0:T(8,128)(2,1)S(1)} %collective-permute-done.9.refs_6_.refs_0_), channel_id=1, source_target_pairs={{0,16},{1,17},{2,18},{3,19},{4,20},{5,21},{6,22},{7,23},{8,24},{9,... | collective-permute-start | bytes 1179656 | tf_op jit(solution)/shard_map/ppermute | solution.py:263
  28.3 6.1 %slice-start.6 = ((s8[12582912]{0:T(1024)(128)(4,1)}), s8[4194304]{0:T(1024)(128)(4,1)S(1)}, s32[]{:S(2)}) async-start(s8[12582912]{0:T(1024)(128)(4,1)} %bitcast.6), calls=%async_computation.6 | async-start | bytes 8388608
  28.3 6.1 %slice-start.7 = ((s8[12582912]{0:T(1024)(128)(4,1)}), s8[4194304]{0:T(1024)(128)(4,1)S(1)}, s32[]{:S(2)}) async-start(s8[12582912]{0:T(1024)(128)(4,1)} %bitcast.6), calls=%async_computation.7 | async-start | bytes 8388608
  30.6 1.7 %collective-permute-start.13 = (bf16[64,3200]{1,0:T(8,128)(2,1)S(1)}, bf16[64,3200]{1,0:T(8,128)(2,1)S(1)}, u32[]{:S(2)}, u32[]{:S(2)}) collective-permute-start(bf16[64,3200]{1,0:T(8,128)(2,1)S(1)} %collective-permute-done.11.refs_0_.refs_5_), channel_id=1, source_target_pairs={{0,16},{1,17},{2,18},{3,19},{4,20},{5,21},{6,22},{7,23},{8,24},{9,... | collective-permute-start | bytes 1228808 | tf_op jit(solution)/shard_map/ppermute | solution.py:263
  32.4 2.2 %slice-start.8 = ((s8[12582912]{0:T(1024)(128)(4,1)}), s8[4194304]{0:T(1024)(128)(4,1)S(1)}, s32[]{:S(2)}) async-start(s8[12582912]{0:T(1024)(128)(4,1)} %bitcast.6), calls=%async_computation.8 | async-start | bytes 8388608
  36.4 2.4 %collective-permute-start.14 = (bf16[128,3072]{1,0:T(8,128)(2,1)S(1)}, bf16[128,3072]{1,0:T(8,128)(2,1)S(1)}, u32[]{:S(2)}, u32[]{:S(2)}) collective-permute-start(bf16[128,3072]{1,0:T(8,128)(2,1)S(1)} %get-tuple-element.46), channel_id=1, source_target_pairs={{0,16},{1,17},{2,18},{3,19},{4,20},{5,21},{6,22},{7,23},{8,24},{9,... | collective-permute-start | bytes 2359304 | tf_op jit(solution)/shard_map/ppermute | solution.py:263
  38.5 2.4 %collective-permute-start.16 = (bf16[128,3072]{1,0:T(8,128)(2,1)S(1)}, bf16[128,3072]{1,0:T(8,128)(2,1)S(1)}, u32[]{:S(2)}, u32[]{:S(2)}) collective-permute-start(bf16[128,3072]{1,0:T(8,128)(2,1)S(1)} %get-tuple-element.50), channel_id=1, source_target_pairs={{0,16},{1,17},{2,18},{3,19},{4,20},{5,21},{6,22},{7,23},{8,24},{9,... | collective-permute-start | bytes 2359304 | tf_op jit(solution)/shard_map/ppermute | solution.py:263
  38.9 7.8 %collective-permute-start.15 = (bf16[64,3072]{1,0:T(8,128)(2,1)S(1)}, bf16[64,3072]{1,0:T(8,128)(2,1)S(1)}, u32[]{:S(2)}, u32[]{:S(2)}) collective-permute-start(bf16[64,3072]{1,0:T(8,128)(2,1)S(1)} %get-tuple-element.49), channel_id=1, source_target_pairs={{0,1},{1,0},{2,3},{3,2},{4,5},{5,4},{6,7},{7,6},{8,9},{9,8},{10,11... | collective-permute-start | bytes 1179656 | tf_op jit(solution)/shard_map/ppermute | solution.py:263
  40.9 12.1 %collective-permute-start.18 = (bf16[64,3072]{1,0:T(8,128)(2,1)S(1)}, bf16[64,3072]{1,0:T(8,128)(2,1)S(1)}, u32[]{:S(2)}, u32[]{:S(2)}) collective-permute-start(bf16[64,3072]{1,0:T(8,128)(2,1)S(1)} %get-tuple-element.54), channel_id=1, source_target_pairs={{0,1},{1,0},{2,3},{3,2},{4,5},{5,4},{6,7},{7,6},{8,9},{9,8},{10,11... | collective-permute-start | bytes 1179656 | tf_op jit(solution)/shard_map/ppermute | solution.py:263
  46.9 7.8 %collective-permute-start.17 = (bf16[32,3072]{1,0:T(8,128)(2,1)S(1)}, bf16[32,3072]{1,0:T(8,128)(2,1)S(1)}, u32[]{:S(2)}, u32[]{:S(2)}) collective-permute-start(bf16[32,3072]{1,0:T(8,128)(2,1)S(1)} %get-tuple-element.53), channel_id=1, source_target_pairs={{0,2},{1,3},{2,0},{3,1},{4,6},{5,7},{6,4},{7,5},{8,10},{9,11},{10,... | collective-permute-start | bytes 589832 | tf_op jit(solution)/shard_map/ppermute | solution.py:263
  53.1 6.1 %collective-permute-start.22 = (bf16[32,3072]{1,0:T(8,128)(2,1)S(1)}, bf16[32,3072]{1,0:T(8,128)(2,1)S(1)}, u32[]{:S(2)}, u32[]{:S(2)}) collective-permute-start(bf16[32,3072]{1,0:T(8,128)(2,1)S(1)} %get-tuple-element.60), channel_id=1, source_target_pairs={{0,2},{1,3},{2,0},{3,1},{4,6},{5,7},{6,4},{7,5},{8,10},{9,11},{10,... | collective-permute-start | bytes 589832 | tf_op jit(solution)/shard_map/ppermute | solution.py:263
  54.7 7.0 %collective-permute-start.19 = (bf16[8,3072]{1,0:T(8,128)(2,1)S(1)}, bf16[8,3072]{1,0:T(8,128)(2,1)S(1)}, u32[]{:S(2)}, u32[]{:S(2)}) collective-permute-start(bf16[8,3072]{1,0:T(8,128)(2,1)S(1)} %get-tuple-element.57), channel_id=1, source_target_pairs={{0,12},{1,13},{2,14},{3,15},{4,8},{5,9},{6,10},{7,11},{8,4},{9,5},... | collective-permute-start | bytes 147464 | tf_op jit(solution)/shard_map/ppermute | solution.py:263
  57.2 6.5 %collective-permute-start.20 = (bf16[8,3072]{1,0:T(8,128)(2,1)S(1)}, bf16[8,3072]{1,0:T(8,128)(2,1)S(1)}, u32[]{:S(2)}, u32[]{:S(2)}) collective-permute-start(bf16[8,3072]{1,0:T(8,128)(2,1)S(1)} %get-tuple-element.58), channel_id=1, source_target_pairs={{0,8},{1,9},{2,10},{3,11},{4,12},{5,13},{6,14},{7,15},{8,0},{9,1},... | collective-permute-start | bytes 147464 | tf_op jit(solution)/shard_map/ppermute | solution.py:263
  57.2 6.5 %collective-permute-start.21 = (bf16[8,3072]{1,0:T(8,128)(2,1)S(1)}, bf16[8,3072]{1,0:T(8,128)(2,1)S(1)}, u32[]{:S(2)}, u32[]{:S(2)}) collective-permute-start(bf16[8,3072]{1,0:T(8,128)(2,1)S(1)} %get-tuple-element.59), channel_id=1, source_target_pairs={{0,4},{1,5},{2,6},{3,7},{4,0},{5,1},{6,2},{7,3},{8,12},{9,13},{10,... | collective-permute-start | bytes 147464 | tf_op jit(solution)/shard_map/ppermute | solution.py:263
  59.2 6.0 %collective-permute-start.23 = (bf16[8,3072]{1,0:T(8,128)(2,1)S(1)}, bf16[8,3072]{1,0:T(8,128)(2,1)S(1)}, u32[]{:S(2)}, u32[]{:S(2)}) collective-permute-start(bf16[8,3072]{1,0:T(8,128)(2,1)S(1)} %get-tuple-element.62), channel_id=1, source_target_pairs={{0,12},{1,13},{2,14},{3,15},{4,8},{5,9},{6,10},{7,11},{8,4},{9,5},... | collective-permute-start | bytes 147464 | tf_op jit(solution)/shard_map/ppermute | solution.py:263
  61.7 5.0 %collective-permute-start.24 = (bf16[8,3072]{1,0:T(8,128)(2,1)S(1)}, bf16[8,3072]{1,0:T(8,128)(2,1)S(1)}, u32[]{:S(2)}, u32[]{:S(2)}) collective-permute-start(bf16[8,3072]{1,0:T(8,128)(2,1)S(1)} %get-tuple-element.63), channel_id=1, source_target_pairs={{0,8},{1,9},{2,10},{3,11},{4,12},{5,13},{6,14},{7,15},{8,0},{9,1},... | collective-permute-start | bytes 147464 | tf_op jit(solution)/shard_map/ppermute | solution.py:263
  61.7 5.0 %collective-permute-start.25 = (bf16[8,3072]{1,0:T(8,128)(2,1)S(1)}, bf16[8,3072]{1,0:T(8,128)(2,1)S(1)}, u32[]{:S(2)}, u32[]{:S(2)}) collective-permute-start(bf16[8,3072]{1,0:T(8,128)(2,1)S(1)} %get-tuple-element.64), channel_id=1, source_target_pairs={{0,4},{1,5},{2,6},{3,7},{4,0},{5,1},{6,2},{7,3},{8,12},{9,13},{10,... | collective-permute-start | bytes 147464 | tf_op jit(solution)/shard_map/ppermute | solution.py:263

commit v4 on v3

--- a/solution.py
+++ b/solution.py
@@ -11,6 +11,7 @@
 SCOPED = 1 << 20
 SMALL = 2 << 20
 GIGA = 10**9
+MERGE_COST = (0.001, 0.001, 0.001)
 STACK_COST = ((1, 1), (4, 4))
 FFN_COST = (0.1, 0.1, 0.1, 0.1, 0.1)
 STRIP = 512
@@ -204,31 +205,31 @@
     )
 
 
-def merge_kernel(taken, fan, total_ref, *refs):
-    received, (keep_ref, *sent) = refs[:taken], refs[len(refs) - fan :]
-    count = keep_ref.shape[0]
-    for at in range(0, total_ref.shape[1], STRIP):
-        columns = pl.ds(at, STRIP)
-        total = total_ref[:, columns]
-        for r in received:
-            total = total + r[:, columns].astype(jnp.float32)
-        keep_ref[:, columns] = total[:count]
-        for k in range(1, fan):
+def fold_kernel(places, fan, *refs):
+    sources, outs = refs[: len(places)], refs[len(refs) - fan :]
+    count, width = outs[0].shape
+    for at in range(0, width, STRIP):
+        total = 0.0
+        for ref, (row, column) in zip(sources, places):
+            piece = ref[pl.ds(row, fan * count), pl.ds(column + at, STRIP)]
+            total = total + piece.astype(jnp.float32)
+        for k, out_ref in enumerate(outs):
             piece = total[k * count : (k + 1) * count]
-            sent[k - 1][:, columns] = piece.astype(jnp.bfloat16)
-
-
-def merge(total, received, fan, after):
-    shape = (total.shape[0] // fan, total.shape[1])
-    keep, *sent = small_call(
-        lambda *refs: merge_kernel(len(received), fan, *refs),
-        "merge",
-        [jax.ShapeDtypeStruct(shape, jnp.float32 if k == 0 else jnp.bfloat16) for k in range(fan)],
-        total,
-        *received,
+            out_ref[:, pl.ds(at, STRIP)] = piece.astype(out_ref.dtype)
+
+
+def fold(sources, shape, types, cost, after=()):
+    places = [place for _, *place in sources]
+    fan = len(types)
+    shape = (shape[0] // fan, shape[1])
+    return small_call(
+        lambda *refs: fold_kernel(places, fan, *refs),
+        "fold",
+        [jax.ShapeDtypeStruct(shape, t) for t in types],
+        *[source for source, *_ in sources],
         after=after,
-    )
-    return keep, sent
+        flops=int(cost * GIGA),
+    )
 
 
 def finish_kernel(taken, *refs):
@@ -311,9 +312,35 @@
         kept, sent = down(experts, hidden, w_down, parts, c, width, cost[4])
         totals.append(kept)
         flying.append(permute([sent], core_swap))
-    for step in steps[::-1]:
+    near, far = steps[-2:]
+    count = rows[0].shape[0] // 2
+    wide, narrow = jnp.float32, jnp.bfloat16
+    inner, outer, passed = [None, None], [None, None], [None, None]
+    for c in range(2):
+        sources = [(totals[c], 0, 0), (*flying[c], 0, 0)]
+        types = (wide, wide, narrow, narrow)
+        after = (totals[1],) if c == 0 else (totals[0][0],)
+        *kept, inside, outside = fold(sources, (4 * count, width), types, MERGE_COST[0], after)
+        totals[c] = kept
+        outer[c] = permute(outside, far)
+        inner[c] = permute(inside, far)
+    for c in range(2):
+        after = (totals[0][0],) if c == 0 else (leaving,)
+        sources = [(totals[c][1], 0, 0), (*outer[c], 0, 0)]
+        (leaving,) = fold(sources, (count, width), (narrow,), MERGE_COST[1], after)
+        passed[c] = permute(leaving, near)
+    after = (leaving,)
+    for c in range(2):
+        sources = [(x, 0, 0) for x in (totals[c][0], *inner[c], *passed[c])]
+        types = (wide,) + (narrow,) * len(steps[-3])
+        totals[c], *sent = fold(sources, (count, width), types, MERGE_COST[2], after)
+        flying[c] = permute(sent, steps[-3])
+        after = (totals[c],)
+    for step in steps[-4::-1]:
         for c in range(2):
-            totals[c], sent = merge(totals[c], flying[c], 1 + len(step), (totals[1 - c],))
+            sources = [(x, 0, 0) for x in (totals[c], *flying[c])]
+            types = (wide,) + (narrow,) * len(step)
+            totals[c], *sent = fold(sources, totals[c].shape, types, MERGE_COST[2])
             flying[c] = permute(sent, step)
     return small_call(
         lambda *refs: finish_kernel(len(flying[0]), *refs),

time: 67.6 us -> 65.3 us (0.966)
  waiting for transfers between devices: 20.7 us -> 17.3 us
  starting transfers between devices: 32.6 us -> 33.7 us
    ppermute x26 -> x28, waiting for transfers between devices: 20.7 us -> 17.3 us  [permute(): lax.ppermute(r, AXES, swap_with(flips))]
    ppermute x26 -> x28, starting transfers between devices: 32.6 us -> 33.7 us  [permute(): lax.ppermute(r, AXES, swap_with(flips))]
  transfers between devices with their start and end apart: 26 -> 28, of which waited for: 12 -> 13; matrix products, arithmetic and copies ran while one was open for 0% -> 0% of each run, Pallas kernels for 12% -> 13%
where the time goes in v4:
time: 65.3 us; the launch traced here: 65.1 us
  starting transfers between devices  33.7 us (52%)
  waiting for transfers between devices  17.3 us (26%)
  Pallas kernels  13.8 us (21%)
    ppermute x28, starting transfers between devices, permute(): lax.ppermute(r, AXES, swap_with(flips))  33.7 us
    ppermute x28, waiting for transfers between devices, permute(): lax.ppermute(r, AXES, swap_with(flips))  17.3 us
    pallas_call x2, Pallas kernels, hidden_rows(): pl.pallas_call(lambda *refs: hidden_kernel(depth, len(parts), *refs), in_...  4.1 us
    pallas_call x2, Pallas kernels, pair(): pl.pallas_call(lambda *refs: pair_kernel(depth, len(parts), *refs), in_sp...  3.83 us
    pallas_call x2, Pallas kernels, down(): pl.pallas_call(lambda *refs: down_kernel(first, experts, len(hidden), *re...  3.58 us
  transfers between devices with their start and end apart: 28, of which 13 were waited for; matrix products, arithmetic and copies ran while one was open for 0% of the time, Pallas kernels for 13%

profile of v4, /device:TPU:0, one launch (start us, length us, event | category | flops | bytes accessed | tf_op | source)
XLA Modules:
  0.0 65.1 jit_solution(4032398011592607860)
XLA Ops:
  0.0 1.0 %cut.1 = (bf16[8,3072]{1,0:T(8,128)(2,1)S(1)}, bf16[8,3200]{1,0:T(8,128)(2,1)S(1)}) custom-call(bf16[8,6144]{1,0:T(8,128)(2,1)} %refs_0_.1, f32[2,8]{1,0:T(2,128)} %bitcast.8, s32[2,8]{1,0:T(2,128)} %bitcast.9), custom_call_target="tpu_custom_call" | custom-call | flops 1000000 | tf_op jit(solution)/shard_map/cut/pallas_call | solution.py:276
  1.0 5.1 %collective-permute-start.5 = (bf16[8,3072]{1,0:T(8,128)(2,1)S(1)}, bf16[8,3072]{1,0:T(8,128)(2,1)S(1)}, u32[]{:S(2)}, u32[]{:S(2)}) collective-permute-start(bf16[8,3072]{1,0:T(8,128)(2,1)S(1)} %get-tuple-element.36.refs_0_), channel_id=1, source_target_pairs={{0,12},{1,13},{2,14},{3,15},{4,8},{5,9},{6,10},{7,11},{8,4},{9,5},... | collective-permute-start | bytes 147464 | tf_op jit(solution)/shard_map/ppermute | solution.py:264
  6.2 0.6 collective-permute-start.3
  6.8 3.7 %collective-permute-start.2 = (bf16[8,3200]{1,0:T(8,128)(2,1)S(1)}, bf16[8,3200]{1,0:T(8,128)(2,1)S(1)}, u32[]{:S(2)}, u32[]{:S(2)}) collective-permute-start(bf16[8,3200]{1,0:T(8,128)(2,1)S(1)} %get-tuple-element.35.refs_4_.refs_0_), channel_id=1, source_target_pairs={{0,12},{1,13},{2,14},{3,15},{4,8},{5,9},{6,10},{7,11},{8,4},{9,5},... | collective-permute-start | bytes 153608 | tf_op jit(solution)/shard_map/ppermute | solution.py:264
  10.5 0.6 collective-permute-start
  11.2 1.3 %collective-permute-done.4.refs_2_ = bf16[8,3072]{1,0:T(8,128)(2,1)S(1)} collective-permute-done((bf16[8,3072]{1,0:T(8,128)(2,1)S(1)}, bf16[8,3072]{1,0:T(8,128)(2,1)S(1)}, u32[]{:S(2)}, u32[]{:S(2)}) %collective-permute-start.4) | collective-permute-done | bytes 49184 | tf_op jit(solution)/shard_map/ppermute | solution.py:264
  12.5 1.6 %collective-permute-start.7 = (bf16[32,3072]{1,0:T(8,128)(2,1)S(1)}, bf16[32,3072]{1,0:T(8,128)(2,1)S(1)}, u32[]{:S(2)}, u32[]{:S(2)}) collective-permute-start(bf16[32,3072]{1,0:T(8,128)(2,1)S(1)} %stack.4.refs_4_.refs_0_), channel_id=1, source_target_pairs={{0,2},{1,3},{2,0},{3,1},{4,6},{5,7},{6,4},{7,5},{8,10},{9,11},{10,... | collective-permute-start | bytes 589832 | tf_op jit(solution)/shard_map/ppermute | solution.py:264
  14.1 1.5 %collective-permute-done.1.refs_2_ = bf16[8,3200]{1,0:T(8,128)(2,1)S(1)} collective-permute-done((bf16[8,3200]{1,0:T(8,128)(2,1)S(1)}, bf16[8,3200]{1,0:T(8,128)(2,1)S(1)}, u32[]{:S(2)}, u32[]{:S(2)}) %collective-permute-start.1) | collective-permute-done | bytes 51232 | tf_op jit(solution)/shard_map/ppermute | solution.py:264
  15.6 1.6 %collective-permute-start.6 = (bf16[32,3200]{1,0:T(8,128)(2,1)S(1)}, bf16[32,3200]{1,0:T(8,128)(2,1)S(1)}, u32[]{:S(2)}, u32[]{:S(2)}) collective-permute-start(bf16[32,3200]{1,0:T(8,128)(2,1)S(1)} %stack.5.refs_2_.refs_0_), channel_id=1, source_target_pairs={{0,2},{1,3},{2,0},{3,1},{4,6},{5,7},{6,4},{7,5},{8,10},{9,11},{10,... | collective-permute-start | bytes 614408 | tf_op jit(solution)/shard_map/ppermute | solution.py:264
  17.1 1.1 %collective-permute-done.7.refs_1_ = bf16[32,3072]{1,0:T(8,128)(2,1)S(1)} collective-permute-done((bf16[32,3072]{1,0:T(8,128)(2,1)S(1)}, bf16[32,3072]{1,0:T(8,128)(2,1)S(1)}, u32[]{:S(2)}, u32[]{:S(2)}) %collective-permute-start.7) | collective-permute-done | bytes 196640 | tf_op jit(solution)/shard_map/ppermute | solution.py:264
  18.3 0.1 collective-permute-start.10
  18.4 1.6 %collective-permute-start.9 = (bf16[64,3072]{1,0:T(8,128)(2,1)S(1)}, bf16[64,3072]{1,0:T(8,128)(2,1)S(1)}, u32[]{:S(2)}, u32[]{:S(2)}) collective-permute-start(bf16[64,3072]{1,0:T(8,128)(2,1)S(1)} %stack.6.refs_2_.refs_0_), channel_id=1, source_target_pairs={{0,1},{1,0},{2,3},{3,2},{4,5},{5,4},{6,7},{7,6},{8,9},{9,8},{10,11... | collective-permute-start | bytes 1179656 | tf_op jit(solution)/shard_map/ppermute | solution.py:264
  20.0 1.4 %collective-permute-done.6.refs_1_ = bf16[32,3200]{1,0:T(8,128)(2,1)S(1)} collective-permute-done((bf16[32,3200]{1,0:T(8,128)(2,1)S(1)}, bf16[32,3200]{1,0:T(8,128)(2,1)S(1)}, u32[]{:S(2)}, u32[]{:S(2)}) %collective-permute-start.6) | collective-permute-done | bytes 204832 | tf_op jit(solution)/shard_map/ppermute | solution.py:264
  21.4 0.1 collective-permute-start.8
  21.5 1.6 %collective-permute-start.11 = (bf16[64,3200]{1,0:T(8,128)(2,1)S(1)}, bf16[64,3200]{1,0:T(8,128)(2,1)S(1)}, u32[]{:S(2)}, u32[]{:S(2)}) collective-permute-start(bf16[64,3200]{1,0:T(8,128)(2,1)S(1)} %stack.7.refs_4_.refs_0_.refs_3_), channel_id=1, source_target_pairs={{0,1},{1,0},{2,3},{3,2},{4,5},{5,4},{6,7},{7,6},{8,9},{9,8},{10,11... | collective-permute-start | bytes 1228808 | tf_op jit(solution)/shard_map/ppermute | solution.py:264
  23.2 1.9 %pair.2 = (f32[128,1024]{1,0:T(8,128)S(1)}, f32[128,1024]{1,0:T(8,128)S(1)}) custom-call(bf16[64,3072]{1,0:T(8,128)(2,1)S(1)} %stack.6.refs_2_.refs_0_, bf16[64,3072]{1,0:T(8,128)(2,1)S(1)} %collective-permute-done.10.refs_1_, bf16[1,6144,1024]{2,1,0:T(8,128)(2,1)S(1)} %bitcast.3, bf16[1,6144,1024]{2,1,0:T(8,128)(2,1)S(1)} %bitcast.5, ...), custom_call_target="tpu_custom_call" | custom-call | flops 100000000 | tf_op jit(solution)/shard_map/pair/pallas_call | solution.py:42
  25.1 1.2 %collective-permute-done.9.refs_6_.refs_0_ = bf16[64,3072]{1,0:T(8,128)(2,1)S(1)} collective-permute-done((bf16[64,3072]{1,0:T(8,128)(2,1)S(1)}, bf16[64,3072]{1,0:T(8,128)(2,1)S(1)}, u32[]{:S(2)}, u32[]{:S(2)}) %collective-permute-start.9) | collective-permute-done | bytes 393248 | tf_op jit(solution)/shard_map/ppermute | solution.py:264
  26.3 2.0 %hidden_rows.2.refs_4_.refs_0_ = bf16[128,1024]{1,0:T(8,128)(2,1)S(1)} custom-call(bf16[64,3200]{1,0:T(8,128)(2,1)S(1)} %stack.7.refs_4_.refs_0_.refs_3_, bf16[64,3200]{1,0:T(8,128)(2,1)S(1)} %collective-permute-done.8.refs_1_.refs_4_, bf16[1,6144,1024]{2,1,0:T(8,128)(2,1)S(1)} %bitcast.3, bf16[1,6144,1024]{2,1,0:T(8,128)(2,1)S(1)} %bitcast.5, ...), custom_call_target="tpu_custom_call" | custom-call | flops 100000000 | tf_op jit(solution)/shard_map/hidden_rows/pallas_call | solution.py:72
  28.3 1.9 %pair.3 = (f32[128,1024]{1,0:T(8,128)S(1)}, f32[128,1024]{1,0:T(8,128)S(1)}) custom-call(bf16[64,3072]{1,0:T(8,128)(2,1)S(1)} %collective-permute-done.9.refs_6_.refs_0_, bf16[64,3072]{1,0:T(8,128)(2,1)S(1)} %collective-permute-done.12.refs_1_, bf16[1,6144,1024]{2,1,0:T(8,128)(2,1)S(1)} %bitcast.3, bf16[1,6144,1024]{2,1,0:T(8,128)(2,1)S(1)} %bitcast.5, ...), custom_call_target="tpu_custom_call" | custom-call | flops 100000000 | tf_op jit(solution)/shard_map/pair/pallas_call | solution.py:42
  30.3 0.4 collective-permute-done.11.refs_0_.refs_5_
  30.6 0.2 collective-permute-start.13
  30.9 1.5 %collective-permute-done.13.refs_1_.refs_6_ = bf16[64,3200]{1,0:T(8,128)(2,1)S(1)} collective-permute-done((bf16[64,3200]{1,0:T(8,128)(2,1)S(1)}, bf16[64,3200]{1,0:T(8,128)(2,1)S(1)}, u32[]{:S(2)}, u32[]{:S(2)}) %collective-permute-start.13) | collective-permute-done | bytes 409632 | tf_op jit(solution)/shard_map/ppermute | solution.py:264
  32.4 2.1 %hidden_rows.3.refs_1_ = bf16[128,1024]{1,0:T(8,128)(2,1)S(1)} custom-call(bf16[64,3200]{1,0:T(8,128)(2,1)S(1)} %collective-permute-done.11.refs_0_.refs_5_, bf16[64,3200]{1,0:T(8,128)(2,1)S(1)} %collective-permute-done.13.refs_1_.refs_6_, bf16[1,6144,1024]{2,1,0:T(8,128)(2,1)S(1)} %bitcast.3, bf16[1,6144,1024]{2,1,0:T(8,128)(2,1)S(1)} %bitcast.5, ...), custom_call_target="tpu_custom_call" | custom-call | flops 100000000 | tf_op jit(solution)/shard_map/hidden_rows/pallas_call | solution.py:72
  34.5 0.1 slice-done.8
  34.6 1.8 %down.2 = (f32[128,3072]{1,0:T(8,128)S(1)}, bf16[128,3072]{1,0:T(8,128)(2,1)S(1)}) custom-call(bf16[128,1024]{1,0:T(8,128)(2,1)S(1)} %hidden_rows.2.refs_4_.refs_0_, bf16[128,1024]{1,0:T(8,128)(2,1)S(1)} %hidden_rows.3.refs_1_, bf16[1,1024,6144]{2,1,0:T(8,128)(2,1)S(1)} %bitcast.7, bf16[64,3200]{1,0:T(8,128)(2,1)S(1)} %stack.7.refs_4_.refs_0_.refs_3_, ...), custom_call_target="tpu_custom_call" | custom-call | flops 100000000 | tf_op jit(solution)/shard_map/down/pallas_call | solution.py:117
  36.4 0.3 collective-permute-start.14
  36.7 1.8 %down.3 = (f32[128,3072]{1,0:T(8,128)S(1)}, bf16[128,3072]{1,0:T(8,128)(2,1)S(1)}) custom-call(bf16[128,1024]{1,0:T(8,128)(2,1)S(1)} %hidden_rows.2.refs_4_.refs_0_, bf16[128,1024]{1,0:T(8,128)(2,1)S(1)} %hidden_rows.3.refs_1_, bf16[1,1024,6144]{2,1,0:T(8,128)(2,1)S(1)} %bitcast.7, bf16[64,3200]{1,0:T(8,128)(2,1)S(1)} %stack.7.refs_4_.refs_0_.refs_3_, ...), custom_call_target="tpu_custom_call" | custom-call | flops 100000000 | tf_op jit(solution)/shard_map/down/pallas_call | solution.py:117
  38.5 0.4 collective-permute-start.18
  38.8 0.1 fold.6
  38.9 1.6 %collective-permute-start.16 = (bf16[32,3072]{1,0:T(8,128)(2,1)S(1)}, bf16[32,3072]{1,0:T(8,128)(2,1)S(1)}, u32[]{:S(2)}, u32[]{:S(2)}) collective-permute-start(bf16[32,3072]{1,0:T(8,128)(2,1)S(1)} %get-tuple-element.51), channel_id=1, source_target_pairs={{0,1},{1,0},{2,3},{3,2},{4,5},{5,4},{6,7},{7,6},{8,9},{9,8},{10,11... | collective-permute-start | bytes 589832 | tf_op jit(solution)/shard_map/ppermute | solution.py:264
  40.5 0.3 collective-permute-done.18.refs_1_
  40.8 0.1 fold.8
  40.9 1.6 %collective-permute-start.19 = (bf16[32,3072]{1,0:T(8,128)(2,1)S(1)}, bf16[32,3072]{1,0:T(8,128)(2,1)S(1)}, u32[]{:S(2)}, u32[]{:S(2)}) collective-permute-start(bf16[32,3072]{1,0:T(8,128)(2,1)S(1)} %get-tuple-element.54), channel_id=1, source_target_pairs={{0,1},{1,0},{2,3},{3,2},{4,5},{5,4},{6,7},{7,6},{8,9},{9,8},{10,11... | collective-permute-start | bytes 589832 | tf_op jit(solution)/shard_map/ppermute | solution.py:264
  42.5 0.5 collective-permute-start.15
  43.0 1.7 %collective-permute-done.16.refs_1_ = bf16[32,3072]{1,0:T(8,128)(2,1)S(1)} collective-permute-done((bf16[32,3072]{1,0:T(8,128)(2,1)S(1)}, bf16[32,3072]{1,0:T(8,128)(2,1)S(1)}, u32[]{:S(2)}, u32[]{:S(2)}) %collective-permute-start.16) | collective-permute-done | bytes 196640 | tf_op jit(solution)/shard_map/ppermute | solution.py:264
  44.7 1.6 %collective-permute-start.17 = (bf16[32,3072]{1,0:T(8,128)(2,1)S(1)}, bf16[32,3072]{1,0:T(8,128)(2,1)S(1)}, u32[]{:S(2)}, u32[]{:S(2)}) collective-permute-start(bf16[32,3072]{1,0:T(8,128)(2,1)S(1)} %fold.7.refs_2_), channel_id=1, source_target_pairs={{0,2},{1,3},{2,0},{3,1},{4,6},{5,7},{6,4},{7,5},{8,10},{9,11},{10,... | collective-permute-start | bytes 589832 | tf_op jit(solution)/shard_map/ppermute | solution.py:264
  46.3 1.5 %collective-permute-start.23 = (bf16[32,3072]{1,0:T(8,128)(2,1)S(1)}, bf16[32,3072]{1,0:T(8,128)(2,1)S(1)}, u32[]{:S(2)}, u32[]{:S(2)}) collective-permute-start(bf16[32,3072]{1,0:T(8,128)(2,1)S(1)} %get-tuple-element.60), channel_id=1, source_target_pairs={{0,1},{1,0},{2,3},{3,2},{4,5},{5,4},{6,7},{7,6},{8,9},{9,8},{10,11... | collective-permute-start | bytes 589832 | tf_op jit(solution)/shard_map/ppermute | solution.py:264
  47.8 0.6 collective-permute-start.24
  48.4 2.5 %collective-permute-done.15.refs_1_ = bf16[32,3072]{1,0:T(8,128)(2,1)S(1)} collective-permute-done((bf16[32,3072]{1,0:T(8,128)(2,1)S(1)}, bf16[32,3072]{1,0:T(8,128)(2,1)S(1)}, u32[]{:S(2)}, u32[]{:S(2)}) %collective-permute-start.15) | collective-permute-done | bytes 196640 | tf_op jit(solution)/shard_map/ppermute | solution.py:264
  51.0 1.4 %collective-permute-done.17.refs_2_ = bf16[32,3072]{1,0:T(8,128)(2,1)S(1)} collective-permute-done((bf16[32,3072]{1,0:T(8,128)(2,1)S(1)}, bf16[32,3072]{1,0:T(8,128)(2,1)S(1)}, u32[]{:S(2)}, u32[]{:S(2)}) %collective-permute-start.17) | collective-permute-done | bytes 196640 | tf_op jit(solution)/shard_map/ppermute | solution.py:264
  52.4 0.1 fold.10
  52.4 2.5 %collective-permute-start.20 = (bf16[8,3072]{1,0:T(8,128)(2,1)S(1)}, bf16[8,3072]{1,0:T(8,128)(2,1)S(1)}, u32[]{:S(2)}, u32[]{:S(2)}) collective-permute-start(bf16[8,3072]{1,0:T(8,128)(2,1)S(1)} %get-tuple-element.56), channel_id=1, source_target_pairs={{0,12},{1,13},{2,14},{3,15},{4,8},{5,9},{6,10},{7,11},{8,4},{9,5},... | collective-permute-start | bytes 147464 | tf_op jit(solution)/shard_map/ppermute | solution.py:264
  54.9 1.9 %collective-permute-start.22 = (bf16[8,3072]{1,0:T(8,128)(2,1)S(1)}, bf16[8,3072]{1,0:T(8,128)(2,1)S(1)}, u32[]{:S(2)}, u32[]{:S(2)}) collective-permute-start(bf16[8,3072]{1,0:T(8,128)(2,1)S(1)} %get-tuple-element.58), channel_id=1, source_target_pairs={{0,4},{1,5},{2,6},{3,7},{4,0},{5,1},{6,2},{7,3},{8,12},{9,13},{10,... | collective-permute-start | bytes 147464 | tf_op jit(solution)/shard_map/ppermute | solution.py:264
  56.9 2.5 %collective-permute-start.25 = (bf16[8,3072]{1,0:T(8,128)(2,1)S(1)}, bf16[8,3072]{1,0:T(8,128)(2,1)S(1)}, u32[]{:S(2)}, u32[]{:S(2)}) collective-permute-start(bf16[8,3072]{1,0:T(8,128)(2,1)S(1)} %get-tuple-element.62), channel_id=1, source_target_pairs={{0,12},{1,13},{2,14},{3,15},{4,8},{5,9},{6,10},{7,11},{8,4},{9,5},... | collective-permute-start | bytes 147464 | tf_op jit(solution)/shard_map/ppermute | solution.py:264
  59.5 1.9 %collective-permute-start.27 = (bf16[8,3072]{1,0:T(8,128)(2,1)S(1)}, bf16[8,3072]{1,0:T(8,128)(2,1)S(1)}, u32[]{:S(2)}, u32[]{:S(2)}) collective-permute-start(bf16[8,3072]{1,0:T(8,128)(2,1)S(1)} %get-tuple-element.64), channel_id=1, source_target_pairs={{0,4},{1,5},{2,6},{3,7},{4,0},{5,1},{6,2},{7,3},{8,12},{9,13},{10,... | collective-permute-start | bytes 147464 | tf_op jit(solution)/shard_map/ppermute | solution.py:264
  61.4 2.0 %collective-permute-done.25.refs_5_ = bf16[8,3072]{1,0:T(8,128)(2,1)S(1)} collective-permute-done((bf16[8,3072]{1,0:T(8,128)(2,1)S(1)}, bf16[8,3072]{1,0:T(8,128)(2,1)S(1)}, u32[]{:S(2)}, u32[]{:S(2)}) %collective-permute-start.25) | collective-permute-done | bytes 49184 | tf_op jit(solution)/shard_map/ppermute | solution.py:264
  63.4 1.0 %collective-permute-done.26.refs_6_ = bf16[8,3072]{1,0:T(8,128)(2,1)S(1)} collective-permute-done((bf16[8,3072]{1,0:T(8,128)(2,1)S(1)}, bf16[8,3072]{1,0:T(8,128)(2,1)S(1)}, u32[]{:S(2)}, u32[]{:S(2)}) %collective-permute-start.26) | collective-permute-done | bytes 49184 | tf_op jit(solution)/shard_map/ppermute | solution.py:264
  64.5 0.7 %finish.1 = bf16[8,6144]{1,0:T(8,128)(2,1)} custom-call(f32[8,3072]{1,0:T(8,128)S(1)} %get-tuple-element.55.refs_3_.refs_0_, bf16[8,3072]{1,0:T(8,128)(2,1)S(1)} %collective-permute-done.20.refs_1_, bf16[8,3072]{1,0:T(8,128)(2,1)S(1)} %collective-permute-done.21.refs_2_, bf16[8,3072]{1,0:T(8,128)(2,1)S(1)} %collective-permute-done.22.refs_3_, ...), custom_call_target="tpu_custom_call" | custom-call | flops 1000000 | tf_op jit(solution)/shard_map/finish/pallas_call | solution.py:134
  (47 shorter events, 0.3 us)
Async XLA Ops:
  1.0 9.5 %collective-permute-start.5 = (bf16[8,3072]{1,0:T(8,128)(2,1)S(1)}, bf16[8,3072]{1,0:T(8,128)(2,1)S(1)}, u32[]{:S(2)}, u32[]{:S(2)}) collective-permute-start(bf16[8,3072]{1,0:T(8,128)(2,1)S(1)} %get-tuple-element.36.refs_0_), channel_id=1, source_target_pairs={{0,12},{1,13},{2,14},{3,15},{4,8},{5,9},{6,10},{7,11},{8,4},{9,5},... | collective-permute-start | bytes 147464 | tf_op jit(solution)/shard_map/ppermute | solution.py:264
  6.2 6.3 %collective-permute-start.4 = (bf16[8,3072]{1,0:T(8,128)(2,1)S(1)}, bf16[8,3072]{1,0:T(8,128)(2,1)S(1)}, u32[]{:S(2)}, u32[]{:S(2)}) collective-permute-start(bf16[8,3072]{1,0:T(8,128)(2,1)S(1)} %get-tuple-element.36.refs_0_), channel_id=1, source_target_pairs={{0,8},{1,9},{2,10},{3,11},{4,12},{5,13},{6,14},{7,15},{8,0},{9,1},... | collective-permute-start | bytes 147464 | tf_op jit(solution)/shard_map/ppermute | solution.py:264
  6.2 6.3 %collective-permute-start.3 = (bf16[8,3072]{1,0:T(8,128)(2,1)S(1)}, bf16[8,3072]{1,0:T(8,128)(2,1)S(1)}, u32[]{:S(2)}, u32[]{:S(2)}) collective-permute-start(bf16[8,3072]{1,0:T(8,128)(2,1)S(1)} %get-tuple-element.36.refs_0_), channel_id=1, source_target_pairs={{0,4},{1,5},{2,6},{3,7},{4,0},{5,1},{6,2},{7,3},{8,12},{9,13},{10,... | collective-permute-start | bytes 147464 | tf_op jit(solution)/shard_map/ppermute | solution.py:264
  6.8 7.3 %collective-permute-start.2 = (bf16[8,3200]{1,0:T(8,128)(2,1)S(1)}, bf16[8,3200]{1,0:T(8,128)(2,1)S(1)}, u32[]{:S(2)}, u32[]{:S(2)}) collective-permute-start(bf16[8,3200]{1,0:T(8,128)(2,1)S(1)} %get-tuple-element.35.refs_4_.refs_0_), channel_id=1, source_target_pairs={{0,12},{1,13},{2,14},{3,15},{4,8},{5,9},{6,10},{7,11},{8,4},{9,5},... | collective-permute-start | bytes 153608 | tf_op jit(solution)/shard_map/ppermute | solution.py:264
  10.5 5.0 %collective-permute-start.1 = (bf16[8,3200]{1,0:T(8,128)(2,1)S(1)}, bf16[8,3200]{1,0:T(8,128)(2,1)S(1)}, u32[]{:S(2)}, u32[]{:S(2)}) collective-permute-start(bf16[8,3200]{1,0:T(8,128)(2,1)S(1)} %get-tuple-element.35.refs_4_.refs_0_), channel_id=1, source_target_pairs={{0,8},{1,9},{2,10},{3,11},{4,12},{5,13},{6,14},{7,15},{8,0},{9,1},... | collective-permute-start | bytes 153608 | tf_op jit(solution)/shard_map/ppermute | solution.py:264
  10.5 5.0 %collective-permute-start = (bf16[8,3200]{1,0:T(8,128)(2,1)S(1)}, bf16[8,3200]{1,0:T(8,128)(2,1)S(1)}, u32[]{:S(2)}, u32[]{:S(2)}) collective-permute-start(bf16[8,3200]{1,0:T(8,128)(2,1)S(1)} %get-tuple-element.35.refs_4_.refs_0_), channel_id=1, source_target_pairs={{0,4},{1,5},{2,6},{3,7},{4,0},{5,1},{6,2},{7,3},{8,12},{9,13},{10,... | collective-permute-start | bytes 153608 | tf_op jit(solution)/shard_map/ppermute | solution.py:264
  12.5 10.6 %slice-start.3 = ((s8[12582912]{0:T(1024)(128)(4,1)}), s8[4194304]{0:T(1024)(128)(4,1)S(1)}, s32[]{:S(2)}) async-start(s8[12582912]{0:T(1024)(128)(4,1)} %bitcast.4), calls=%async_computation.3 | async-start | bytes 8388608
  12.5 10.6 %slice-start.4 = ((s8[12582912]{0:T(1024)(128)(4,1)}), s8[4194304]{0:T(1024)(128)(4,1)S(1)}, s32[]{:S(2)}) async-start(s8[12582912]{0:T(1024)(128)(4,1)} %bitcast.4), calls=%async_computation.4 | async-start | bytes 8388608
  12.5 5.7 %collective-permute-start.7 = (bf16[32,3072]{1,0:T(8,128)(2,1)S(1)}, bf16[32,3072]{1,0:T(8,128)(2,1)S(1)}, u32[]{:S(2)}, u32[]{:S(2)}) collective-permute-start(bf16[32,3072]{1,0:T(8,128)(2,1)S(1)} %stack.4.refs_4_.refs_0_), channel_id=1, source_target_pairs={{0,2},{1,3},{2,0},{3,1},{4,6},{5,7},{6,4},{7,5},{8,10},{9,11},{10,... | collective-permute-start | bytes 589832 | tf_op jit(solution)/shard_map/ppermute | solution.py:264
  15.6 7.6 %slice-start = ((s8[12582912]{0:T(1024)(128)(4,1)}), s8[4194304]{0:T(1024)(128)(4,1)S(1)}, s32[]{:S(2)}) async-start(s8[12582912]{0:T(1024)(128)(4,1)} %bitcast.2), calls=%async_computation | async-start | bytes 8388608
  15.6 7.6 %slice-start.1 = ((s8[12582912]{0:T(1024)(128)(4,1)}), s8[4194304]{0:T(1024)(128)(4,1)S(1)}, s32[]{:S(2)}) async-start(s8[12582912]{0:T(1024)(128)(4,1)} %bitcast.2), calls=%async_computation.1 | async-start | bytes 8388608
  15.6 5.8 %collective-permute-start.6 = (bf16[32,3200]{1,0:T(8,128)(2,1)S(1)}, bf16[32,3200]{1,0:T(8,128)(2,1)S(1)}, u32[]{:S(2)}, u32[]{:S(2)}) collective-permute-start(bf16[32,3200]{1,0:T(8,128)(2,1)S(1)} %stack.5.refs_2_.refs_0_), channel_id=1, source_target_pairs={{0,2},{1,3},{2,0},{3,1},{4,6},{5,7},{6,4},{7,5},{8,10},{9,11},{10,... | collective-permute-start | bytes 614408 | tf_op jit(solution)/shard_map/ppermute | solution.py:264
  18.3 4.8 %slice-start.2 = ((s8[12582912]{0:T(1024)(128)(4,1)}), s8[4194304]{0:T(1024)(128)(4,1)S(1)}, s32[]{:S(2)}) async-start(s8[12582912]{0:T(1024)(128)(4,1)} %bitcast.2), calls=%async_computation.2 | async-start | bytes 8388608
  18.3 4.8 %slice-start.5 = ((s8[12582912]{0:T(1024)(128)(4,1)}), s8[4194304]{0:T(1024)(128)(4,1)S(1)}, s32[]{:S(2)}) async-start(s8[12582912]{0:T(1024)(128)(4,1)} %bitcast.4), calls=%async_computation.5 | async-start | bytes 8388608
  18.3 4.8 %collective-permute-start.10 = (bf16[64,3072]{1,0:T(8,128)(2,1)S(1)}, bf16[64,3072]{1,0:T(8,128)(2,1)S(1)}, u32[]{:S(2)}, u32[]{:S(2)}) collective-permute-start(bf16[64,3072]{1,0:T(8,128)(2,1)S(1)} %stack.6.refs_2_.refs_0_), channel_id=1, source_target_pairs={{0,16},{1,17},{2,18},{3,19},{4,20},{5,21},{6,22},{7,23},{8,24},{9,... | collective-permute-start | bytes 1179656 | tf_op jit(solution)/shard_map/ppermute | solution.py:264
  18.4 7.8 %collective-permute-start.9 = (bf16[64,3072]{1,0:T(8,128)(2,1)S(1)}, bf16[64,3072]{1,0:T(8,128)(2,1)S(1)}, u32[]{:S(2)}, u32[]{:S(2)}) collective-permute-start(bf16[64,3072]{1,0:T(8,128)(2,1)S(1)} %stack.6.refs_2_.refs_0_), channel_id=1, source_target_pairs={{0,1},{1,0},{2,3},{3,2},{4,5},{5,4},{6,7},{7,6},{8,9},{9,8},{10,11... | collective-permute-start | bytes 1179656 | tf_op jit(solution)/shard_map/ppermute | solution.py:264
  21.4 4.8 %collective-permute-start.8 = (bf16[64,3200]{1,0:T(8,128)(2,1)S(1)}, bf16[64,3200]{1,0:T(8,128)(2,1)S(1)}, u32[]{:S(2)}, u32[]{:S(2)}) collective-permute-start(bf16[64,3200]{1,0:T(8,128)(2,1)S(1)} %stack.7.refs_4_.refs_0_.refs_3_), channel_id=1, source_target_pairs={{0,16},{1,17},{2,18},{3,19},{4,20},{5,21},{6,22},{7,23},{8,24},{9,... | collective-permute-start | bytes 1228808 | tf_op jit(solution)/shard_map/ppermute | solution.py:264
  21.5 9.1 %collective-permute-start.11 = (bf16[64,3200]{1,0:T(8,128)(2,1)S(1)}, bf16[64,3200]{1,0:T(8,128)(2,1)S(1)}, u32[]{:S(2)}, u32[]{:S(2)}) collective-permute-start(bf16[64,3200]{1,0:T(8,128)(2,1)S(1)} %stack.7.refs_4_.refs_0_.refs_3_), channel_id=1, source_target_pairs={{0,1},{1,0},{2,3},{3,2},{4,5},{5,4},{6,7},{7,6},{8,9},{9,8},{10,11... | collective-permute-start | bytes 1228808 | tf_op jit(solution)/shard_map/ppermute | solution.py:264
  26.2 2.1 %collective-permute-start.12 = (bf16[64,3072]{1,0:T(8,128)(2,1)S(1)}, bf16[64,3072]{1,0:T(8,128)(2,1)S(1)}, u32[]{:S(2)}, u32[]{:S(2)}) collective-permute-start(bf16[64,3072]{1,0:T(8,128)(2,1)S(1)} %collective-permute-done.9.refs_6_.refs_0_), channel_id=1, source_target_pairs={{0,16},{1,17},{2,18},{3,19},{4,20},{5,21},{6,22},{7,23},{8,24},{9,... | collective-permute-start | bytes 1179656 | tf_op jit(solution)/shard_map/ppermute | solution.py:264
  28.3 6.1 %slice-start.6 = ((s8[12582912]{0:T(1024)(128)(4,1)}), s8[4194304]{0:T(1024)(128)(4,1)S(1)}, s32[]{:S(2)}) async-start(s8[12582912]{0:T(1024)(128)(4,1)} %bitcast.6), calls=%async_computation.6 | async-start | bytes 8388608
  28.3 6.1 %slice-start.7 = ((s8[12582912]{0:T(1024)(128)(4,1)}), s8[4194304]{0:T(1024)(128)(4,1)S(1)}, s32[]{:S(2)}) async-start(s8[12582912]{0:T(1024)(128)(4,1)} %bitcast.6), calls=%async_computation.7 | async-start | bytes 8388608
  30.6 1.7 %collective-permute-start.13 = (bf16[64,3200]{1,0:T(8,128)(2,1)S(1)}, bf16[64,3200]{1,0:T(8,128)(2,1)S(1)}, u32[]{:S(2)}, u32[]{:S(2)}) collective-permute-start(bf16[64,3200]{1,0:T(8,128)(2,1)S(1)} %collective-permute-done.11.refs_0_.refs_5_), channel_id=1, source_target_pairs={{0,16},{1,17},{2,18},{3,19},{4,20},{5,21},{6,22},{7,23},{8,24},{9,... | collective-permute-start | bytes 1228808 | tf_op jit(solution)/shard_map/ppermute | solution.py:264
  32.4 2.2 %slice-start.8 = ((s8[12582912]{0:T(1024)(128)(4,1)}), s8[4194304]{0:T(1024)(128)(4,1)S(1)}, s32[]{:S(2)}) async-start(s8[12582912]{0:T(1024)(128)(4,1)} %bitcast.6), calls=%async_computation.8 | async-start | bytes 8388608
  36.4 2.4 %collective-permute-start.14 = (bf16[128,3072]{1,0:T(8,128)(2,1)S(1)}, bf16[128,3072]{1,0:T(8,128)(2,1)S(1)}, u32[]{:S(2)}, u32[]{:S(2)}) collective-permute-start(bf16[128,3072]{1,0:T(8,128)(2,1)S(1)} %get-tuple-element.46), channel_id=1, source_target_pairs={{0,16},{1,17},{2,18},{3,19},{4,20},{5,21},{6,22},{7,23},{8,24},{9,... | collective-permute-start | bytes 2359304 | tf_op jit(solution)/shard_map/ppermute | solution.py:264
  38.5 2.4 %collective-permute-start.18 = (bf16[128,3072]{1,0:T(8,128)(2,1)S(1)}, bf16[128,3072]{1,0:T(8,128)(2,1)S(1)}, u32[]{:S(2)}, u32[]{:S(2)}) collective-permute-start(bf16[128,3072]{1,0:T(8,128)(2,1)S(1)} %get-tuple-element.52), channel_id=1, source_target_pairs={{0,16},{1,17},{2,18},{3,19},{4,20},{5,21},{6,22},{7,23},{8,24},{9,... | collective-permute-start | bytes 2359304 | tf_op jit(solution)/shard_map/ppermute | solution.py:264
  38.9 5.7 %collective-permute-start.16 = (bf16[32,3072]{1,0:T(8,128)(2,1)S(1)}, bf16[32,3072]{1,0:T(8,128)(2,1)S(1)}, u32[]{:S(2)}, u32[]{:S(2)}) collective-permute-start(bf16[32,3072]{1,0:T(8,128)(2,1)S(1)} %get-tuple-element.51), channel_id=1, source_target_pairs={{0,1},{1,0},{2,3},{3,2},{4,5},{5,4},{6,7},{7,6},{8,9},{9,8},{10,11... | collective-permute-start | bytes 589832 | tf_op jit(solution)/shard_map/ppermute | solution.py:264
  40.9 6.9 %collective-permute-start.19 = (bf16[32,3072]{1,0:T(8,128)(2,1)S(1)}, bf16[32,3072]{1,0:T(8,128)(2,1)S(1)}, u32[]{:S(2)}, u32[]{:S(2)}) collective-permute-start(bf16[32,3072]{1,0:T(8,128)(2,1)S(1)} %get-tuple-element.54), channel_id=1, source_target_pairs={{0,1},{1,0},{2,3},{3,2},{4,5},{5,4},{6,7},{7,6},{8,9},{9,8},{10,11... | collective-permute-start | bytes 589832 | tf_op jit(solution)/shard_map/ppermute | solution.py:264
  42.5 8.5 %collective-permute-start.15 = (bf16[32,3072]{1,0:T(8,128)(2,1)S(1)}, bf16[32,3072]{1,0:T(8,128)(2,1)S(1)}, u32[]{:S(2)}, u32[]{:S(2)}) collective-permute-start(bf16[32,3072]{1,0:T(8,128)(2,1)S(1)} %get-tuple-element.49), channel_id=1, source_target_pairs={{0,1},{1,0},{2,3},{3,2},{4,5},{5,4},{6,7},{7,6},{8,9},{9,8},{10,11... | collective-permute-start | bytes 589832 | tf_op jit(solution)/shard_map/ppermute | solution.py:264
  44.7 7.6 %collective-permute-start.17 = (bf16[32,3072]{1,0:T(8,128)(2,1)S(1)}, bf16[32,3072]{1,0:T(8,128)(2,1)S(1)}, u32[]{:S(2)}, u32[]{:S(2)}) collective-permute-start(bf16[32,3072]{1,0:T(8,128)(2,1)S(1)} %fold.7.refs_2_), channel_id=1, source_target_pairs={{0,2},{1,3},{2,0},{3,1},{4,6},{5,7},{6,4},{7,5},{8,10},{9,11},{10,... | collective-permute-start | bytes 589832 | tf_op jit(solution)/shard_map/ppermute | solution.py:264
  46.3 10.6 %collective-permute-start.23 = (bf16[32,3072]{1,0:T(8,128)(2,1)S(1)}, bf16[32,3072]{1,0:T(8,128)(2,1)S(1)}, u32[]{:S(2)}, u32[]{:S(2)}) collective-permute-start(bf16[32,3072]{1,0:T(8,128)(2,1)S(1)} %get-tuple-element.60), channel_id=1, source_target_pairs={{0,1},{1,0},{2,3},{3,2},{4,5},{5,4},{6,7},{7,6},{8,9},{9,8},{10,11... | collective-permute-start | bytes 589832 | tf_op jit(solution)/shard_map/ppermute | solution.py:264
  47.8 9.0 %collective-permute-start.24 = (bf16[32,3072]{1,0:T(8,128)(2,1)S(1)}, bf16[32,3072]{1,0:T(8,128)(2,1)S(1)}, u32[]{:S(2)}, u32[]{:S(2)}) collective-permute-start(bf16[32,3072]{1,0:T(8,128)(2,1)S(1)} %fold.9.refs_3_), channel_id=1, source_target_pairs={{0,2},{1,3},{2,0},{3,1},{4,6},{5,7},{6,4},{7,5},{8,10},{9,11},{10,... | collective-permute-start | bytes 589832 | tf_op jit(solution)/shard_map/ppermute | solution.py:264
  52.4 7.1 %collective-permute-start.20 = (bf16[8,3072]{1,0:T(8,128)(2,1)S(1)}, bf16[8,3072]{1,0:T(8,128)(2,1)S(1)}, u32[]{:S(2)}, u32[]{:S(2)}) collective-permute-start(bf16[8,3072]{1,0:T(8,128)(2,1)S(1)} %get-tuple-element.56), channel_id=1, source_target_pairs={{0,12},{1,13},{2,14},{3,15},{4,8},{5,9},{6,10},{7,11},{8,4},{9,5},... | collective-permute-start | bytes 147464 | tf_op jit(solution)/shard_map/ppermute | solution.py:264
  54.9 6.5 %collective-permute-start.21 = (bf16[8,3072]{1,0:T(8,128)(2,1)S(1)}, bf16[8,3072]{1,0:T(8,128)(2,1)S(1)}, u32[]{:S(2)}, u32[]{:S(2)}) collective-permute-start(bf16[8,3072]{1,0:T(8,128)(2,1)S(1)} %get-tuple-element.57), channel_id=1, source_target_pairs={{0,8},{1,9},{2,10},{3,11},{4,12},{5,13},{6,14},{7,15},{8,0},{9,1},... | collective-permute-start | bytes 147464 | tf_op jit(solution)/shard_map/ppermute | solution.py:264
  54.9 6.5 %collective-permute-start.22 = (bf16[8,3072]{1,0:T(8,128)(2,1)S(1)}, bf16[8,3072]{1,0:T(8,128)(2,1)S(1)}, u32[]{:S(2)}, u32[]{:S(2)}) collective-permute-start(bf16[8,3072]{1,0:T(8,128)(2,1)S(1)} %get-tuple-element.58), channel_id=1, source_target_pairs={{0,4},{1,5},{2,6},{3,7},{4,0},{5,1},{6,2},{7,3},{8,12},{9,13},{10,... | collective-permute-start | bytes 147464 | tf_op jit(solution)/shard_map/ppermute | solution.py:264
  56.9 6.5 %collective-permute-start.25 = (bf16[8,3072]{1,0:T(8,128)(2,1)S(1)}, bf16[8,3072]{1,0:T(8,128)(2,1)S(1)}, u32[]{:S(2)}, u32[]{:S(2)}) collective-permute-start(bf16[8,3072]{1,0:T(8,128)(2,1)S(1)} %get-tuple-element.62), channel_id=1, source_target_pairs={{0,12},{1,13},{2,14},{3,15},{4,8},{5,9},{6,10},{7,11},{8,4},{9,5},... | collective-permute-start | bytes 147464 | tf_op jit(solution)/shard_map/ppermute | solution.py:264
  59.5 5.0 %collective-permute-start.26 = (bf16[8,3072]{1,0:T(8,128)(2,1)S(1)}, bf16[8,3072]{1,0:T(8,128)(2,1)S(1)}, u32[]{:S(2)}, u32[]{:S(2)}) collective-permute-start(bf16[8,3072]{1,0:T(8,128)(2,1)S(1)} %get-tuple-element.63), channel_id=1, source_target_pairs={{0,8},{1,9},{2,10},{3,11},{4,12},{5,13},{6,14},{7,15},{8,0},{9,1},... | collective-permute-start | bytes 147464 | tf_op jit(solution)/shard_map/ppermute | solution.py:264
  59.5 5.0 %collective-permute-start.27 = (bf16[8,3072]{1,0:T(8,128)(2,1)S(1)}, bf16[8,3072]{1,0:T(8,128)(2,1)S(1)}, u32[]{:S(2)}, u32[]{:S(2)}) collective-permute-start(bf16[8,3072]{1,0:T(8,128)(2,1)S(1)} %get-tuple-element.64), channel_id=1, source_target_pairs={{0,4},{1,5},{2,6},{3,7},{4,0},{5,1},{6,2},{7,3},{8,12},{9,13},{10,... | collective-permute-start | bytes 147464 | tf_op jit(solution)/shard_map/ppermute | solution.py:264
